TPU v7x, 128 devices: a whole 4x4x4 slice. The times are simulated.
128 devices in a mesh: comp: 2 (over core), tile: 64 (over x, y, z).
Axes of the slice: x: 4, y: 4, z: 4, core: 2. Of those that a mesh axis runs over, the one named last changes fastest.
Arguments:
- tracer: float32 [2, 16, 4, 256, 1024], P('comp', None, None, 'tile'), may hold values from -6 to 6
- velocity: float32 [2, 2, 4, 256, 1024], P('comp', None, None, 'tile'), may hold values from -0.3 to 0.3
- coupling: float32 [2, 16, 256, 1024], P('comp', None, 'tile'), may hold values from 0.05 to 0.5
- sea_mask: int32 [2, 256, 1024], P('comp', 'tile'), may hold values 0 or 1
- send_rows: int32 [2, 64, 4, 2048], P('comp', 'tile'), may hold values from 0 to 3
- send_cols: int32 [2, 64, 4, 2048], P('comp', 'tile'), may hold values from 0 to 1023
- intersection_near: int32 [2, 8, 256, 1024], P('comp', None, 'tile'), may hold values from 0 to 3
- intersection_slot: int32 [2, 8, 256, 1024], P('comp', None, 'tile'), may hold values from 0 to 2047
- intersection_weight: float32 [2, 8, 256, 1024], P('comp', None, 'tile'), as said below
Outputs:
- tracer_out: float32 [2, 16, 4, 256, 1024], P('comp', None, None, 'tile')
Inputs may be any that keep to these rules, and one draw needn't show every extreme that they name: `intersection_weight`: positive, summing to one over the 8 intersections of a cell.
All inputs are finite; a program needn't handle non-finite values. No bound on the sum of `sea_mask` on one device may be relied on, other than what follows from the above.
Results may differ from a plain program's by a relative error of at most 0.000088.
Values sent between devices are 32-bit elements; how exact they have to be, the bound alone decides.
No kernel may reach another device: no remote copies, remote signals or barrier semaphores. Data moves between devices by JAX's collectives and lax.ppermute only.
A program may use at most 64 MiB of HBM per device.

v0:
```python
import math

import jax
import jax.numpy as jnp
from jax import lax
from jax.sharding import PartitionSpec as P

diffusion = 0.12


def passed_along(value, axis, steps):
    count = lax.axis_size(axis)
    pairs = [(source, (source + steps) % count) for source in range(count)]
    return lax.ppermute(value, axis, pairs)


def swapped(value, axis, bit):
    mask = 2**bit
    pairs = [(source, source ^ mask) for source in range(lax.axis_size(axis))]
    return lax.ppermute(value, axis, pairs)


def with_halo(x, sides, width):
    for axis, dim in sides:
        devices, length = (lax.axis_size(axis), x.shape[dim])
        up = [(i, (i + 1) % devices) for i in range(devices)]
        down = [(j, i) for i, j in up]
        last = lax.slice_in_dim(x, length - width, length, axis=dim)
        first = lax.slice_in_dim(x, 0, width, axis=dim)
        before = lax.ppermute(last, axis, up)
        after = lax.ppermute(first, axis, down)
        x = jnp.concatenate([before, x, after], axis=dim)
    return x


def substep(padded, speed):
    field = padded[:, :, 1:-1]
    east = padded[:, :, 2:]
    west = padded[:, :, :-2]
    north = jnp.roll(field, -1, axis=3)
    south = jnp.roll(field, 1, axis=3)
    return (
        field
        - 0.5 * speed[0] * (east - west)
        - 0.5 * speed[1] * (north - south)
        + diffusion * (east + west + north + south - 4.0 * field)
    )


def pack_rows(surface, rows, cols):
    tracers, rows_x, width = surface.shape
    neighbours, capacity = rows.shape
    total_slots = neighbours * capacity
    block = math.gcd(total_slots, 1024)
    count = total_slots // block
    row_blocks = rows.reshape(count, block)
    col_blocks = cols.reshape(count, block)

    def pack_one_block(pair):
        row_ids, col_ids = pair
        col_hot = (lax.broadcasted_iota(jnp.int32, (width, block), 0) == col_ids[None, :]).astype(
            jnp.float32
        )
        partial_rows = jnp.einsum(
            "qry,ys->qrs",
            surface,
            col_hot,
            precision=lax.Precision.HIGHEST,
            preferred_element_type=jnp.float32,
        )
        row_hot = (lax.broadcasted_iota(jnp.int32, (rows_x, block), 0) == row_ids[None, :]).astype(
            jnp.float32
        )
        return jnp.sum(partial_rows * row_hot[None], axis=1)

    packed = lax.map(pack_one_block, (row_blocks, col_blocks))
    return jnp.transpose(packed, (1, 0, 2)).reshape(tracers, neighbours, capacity)


def per_device(
    tracer,
    velocity,
    coupling,
    sea_mask,
    send_rows,
    send_cols,
    intersection_near,
    intersection_slot,
    intersection_weight,
):
    field = tracer[0]
    speed = velocity[0]
    tracers, levels, rows_x, width = field.shape
    neighbours = send_rows.shape[2]
    capacity = send_rows.shape[3]
    intersections = intersection_slot.shape[1]
    cells = rows_x * width
    surface = field[:, 0]
    cell_block = math.gcd(cells, 512)
    cell_count = cells // cell_block
    near_blocks = jnp.transpose(
        intersection_near[0].reshape(intersections, cell_count, cell_block), (1, 0, 2)
    )
    slot_blocks = jnp.transpose(
        intersection_slot[0].reshape(intersections, cell_count, cell_block), (1, 0, 2)
    )
    weight_blocks = jnp.transpose(
        intersection_weight[0].reshape(intersections, cell_count, cell_block), (1, 0, 2)
    )
    packed = pack_rows(surface, send_rows[0, 0], send_cols[0, 0])
    pieces = []
    for near in range(neighbours):
        pieces.append(passed_along(packed[:, near], "tile", 1 - near))
    gathered = jnp.stack(pieces, axis=1)
    received = swapped(gathered, "comp", 0)

    def remap_one_block(triple):
        near_ids, slot_ids, weight_vals = triple
        positions = lax.broadcasted_iota(jnp.int32, (capacity, cell_block), 0)
        total = jnp.zeros((tracers, cell_block), jnp.float32)
        for near in range(neighbours):
            table = jnp.zeros((capacity, cell_block), jnp.float32)
            for k in range(intersections):
                hit = (positions == slot_ids[k][None, :]) & (near_ids[k][None, :] == near)
                table = table + jnp.where(hit, weight_vals[k][None, :], 0.0)
            total = total + jnp.dot(
                received[:, near],
                table,
                precision=lax.Precision.HIGHEST,
                preferred_element_type=jnp.float32,
            )
        return total

    blocks = lax.map(remap_one_block, (near_blocks, slot_blocks, weight_blocks))
    remapped = jnp.transpose(blocks, (1, 0, 2)).reshape(tracers, rows_x, width)
    level0 = field[:, 0]
    masked = sea_mask[0].astype(jnp.float32)
    new0 = level0 + coupling[0] * masked * (remapped - level0)
    field = field.at[:, 0].set(new0)
    for step in range(2):
        padded = with_halo(field, (("tile", 2),), 1)
        field = substep(padded, speed)
    return field[None]


def solution(mesh):
    in_specs = (
        P("comp", None, None, "tile", None),
        P("comp", None, None, "tile", None),
        P("comp", None, "tile", None),
        P("comp", "tile", None),
        P("comp", "tile", None, None),
        P("comp", "tile", None, None),
        P("comp", None, "tile", None),
        P("comp", None, "tile", None),
        P("comp", None, "tile", None),
    )
    out_specs = P("comp", None, None, "tile", None)
    return jax.shard_map(
        per_device, mesh=mesh, in_specs=in_specs, out_specs=out_specs, check_vma=False
    )
```

profile of v0, /device:TPU:1, one launch (start us, length us, event | category | flops | bytes accessed | tf_op | source)
XLA Modules:
  0.0 379.9 jit_solution(10959315775401449040)
XLA Ops:
  2.2 13.5 %while.21 = (s32[]{:T(128)}, f32[8,16,1024]{2,1,0:T(8,128)S(1)}, s32[8,1024]{1,0:T(8,128)S(1)}, f32[16,4,1024]{2,0,1:T(8,128)S(1)}, s32[8,1024]{1,0:T(8,128)S(1)}, /*index=5*/s32[]{:T(128)}) while((s32[]{:T(128)}, f32[8,16,1024]{2,1,0:T(8,128)S(1)}, s32[8,1024]{1,0:T(8,128)S(1)}, f32[16,4,1024]{2,0,1:T(8,128)S(1)}, s32[8,1024]{1,0:T(8,128)S(1)}, ...), condition=%wide.region_2.3_spmd, body=%wide.region_0.2_spmd.sunk | while | flops 806477824 | bytes 516181 | solution.py:76
  2.2 1.6 fusion.309
  3.9 1.6 fusion.309
  5.6 1.6 fusion.309
  14.1 1.6 fusion.309
  16.8 9.3 %collective-permute-start.2 = (f32[16,2048]{1,0:T(8,128)S(1)}, f32[16,2048]{1,0:T(8,128)S(1)}, u32[]{:S(2)}, u32[]{:S(2)}) collective-permute-start(f32[16,2048]{1,0:T(8,128)S(1)} %bitcast.270), channel_id=1, source_target_pairs={{0,63},{1,0},{2,1},{3,2},{4,3},{5,4},{6,5},{7,6},{8,7},{9,8},{10,9... | collective-permute-start | bytes 393224 | tf_op jit(solution)/shard_map/ppermute | solution.py:14
  28.0 3.5 collective-permute-done.3
  31.5 4.2 %collective-permute-done = f32[16,2048]{1,0:T(8,128)S(1)} collective-permute-done((f32[16,2048]{1,0:T(8,128)S(1)}, f32[16,2048]{1,0:T(8,128)S(1)}, u32[]{:S(2)}, u32[]{:S(2)}) %collective-permute-start) | collective-permute-done | bytes 131104 | tf_op jit(solution)/shard_map/ppermute | solution.py:14
  35.8 2.2 collective-permute-start.4
  39.8 306.2 %while.22 = (s32[]{:T(128)}, f32[8,16,512]{2,1,0:T(8,128)S(1)}, s32[8,8,512]{2,0,1:T(8,128)S(1)}, s32[8,8,512]{2,0,1:T(8,128)S(1)}, f32[8,8,512]{2,0,1:T(8,128)S...) while((s32[]{:T(128)}, f32[8,16,512]{2,1,0:T(8,128)S(1)}, ...), condition=%wide.region_4.5_spmd, body=%wide.region_3.4_spmd.sunk | while | flops 935370752 | bytes 2048333 | solution.py:134
  40.7 9.4 %fusion.319 = f32[512,16]{0,1:T(8,128)S(1)} fusion(f32[512]{0:T(512)S(1)} %bitcast.307, s32[512]{0:T(512)S(1)} %bitcast.339, f32[512]{0:T(512)S(1)} %bitcast.283, s32[512]{0:T(512)S(1)} %bitcast.315, f32[512]{0:T(512)S(1)} %bitcast.287, s32[512]{0:T(512)S(1)} %bitcast.319, f32[512]{0:T(512)S(1)} %bitcast.291, s32[512]{0:T(512)S(1)} %bitcast.323, ...), kind=kOutput, calls=%fused_computation.12.clone.1 | convolution fusion | flops 233832448 | bytes 200704 | tf_op jit(solution)/shard_map/while/body/eval_jaxpr/dot_general | solution.py:126
  50.1 9.4 %fusion.320 = f32[512,16]{0,1:T(8,128)S(1)} fusion(f32[512]{0:T(512)S(1)} %bitcast.308, s32[512]{0:T(512)S(1)} %bitcast.340, f32[512]{0:T(512)S(1)} %bitcast.284, s32[512]{0:T(512)S(1)} %bitcast.316, f32[512]{0:T(512)S(1)} %bitcast.288, s32[512]{0:T(512)S(1)} %bitcast.320, f32[512]{0:T(512)S(1)} %bitcast.292, s32[512]{0:T(512)S(1)} %bitcast.324, ...), kind=kOutput, calls=%fused_computation.28.clone.1 | convolution fusion | flops 233832448 | bytes 200704 | tf_op jit(solution)/shard_map/while/body/eval_jaxpr/dot_general | solution.py:126
  59.5 9.4 %fusion.321 = f32[512,16]{0,1:T(8,128)S(1)} fusion(f32[512]{0:T(512)S(1)} %bitcast.309, s32[512]{0:T(512)S(1)} %bitcast.341, f32[512]{0:T(512)S(1)} %bitcast.285, s32[512]{0:T(512)S(1)} %bitcast.317, f32[512]{0:T(512)S(1)} %bitcast.289, s32[512]{0:T(512)S(1)} %bitcast.321, f32[512]{0:T(512)S(1)} %bitcast.293, s32[512]{0:T(512)S(1)} %bitcast.325, ...), kind=kOutput, calls=%fused_computation.44.clone.1 | convolution fusion | flops 233832448 | bytes 200704 | tf_op jit(solution)/shard_map/while/body/eval_jaxpr/dot_general | solution.py:126
  68.9 9.4 %fusion.322 = f32[8,16,512]{2,1,0:T(8,128)S(1)} fusion(f32[8,16,512]{2,1,0:T(8,128)S(1)} %get-tuple-element.398, s32[]{:T(128)S(6)} %copy.102, f32[512,16]{0,1:T(8,128)S(1)} %fusion.319, f32[512,16]{0,1:T(8,128)S(1)} %fusion.320, f32[512,16]{0,1:T(8,128)S(1)} %fusion.321, f32[512]{0:T(512)S(1)} %bitcast.310, s32[512]{0:T(512)S(1)} %bitcast.342, ...), kind=kOutput, calls=%fused_computation.220.clone.1 | convolution fusion | flops 233857024 | bytes 299012 | tf_op jit(solution)/shard_map/while/body/eval_jaxpr/dot_general | solution.py:126
  79.0 9.4 %fusion.319 = f32[512,16]{0,1:T(8,128)S(1)} fusion(f32[512]{0:T(512)S(1)} %bitcast.307, s32[512]{0:T(512)S(1)} %bitcast.339, f32[512]{0:T(512)S(1)} %bitcast.283, s32[512]{0:T(512)S(1)} %bitcast.315, f32[512]{0:T(512)S(1)} %bitcast.287, s32[512]{0:T(512)S(1)} %bitcast.319, f32[512]{0:T(512)S(1)} %bitcast.291, s32[512]{0:T(512)S(1)} %bitcast.323, ...), kind=kOutput, calls=%fused_computation.12.clone.1 | convolution fusion | flops 233832448 | bytes 200704 | tf_op jit(solution)/shard_map/while/body/eval_jaxpr/dot_general | solution.py:126
  88.3 9.4 %fusion.320 = f32[512,16]{0,1:T(8,128)S(1)} fusion(f32[512]{0:T(512)S(1)} %bitcast.308, s32[512]{0:T(512)S(1)} %bitcast.340, f32[512]{0:T(512)S(1)} %bitcast.284, s32[512]{0:T(512)S(1)} %bitcast.316, f32[512]{0:T(512)S(1)} %bitcast.288, s32[512]{0:T(512)S(1)} %bitcast.320, f32[512]{0:T(512)S(1)} %bitcast.292, s32[512]{0:T(512)S(1)} %bitcast.324, ...), kind=kOutput, calls=%fused_computation.28.clone.1 | convolution fusion | flops 233832448 | bytes 200704 | tf_op jit(solution)/shard_map/while/body/eval_jaxpr/dot_general | solution.py:126
  97.7 9.4 %fusion.321 = f32[512,16]{0,1:T(8,128)S(1)} fusion(f32[512]{0:T(512)S(1)} %bitcast.309, s32[512]{0:T(512)S(1)} %bitcast.341, f32[512]{0:T(512)S(1)} %bitcast.285, s32[512]{0:T(512)S(1)} %bitcast.317, f32[512]{0:T(512)S(1)} %bitcast.289, s32[512]{0:T(512)S(1)} %bitcast.321, f32[512]{0:T(512)S(1)} %bitcast.293, s32[512]{0:T(512)S(1)} %bitcast.325, ...), kind=kOutput, calls=%fused_computation.44.clone.1 | convolution fusion | flops 233832448 | bytes 200704 | tf_op jit(solution)/shard_map/while/body/eval_jaxpr/dot_general | solution.py:126
  107.1 9.4 %fusion.322 = f32[8,16,512]{2,1,0:T(8,128)S(1)} fusion(f32[8,16,512]{2,1,0:T(8,128)S(1)} %get-tuple-element.398, s32[]{:T(128)S(6)} %copy.102, f32[512,16]{0,1:T(8,128)S(1)} %fusion.319, f32[512,16]{0,1:T(8,128)S(1)} %fusion.320, f32[512,16]{0,1:T(8,128)S(1)} %fusion.321, f32[512]{0:T(512)S(1)} %bitcast.310, s32[512]{0:T(512)S(1)} %bitcast.342, ...), kind=kOutput, calls=%fused_computation.220.clone.1 | convolution fusion | flops 233857024 | bytes 299012 | tf_op jit(solution)/shard_map/while/body/eval_jaxpr/dot_general | solution.py:126
  117.2 9.4 %fusion.319 = f32[512,16]{0,1:T(8,128)S(1)} fusion(f32[512]{0:T(512)S(1)} %bitcast.307, s32[512]{0:T(512)S(1)} %bitcast.339, f32[512]{0:T(512)S(1)} %bitcast.283, s32[512]{0:T(512)S(1)} %bitcast.315, f32[512]{0:T(512)S(1)} %bitcast.287, s32[512]{0:T(512)S(1)} %bitcast.319, f32[512]{0:T(512)S(1)} %bitcast.291, s32[512]{0:T(512)S(1)} %bitcast.323, ...), kind=kOutput, calls=%fused_computation.12.clone.1 | convolution fusion | flops 233832448 | bytes 200704 | tf_op jit(solution)/shard_map/while/body/eval_jaxpr/dot_general | solution.py:126
  126.5 9.4 %fusion.320 = f32[512,16]{0,1:T(8,128)S(1)} fusion(f32[512]{0:T(512)S(1)} %bitcast.308, s32[512]{0:T(512)S(1)} %bitcast.340, f32[512]{0:T(512)S(1)} %bitcast.284, s32[512]{0:T(512)S(1)} %bitcast.316, f32[512]{0:T(512)S(1)} %bitcast.288, s32[512]{0:T(512)S(1)} %bitcast.320, f32[512]{0:T(512)S(1)} %bitcast.292, s32[512]{0:T(512)S(1)} %bitcast.324, ...), kind=kOutput, calls=%fused_computation.28.clone.1 | convolution fusion | flops 233832448 | bytes 200704 | tf_op jit(solution)/shard_map/while/body/eval_jaxpr/dot_general | solution.py:126
  135.9 9.4 %fusion.321 = f32[512,16]{0,1:T(8,128)S(1)} fusion(f32[512]{0:T(512)S(1)} %bitcast.309, s32[512]{0:T(512)S(1)} %bitcast.341, f32[512]{0:T(512)S(1)} %bitcast.285, s32[512]{0:T(512)S(1)} %bitcast.317, f32[512]{0:T(512)S(1)} %bitcast.289, s32[512]{0:T(512)S(1)} %bitcast.321, f32[512]{0:T(512)S(1)} %bitcast.293, s32[512]{0:T(512)S(1)} %bitcast.325, ...), kind=kOutput, calls=%fused_computation.44.clone.1 | convolution fusion | flops 233832448 | bytes 200704 | tf_op jit(solution)/shard_map/while/body/eval_jaxpr/dot_general | solution.py:126
  145.3 9.4 %fusion.322 = f32[8,16,512]{2,1,0:T(8,128)S(1)} fusion(f32[8,16,512]{2,1,0:T(8,128)S(1)} %get-tuple-element.398, s32[]{:T(128)S(6)} %copy.102, f32[512,16]{0,1:T(8,128)S(1)} %fusion.319, f32[512,16]{0,1:T(8,128)S(1)} %fusion.320, f32[512,16]{0,1:T(8,128)S(1)} %fusion.321, f32[512]{0:T(512)S(1)} %bitcast.310, s32[512]{0:T(512)S(1)} %bitcast.342, ...), kind=kOutput, calls=%fused_computation.220.clone.1 | convolution fusion | flops 233857024 | bytes 299012 | tf_op jit(solution)/shard_map/while/body/eval_jaxpr/dot_general | solution.py:126
  155.4 9.4 %fusion.319 = f32[512,16]{0,1:T(8,128)S(1)} fusion(f32[512]{0:T(512)S(1)} %bitcast.307, s32[512]{0:T(512)S(1)} %bitcast.339, f32[512]{0:T(512)S(1)} %bitcast.283, s32[512]{0:T(512)S(1)} %bitcast.315, f32[512]{0:T(512)S(1)} %bitcast.287, s32[512]{0:T(512)S(1)} %bitcast.319, f32[512]{0:T(512)S(1)} %bitcast.291, s32[512]{0:T(512)S(1)} %bitcast.323, ...), kind=kOutput, calls=%fused_computation.12.clone.1 | convolution fusion | flops 233832448 | bytes 200704 | tf_op jit(solution)/shard_map/while/body/eval_jaxpr/dot_general | solution.py:126
  164.8 9.4 %fusion.320 = f32[512,16]{0,1:T(8,128)S(1)} fusion(f32[512]{0:T(512)S(1)} %bitcast.308, s32[512]{0:T(512)S(1)} %bitcast.340, f32[512]{0:T(512)S(1)} %bitcast.284, s32[512]{0:T(512)S(1)} %bitcast.316, f32[512]{0:T(512)S(1)} %bitcast.288, s32[512]{0:T(512)S(1)} %bitcast.320, f32[512]{0:T(512)S(1)} %bitcast.292, s32[512]{0:T(512)S(1)} %bitcast.324, ...), kind=kOutput, calls=%fused_computation.28.clone.1 | convolution fusion | flops 233832448 | bytes 200704 | tf_op jit(solution)/shard_map/while/body/eval_jaxpr/dot_general | solution.py:126
  174.1 9.4 %fusion.321 = f32[512,16]{0,1:T(8,128)S(1)} fusion(f32[512]{0:T(512)S(1)} %bitcast.309, s32[512]{0:T(512)S(1)} %bitcast.341, f32[512]{0:T(512)S(1)} %bitcast.285, s32[512]{0:T(512)S(1)} %bitcast.317, f32[512]{0:T(512)S(1)} %bitcast.289, s32[512]{0:T(512)S(1)} %bitcast.321, f32[512]{0:T(512)S(1)} %bitcast.293, s32[512]{0:T(512)S(1)} %bitcast.325, ...), kind=kOutput, calls=%fused_computation.44.clone.1 | convolution fusion | flops 233832448 | bytes 200704 | tf_op jit(solution)/shard_map/while/body/eval_jaxpr/dot_general | solution.py:126
  183.5 9.4 %fusion.322 = f32[8,16,512]{2,1,0:T(8,128)S(1)} fusion(f32[8,16,512]{2,1,0:T(8,128)S(1)} %get-tuple-element.398, s32[]{:T(128)S(6)} %copy.102, f32[512,16]{0,1:T(8,128)S(1)} %fusion.319, f32[512,16]{0,1:T(8,128)S(1)} %fusion.320, f32[512,16]{0,1:T(8,128)S(1)} %fusion.321, f32[512]{0:T(512)S(1)} %bitcast.310, s32[512]{0:T(512)S(1)} %bitcast.342, ...), kind=kOutput, calls=%fused_computation.220.clone.1 | convolution fusion | flops 233857024 | bytes 299012 | tf_op jit(solution)/shard_map/while/body/eval_jaxpr/dot_general | solution.py:126
  193.6 9.4 %fusion.319 = f32[512,16]{0,1:T(8,128)S(1)} fusion(f32[512]{0:T(512)S(1)} %bitcast.307, s32[512]{0:T(512)S(1)} %bitcast.339, f32[512]{0:T(512)S(1)} %bitcast.283, s32[512]{0:T(512)S(1)} %bitcast.315, f32[512]{0:T(512)S(1)} %bitcast.287, s32[512]{0:T(512)S(1)} %bitcast.319, f32[512]{0:T(512)S(1)} %bitcast.291, s32[512]{0:T(512)S(1)} %bitcast.323, ...), kind=kOutput, calls=%fused_computation.12.clone.1 | convolution fusion | flops 233832448 | bytes 200704 | tf_op jit(solution)/shard_map/while/body/eval_jaxpr/dot_general | solution.py:126
  203.0 9.4 %fusion.320 = f32[512,16]{0,1:T(8,128)S(1)} fusion(f32[512]{0:T(512)S(1)} %bitcast.308, s32[512]{0:T(512)S(1)} %bitcast.340, f32[512]{0:T(512)S(1)} %bitcast.284, s32[512]{0:T(512)S(1)} %bitcast.316, f32[512]{0:T(512)S(1)} %bitcast.288, s32[512]{0:T(512)S(1)} %bitcast.320, f32[512]{0:T(512)S(1)} %bitcast.292, s32[512]{0:T(512)S(1)} %bitcast.324, ...), kind=kOutput, calls=%fused_computation.28.clone.1 | convolution fusion | flops 233832448 | bytes 200704 | tf_op jit(solution)/shard_map/while/body/eval_jaxpr/dot_general | solution.py:126
  212.4 9.4 %fusion.321 = f32[512,16]{0,1:T(8,128)S(1)} fusion(f32[512]{0:T(512)S(1)} %bitcast.309, s32[512]{0:T(512)S(1)} %bitcast.341, f32[512]{0:T(512)S(1)} %bitcast.285, s32[512]{0:T(512)S(1)} %bitcast.317, f32[512]{0:T(512)S(1)} %bitcast.289, s32[512]{0:T(512)S(1)} %bitcast.321, f32[512]{0:T(512)S(1)} %bitcast.293, s32[512]{0:T(512)S(1)} %bitcast.325, ...), kind=kOutput, calls=%fused_computation.44.clone.1 | convolution fusion | flops 233832448 | bytes 200704 | tf_op jit(solution)/shard_map/while/body/eval_jaxpr/dot_general | solution.py:126
  221.7 9.4 %fusion.322 = f32[8,16,512]{2,1,0:T(8,128)S(1)} fusion(f32[8,16,512]{2,1,0:T(8,128)S(1)} %get-tuple-element.398, s32[]{:T(128)S(6)} %copy.102, f32[512,16]{0,1:T(8,128)S(1)} %fusion.319, f32[512,16]{0,1:T(8,128)S(1)} %fusion.320, f32[512,16]{0,1:T(8,128)S(1)} %fusion.321, f32[512]{0:T(512)S(1)} %bitcast.310, s32[512]{0:T(512)S(1)} %bitcast.342, ...), kind=kOutput, calls=%fused_computation.220.clone.1 | convolution fusion | flops 233857024 | bytes 299012 | tf_op jit(solution)/shard_map/while/body/eval_jaxpr/dot_general | solution.py:126
  231.8 9.4 %fusion.319 = f32[512,16]{0,1:T(8,128)S(1)} fusion(f32[512]{0:T(512)S(1)} %bitcast.307, s32[512]{0:T(512)S(1)} %bitcast.339, f32[512]{0:T(512)S(1)} %bitcast.283, s32[512]{0:T(512)S(1)} %bitcast.315, f32[512]{0:T(512)S(1)} %bitcast.287, s32[512]{0:T(512)S(1)} %bitcast.319, f32[512]{0:T(512)S(1)} %bitcast.291, s32[512]{0:T(512)S(1)} %bitcast.323, ...), kind=kOutput, calls=%fused_computation.12.clone.1 | convolution fusion | flops 233832448 | bytes 200704 | tf_op jit(solution)/shard_map/while/body/eval_jaxpr/dot_general | solution.py:126
  241.2 9.4 %fusion.320 = f32[512,16]{0,1:T(8,128)S(1)} fusion(f32[512]{0:T(512)S(1)} %bitcast.308, s32[512]{0:T(512)S(1)} %bitcast.340, f32[512]{0:T(512)S(1)} %bitcast.284, s32[512]{0:T(512)S(1)} %bitcast.316, f32[512]{0:T(512)S(1)} %bitcast.288, s32[512]{0:T(512)S(1)} %bitcast.320, f32[512]{0:T(512)S(1)} %bitcast.292, s32[512]{0:T(512)S(1)} %bitcast.324, ...), kind=kOutput, calls=%fused_computation.28.clone.1 | convolution fusion | flops 233832448 | bytes 200704 | tf_op jit(solution)/shard_map/while/body/eval_jaxpr/dot_general | solution.py:126
  250.6 9.4 %fusion.321 = f32[512,16]{0,1:T(8,128)S(1)} fusion(f32[512]{0:T(512)S(1)} %bitcast.309, s32[512]{0:T(512)S(1)} %bitcast.341, f32[512]{0:T(512)S(1)} %bitcast.285, s32[512]{0:T(512)S(1)} %bitcast.317, f32[512]{0:T(512)S(1)} %bitcast.289, s32[512]{0:T(512)S(1)} %bitcast.321, f32[512]{0:T(512)S(1)} %bitcast.293, s32[512]{0:T(512)S(1)} %bitcast.325, ...), kind=kOutput, calls=%fused_computation.44.clone.1 | convolution fusion | flops 233832448 | bytes 200704 | tf_op jit(solution)/shard_map/while/body/eval_jaxpr/dot_general | solution.py:126
  260.0 9.4 %fusion.322 = f32[8,16,512]{2,1,0:T(8,128)S(1)} fusion(f32[8,16,512]{2,1,0:T(8,128)S(1)} %get-tuple-element.398, s32[]{:T(128)S(6)} %copy.102, f32[512,16]{0,1:T(8,128)S(1)} %fusion.319, f32[512,16]{0,1:T(8,128)S(1)} %fusion.320, f32[512,16]{0,1:T(8,128)S(1)} %fusion.321, f32[512]{0:T(512)S(1)} %bitcast.310, s32[512]{0:T(512)S(1)} %bitcast.342, ...), kind=kOutput, calls=%fused_computation.220.clone.1 | convolution fusion | flops 233857024 | bytes 299012 | tf_op jit(solution)/shard_map/while/body/eval_jaxpr/dot_general | solution.py:126
  270.1 9.4 %fusion.319 = f32[512,16]{0,1:T(8,128)S(1)} fusion(f32[512]{0:T(512)S(1)} %bitcast.307, s32[512]{0:T(512)S(1)} %bitcast.339, f32[512]{0:T(512)S(1)} %bitcast.283, s32[512]{0:T(512)S(1)} %bitcast.315, f32[512]{0:T(512)S(1)} %bitcast.287, s32[512]{0:T(512)S(1)} %bitcast.319, f32[512]{0:T(512)S(1)} %bitcast.291, s32[512]{0:T(512)S(1)} %bitcast.323, ...), kind=kOutput, calls=%fused_computation.12.clone.1 | convolution fusion | flops 233832448 | bytes 200704 | tf_op jit(solution)/shard_map/while/body/eval_jaxpr/dot_general | solution.py:126
  279.4 9.4 %fusion.320 = f32[512,16]{0,1:T(8,128)S(1)} fusion(f32[512]{0:T(512)S(1)} %bitcast.308, s32[512]{0:T(512)S(1)} %bitcast.340, f32[512]{0:T(512)S(1)} %bitcast.284, s32[512]{0:T(512)S(1)} %bitcast.316, f32[512]{0:T(512)S(1)} %bitcast.288, s32[512]{0:T(512)S(1)} %bitcast.320, f32[512]{0:T(512)S(1)} %bitcast.292, s32[512]{0:T(512)S(1)} %bitcast.324, ...), kind=kOutput, calls=%fused_computation.28.clone.1 | convolution fusion | flops 233832448 | bytes 200704 | tf_op jit(solution)/shard_map/while/body/eval_jaxpr/dot_general | solution.py:126
  288.8 9.4 %fusion.321 = f32[512,16]{0,1:T(8,128)S(1)} fusion(f32[512]{0:T(512)S(1)} %bitcast.309, s32[512]{0:T(512)S(1)} %bitcast.341, f32[512]{0:T(512)S(1)} %bitcast.285, s32[512]{0:T(512)S(1)} %bitcast.317, f32[512]{0:T(512)S(1)} %bitcast.289, s32[512]{0:T(512)S(1)} %bitcast.321, f32[512]{0:T(512)S(1)} %bitcast.293, s32[512]{0:T(512)S(1)} %bitcast.325, ...), kind=kOutput, calls=%fused_computation.44.clone.1 | convolution fusion | flops 233832448 | bytes 200704 | tf_op jit(solution)/shard_map/while/body/eval_jaxpr/dot_general | solution.py:126
  298.2 9.4 %fusion.322 = f32[8,16,512]{2,1,0:T(8,128)S(1)} fusion(f32[8,16,512]{2,1,0:T(8,128)S(1)} %get-tuple-element.398, s32[]{:T(128)S(6)} %copy.102, f32[512,16]{0,1:T(8,128)S(1)} %fusion.319, f32[512,16]{0,1:T(8,128)S(1)} %fusion.320, f32[512,16]{0,1:T(8,128)S(1)} %fusion.321, f32[512]{0:T(512)S(1)} %bitcast.310, s32[512]{0:T(512)S(1)} %bitcast.342, ...), kind=kOutput, calls=%fused_computation.220.clone.1 | convolution fusion | flops 233857024 | bytes 299012 | tf_op jit(solution)/shard_map/while/body/eval_jaxpr/dot_general | solution.py:126
  308.3 9.4 %fusion.319 = f32[512,16]{0,1:T(8,128)S(1)} fusion(f32[512]{0:T(512)S(1)} %bitcast.307, s32[512]{0:T(512)S(1)} %bitcast.339, f32[512]{0:T(512)S(1)} %bitcast.283, s32[512]{0:T(512)S(1)} %bitcast.315, f32[512]{0:T(512)S(1)} %bitcast.287, s32[512]{0:T(512)S(1)} %bitcast.319, f32[512]{0:T(512)S(1)} %bitcast.291, s32[512]{0:T(512)S(1)} %bitcast.323, ...), kind=kOutput, calls=%fused_computation.12.clone.1 | convolution fusion | flops 233832448 | bytes 200704 | tf_op jit(solution)/shard_map/while/body/eval_jaxpr/dot_general | solution.py:126
  317.6 9.4 %fusion.320 = f32[512,16]{0,1:T(8,128)S(1)} fusion(f32[512]{0:T(512)S(1)} %bitcast.308, s32[512]{0:T(512)S(1)} %bitcast.340, f32[512]{0:T(512)S(1)} %bitcast.284, s32[512]{0:T(512)S(1)} %bitcast.316, f32[512]{0:T(512)S(1)} %bitcast.288, s32[512]{0:T(512)S(1)} %bitcast.320, f32[512]{0:T(512)S(1)} %bitcast.292, s32[512]{0:T(512)S(1)} %bitcast.324, ...), kind=kOutput, calls=%fused_computation.28.clone.1 | convolution fusion | flops 233832448 | bytes 200704 | tf_op jit(solution)/shard_map/while/body/eval_jaxpr/dot_general | solution.py:126
  327.0 9.4 %fusion.321 = f32[512,16]{0,1:T(8,128)S(1)} fusion(f32[512]{0:T(512)S(1)} %bitcast.309, s32[512]{0:T(512)S(1)} %bitcast.341, f32[512]{0:T(512)S(1)} %bitcast.285, s32[512]{0:T(512)S(1)} %bitcast.317, f32[512]{0:T(512)S(1)} %bitcast.289, s32[512]{0:T(512)S(1)} %bitcast.321, f32[512]{0:T(512)S(1)} %bitcast.293, s32[512]{0:T(512)S(1)} %bitcast.325, ...), kind=kOutput, calls=%fused_computation.44.clone.1 | convolution fusion | flops 233832448 | bytes 200704 | tf_op jit(solution)/shard_map/while/body/eval_jaxpr/dot_general | solution.py:126
  336.4 9.4 %fusion.322 = f32[8,16,512]{2,1,0:T(8,128)S(1)} fusion(f32[8,16,512]{2,1,0:T(8,128)S(1)} %get-tuple-element.398, s32[]{:T(128)S(6)} %copy.102, f32[512,16]{0,1:T(8,128)S(1)} %fusion.319, f32[512,16]{0,1:T(8,128)S(1)} %fusion.320, f32[512,16]{0,1:T(8,128)S(1)} %fusion.321, f32[512]{0:T(512)S(1)} %bitcast.310, s32[512]{0:T(512)S(1)} %bitcast.342, ...), kind=kOutput, calls=%fused_computation.220.clone.1 | convolution fusion | flops 233857024 | bytes 299012 | tf_op jit(solution)/shard_map/while/body/eval_jaxpr/dot_general | solution.py:126
  349.0 6.9 %collective-permute-start.5 = (f32[16,4,1,1024]{3,2,1,0:T(1,128)S(1)}, f32[16,4,1,1024]{3,2,1,0:T(1,128)S(1)}, u32[]{:S(2)}, u32[]{:S(2)}) collective-permute-start(f32[16,4,1,1024]{3,2,1,0:T(1,128)S(1)} %get-tuple-element.177), channel_id=1, source_target_pairs={{1,0},{2,1},{3,2},{4,3},{5,4},{6,5},{7,6},{8,7},{9,8},{10,9},{11,1... | collective-permute-start | bytes 786440 | tf_op jit(solution)/shard_map/ppermute | solution.py:31
  356.6 5.3 %collective-permute-done.6 = f32[16,4,1,1024]{3,2,1,0:T(1,128)S(1)} collective-permute-done((f32[16,4,1,1024]{3,2,1,0:T(1,128)S(1)}, f32[16,4,1,1024]{3,2,1,0:T(1,128)S(1)}, u32[]{:S(2)}, u32[]{:S(2)}) %collective-permute-start.6) | collective-permute-done | bytes 262176 | tf_op jit(solution)/shard_map/ppermute | solution.py:30
  361.9 2.2 multiply_add_fusion
  364.8 6.9 %collective-permute-start.7 = (f32[16,4,1,1024]{3,2,1,0:T(1,128)S(1)}, f32[16,4,1,1024]{3,2,1,0:T(1,128)S(1)}, u32[]{:S(2)}, u32[]{:S(2)}) collective-permute-start(f32[16,4,1,1024]{3,2,1,0:T(1,128)S(1)} %get-tuple-element.171), channel_id=1, source_target_pairs={{1,0},{2,1},{3,2},{4,3},{5,4},{6,5},{7,6},{8,7},{9,8},{10,9},{11,1... | collective-permute-start | bytes 786440 | tf_op jit(solution)/shard_map/ppermute | solution.py:31
  372.5 4.3 %collective-permute-done.8 = f32[16,4,1,1024]{3,2,1,0:T(1,128)S(1)} collective-permute-done((f32[16,4,1,1024]{3,2,1,0:T(1,128)S(1)}, f32[16,4,1,1024]{3,2,1,0:T(1,128)S(1)}, u32[]{:S(2)}, u32[]{:S(2)}) %collective-permute-start.8) | collective-permute-done | bytes 262176 | tf_op jit(solution)/shard_map/ppermute | solution.py:30
  376.8 3.0 add_bitcast_fusion
  (122 shorter events, 24.1 us)
Async XLA Ops:
  0.0 1.2 copy-start.8
  0.0 1.3 copy-start.9
  1.2 1.0 copy-start
  16.7 21.3 %copy-start.4 = (s32[1,8,4,1024]{3,2,1,0:T(4,128)S(1)}, s32[1,8,4,1024]{3,2,1,0:T(4,128)}, u32[]{:S(2)}) copy-start(s32[1,8,4,1024]{3,2,1,0:T(4,128)} %param.21) | copy-start | bytes 393220
  16.8 11.2 %collective-permute-start.2 = (f32[16,2048]{1,0:T(8,128)S(1)}, f32[16,2048]{1,0:T(8,128)S(1)}, u32[]{:S(2)}, u32[]{:S(2)}) collective-permute-start(f32[16,2048]{1,0:T(8,128)S(1)} %bitcast.270), channel_id=1, source_target_pairs={{0,63},{1,0},{2,1},{3,2},{4,3},{5,4},{6,5},{7,6},{8,7},{9,8},{10,9... | collective-permute-start | bytes 393224 | tf_op jit(solution)/shard_map/ppermute | solution.py:14
  26.1 12.0 %copy-start.5 = (s32[1,8,4,1024]{3,2,1,0:T(4,128)S(1)}, s32[1,8,4,1024]{3,2,1,0:T(4,128)}, u32[]{:S(2)}) copy-start(s32[1,8,4,1024]{3,2,1,0:T(4,128)} %param.22) | copy-start | bytes 393220
  26.1 5.4 %collective-permute-start.3 = (f32[16,2048]{1,0:T(8,128)S(1)}, f32[16,2048]{1,0:T(8,128)S(1)}, u32[]{:S(2)}, u32[]{:S(2)}) collective-permute-start(f32[16,2048]{1,0:T(8,128)S(1)} %bitcast.271), channel_id=1, source_target_pairs={{0,62},{1,63},{2,0},{3,1},{4,2},{5,3},{6,4},{7,5},{8,6},{9,7},{10,... | collective-permute-start | bytes 393224 | tf_op jit(solution)/shard_map/ppermute | solution.py:14
  26.2 11.9 %copy-start.6 = (f32[1,8,4,1024]{3,2,1,0:T(4,128)S(1)}, f32[1,8,4,1024]{3,2,1,0:T(4,128)}, u32[]{:S(2)}) copy-start(f32[1,8,4,1024]{3,2,1,0:T(4,128)} %param.23) | copy-start | bytes 393220
  26.3 5.2 %collective-permute-start.1 = (f32[16,2048]{1,0:T(8,128)S(1)}, f32[16,2048]{1,0:T(8,128)S(1)}, u32[]{:S(2)}, u32[]{:S(2)}) collective-permute-start(f32[16,2048]{1,0:T(8,128)S(1)} %bitcast.272), channel_id=1, source_target_pairs={{0,0},{1,1},{2,2},{3,3},{4,4},{5,5},{6,6},{7,7},{8,8},{9,9},{10,10... | collective-permute-start | bytes 393224 | tf_op jit(solution)/shard_map/ppermute | solution.py:14
  26.3 11.9 %copy-start.10 = (s32[1,4,1024]{2,1,0:T(4,128)S(1)}, s32[1,4,1024]{2,1,0:T(4,128)}, u32[]{:S(2)}) copy-start(s32[1,4,1024]{2,1,0:T(4,128)} %param.18) | copy-start | bytes 49156
  26.3 12.5 %copy-start.7 = (f32[1,2,4,4,1024]{4,3,2,1,0:T(4,128)S(1)}, f32[1,2,4,4,1024]{4,3,2,1,0:T(4,128)}, u32[]{:S(2)}) copy-start(f32[1,2,4,4,1024]{4,3,2,1,0:T(4,128)} %param.16) | copy-start | bytes 393220
  26.4 9.4 %collective-permute-start = (f32[16,2048]{1,0:T(8,128)S(1)}, f32[16,2048]{1,0:T(8,128)S(1)}, u32[]{:S(2)}, u32[]{:S(2)}) collective-permute-start(f32[16,2048]{1,0:T(8,128)S(1)} %bitcast.273), channel_id=1, source_target_pairs={{0,1},{1,2},{2,3},{3,4},{4,5},{5,6},{6,7},{7,8},{8,9},{9,10},{10,1... | collective-permute-start | bytes 393224 | tf_op jit(solution)/shard_map/ppermute | solution.py:14
  35.8 3.7 collective-permute-start.4
  346.0 1.2 copy-start.1
  348.9 13.0 %collective-permute-start.6 = (f32[16,4,1,1024]{3,2,1,0:T(1,128)S(1)}, f32[16,4,1,1024]{3,2,1,0:T(1,128)S(1)}, u32[]{:S(2)}, u32[]{:S(2)}) collective-permute-start(f32[16,4,1,1024]{3,2,1,0:T(1,128)S(1)} %get-tuple-element.176), channel_id=1, source_target_pairs={{0,1},{1,2},{2,3},{3,4},{4,5},{5,6},{6,7},{7,8},{8,9},{9,10},{10,1... | collective-permute-start | bytes 786440 | tf_op jit(solution)/shard_map/ppermute | solution.py:30
  349.0 12.9 %copy-start.2 = (f32[4,4,1024]{2,1,0:T(4,128)S(1)}, f32[4,4,1024]{2,1,0:T(4,128)}, u32[]{:S(2)}) copy-start(f32[4,4,1024]{2,1,0:T(4,128)} %get-tuple-element.186) | copy-start | bytes 196612
  349.0 12.9 %copy-start.3 = (f32[4,4,1024]{2,1,0:T(4,128)S(1)}, f32[4,4,1024]{2,1,0:T(4,128)}, u32[]{:S(2)}) copy-start(f32[4,4,1024]{2,1,0:T(4,128)} %get-tuple-element.187) | copy-start | bytes 196612
  349.0 12.9 %collective-permute-start.5 = (f32[16,4,1,1024]{3,2,1,0:T(1,128)S(1)}, f32[16,4,1,1024]{3,2,1,0:T(1,128)S(1)}, u32[]{:S(2)}, u32[]{:S(2)}) collective-permute-start(f32[16,4,1,1024]{3,2,1,0:T(1,128)S(1)} %get-tuple-element.177), channel_id=1, source_target_pairs={{1,0},{2,1},{3,2},{4,3},{5,4},{6,5},{7,6},{8,7},{9,8},{10,9},{11,1... | collective-permute-start | bytes 786440 | tf_op jit(solution)/shard_map/ppermute | solution.py:31
  364.7 12.1 %collective-permute-start.8 = (f32[16,4,1,1024]{3,2,1,0:T(1,128)S(1)}, f32[16,4,1,1024]{3,2,1,0:T(1,128)S(1)}, u32[]{:S(2)}, u32[]{:S(2)}) collective-permute-start(f32[16,4,1,1024]{3,2,1,0:T(1,128)S(1)} %get-tuple-element.170), channel_id=1, source_target_pairs={{0,1},{1,2},{2,3},{3,4},{4,5},{5,6},{6,7},{7,8},{8,9},{9,10},{10,1... | collective-permute-start | bytes 786440 | tf_op jit(solution)/shard_map/ppermute | solution.py:30
  364.8 12.0 %collective-permute-start.7 = (f32[16,4,1,1024]{3,2,1,0:T(1,128)S(1)}, f32[16,4,1,1024]{3,2,1,0:T(1,128)S(1)}, u32[]{:S(2)}, u32[]{:S(2)}) collective-permute-start(f32[16,4,1,1024]{3,2,1,0:T(1,128)S(1)} %get-tuple-element.171), channel_id=1, source_target_pairs={{1,0},{2,1},{3,2},{4,3},{5,4},{6,5},{7,6},{8,7},{9,8},{10,9},{11,1... | collective-permute-start | bytes 786440 | tf_op jit(solution)/shard_map/ppermute | solution.py:31
where the time goes:
time: 381 us; the launch traced here: 380 us
  matrix products  313 us (82%)
  starting transfers between devices  26.2 us (7%)
  waiting for transfers between devices  18.3 us (5%)
  local copies, waits for them, and re-layouts  11.4 us (3%)
  other arithmetic  9.55 us (3%)
    dot_general x32, matrix products, remap_one_block(): jnp.dot(received[:, near], table, precision=lax.Precision.HIGHEST, prefer...  300 us
    ppermute x2, starting transfers between devices, with_halo(): after = lax.ppermute(first, axis, down)  13.7 us
    dot_general x8, matrix products, pack_one_block(): jnp.einsum('qry,ys->qrs', surface, col_hot, precision=lax.Precision.HIGHE...  12.9 us
    ppermute x4, starting transfers between devices, passed_along(): return lax.ppermute(value, axis, pairs)  10.1 us
    ppermute x2, waiting for transfers between devices, with_halo(): before = lax.ppermute(last, axis, up)  9.6 us
    ppermute x4, waiting for transfers between devices, passed_along(): return lax.ppermute(value, axis, pairs)  8.62 us
  transfers between devices with their start and end apart: 9, of which 5 were waited for; matrix products, arithmetic and copies ran while one was open for 1% of the time, Pallas kernels for 0%

commit v1 on v0

v1 whole, which is shorter than its diff:
```python
import functools

import jax
import jax.numpy as jnp
from jax import lax
from jax.experimental import pallas as pl
from jax.experimental.pallas import tpu as pltpu
from jax.sharding import PartitionSpec as P

diffusion = 0.12
LOW = 128
VMEM_LIMIT = 48 * 2**20


def moved(value, steps, swap):
    tiles = lax.axis_size("tile")
    pairs = []
    for comp in range(lax.axis_size("comp")):
        for tile in range(tiles):
            target = (comp ^ 1 if swap else comp) * tiles + (tile + steps) % tiles
            pairs.append((comp * tiles + tile, target))
    return lax.ppermute(value, ("comp", "tile"), pairs)


def put_table(table, source, first, count):
    tracers = source.shape[0]
    for high in range(count):
        value = source[:, high * LOW : (high + 1) * LOW]
        leading = value.astype(jnp.bfloat16)
        rest = (value - leading.astype(jnp.float32)).astype(jnp.bfloat16)
        row = (first + high) * tracers
        table[row : row + tracers, :] = jnp.concatenate([leading, rest], axis=1)


def one_hot(low):
    width = low.shape[1]
    position = lax.broadcasted_iota(jnp.int32, (LOW, width), 0).astype(jnp.float32).astype(jnp.bfloat16)
    wanted = jnp.broadcast_to(low.astype(jnp.float32), (16, width)).astype(jnp.bfloat16)
    wanted = jnp.concatenate([wanted] * (LOW // 16), axis=0)
    return jnp.where(position == wanted, jnp.bfloat16(1), jnp.bfloat16(0))


def chosen(values, high):
    bit = 0
    while len(values) > 1:
        odd = ((high >> bit) & 1) == 1
        values = [jnp.where(odd, values[i + 1], values[i]) for i in range(0, len(values), 2)]
        bit += 1
    return values[0]


def looked_up(table, entry, tracers):
    width = entry.shape[1]
    highs = table.shape[0] // tracers
    hot = one_hot(entry & (LOW - 1))
    hot = jnp.concatenate([hot, hot], axis=0)
    product = jnp.dot(table[...], hot, preferred_element_type=jnp.float32)
    high = jnp.broadcast_to(entry // LOW, (tracers, width))
    return chosen([product[tracers * h : tracers * (h + 1)] for h in range(highs)], high)


def pack_kernel(surface, rows, cols, *rest):
    outs, table = rest[:-1], rest[-1]
    tracers, cells = surface.shape
    capacity = rows.shape[1]
    width = cells // 4
    put_table(table, surface, 0, cells // LOW)
    block = 512

    for near, out in enumerate(outs):

        def body(step, carry, near=near, out=out):
            at = pl.ds(pl.multiple_of(step * block, block), block)
            entry = rows[near : near + 1, at] * width + cols[near : near + 1, at]
            out[:, at] = looked_up(table, entry, tracers)
            return carry

        lax.fori_loop(0, capacity // block, body, 0)


def pack(surface, rows, cols):
    tracers, cells = surface.shape
    neighbours, capacity = rows.shape
    return pl.pallas_call(
        pack_kernel,
        out_shape=[jax.ShapeDtypeStruct((tracers, capacity), jnp.float32)] * neighbours,
        scratch_shapes=[pltpu.VMEM((cells // LOW * tracers, 2 * LOW), jnp.bfloat16)],
        compiler_params=pltpu.CompilerParams(vmem_limit_bytes=VMEM_LIMIT),
        cost_estimate=pl.CostEstimate(flops=4 * 10**9, bytes_accessed=10**6, transcendentals=0),
        name="pack",
    )(surface, rows, cols)


def remap_kernel(grid_rows, near, slot, weight, level0, coupling, mask, *rest):
    pieces, out, table = rest[:-2], rest[-2], rest[-1]
    tracers, capacity = pieces[0].shape
    width = level0.shape[2]
    for index, piece in enumerate(pieces):
        put_table(table, piece, index * (capacity // LOW), capacity // LOW)
    block = 512
    for place, row in enumerate(grid_rows):

        def body(step, carry, place=place, row=row):
            at = pl.ds(pl.multiple_of(step * block, block), block)
            total = jnp.zeros((tracers, block), jnp.float32)
            for k in range(near.shape[0]):
                entry = near[k, row : row + 1, at] * capacity + slot[k, row : row + 1, at]
                total = total + weight[k, row : row + 1, at] * looked_up(table, entry, tracers)
            own = level0[:, row, at]
            wet = mask[row : row + 1, at].astype(jnp.float32)
            out[:, place, at] = own + coupling[:, row, at] * wet * (total - own)
            return carry

        lax.fori_loop(0, width // block, body, 0)


def remap(grid_rows, pieces, near, slot, weight, level0, coupling, mask):
    tracers, capacity = pieces[0].shape
    return pl.pallas_call(
        functools.partial(remap_kernel, grid_rows),
        out_shape=jax.ShapeDtypeStruct((tracers, len(grid_rows), level0.shape[2]), jnp.float32),
        scratch_shapes=[pltpu.VMEM((len(pieces) * capacity // LOW * tracers, 2 * LOW), jnp.bfloat16)],
        compiler_params=pltpu.CompilerParams(vmem_limit_bytes=VMEM_LIMIT),
        cost_estimate=pl.CostEstimate(flops=15 * 10**9, bytes_accessed=10**6, transcendentals=0),
        name="remap",
    )(near, slot, weight, level0, coupling, mask, *pieces)


def substep(field, speed_x, speed_y):
    east = jnp.roll(field, -1, axis=0)
    west = jnp.roll(field, 1, axis=0)
    north = jnp.roll(field, -1, axis=1)
    south = jnp.roll(field, 1, axis=1)
    return (
        field
        - 0.5 * speed_x * (east - west)
        - 0.5 * speed_y * (north - south)
        + diffusion * (east + west + north + south - 4.0 * field)
    )


def upper_kernel(field, before, after, velocity, out):
    level = pl.program_id(0)
    tracers = field.shape[0]
    levels = velocity.shape[1]
    padded = []
    for which in range(2):
        at = 3 * tracers + which * levels + 1 + level
        padded.append(jnp.concatenate([before[at], velocity[which, 1 + level], after[at]], axis=0))

    def body(tracer, carry):
        at = 3 * tracer + level
        value = jnp.concatenate([before[at], field[tracer, 0], after[at]], axis=0)
        for _ in range(2):
            value = substep(value, *padded)
        out[tracer, 0] = value[2:6]
        return carry

    lax.fori_loop(0, tracers, body, 0)


def surface_kernel(velocity, before_v, after_v, first, last, before, after, whole, out):
    del whole
    tracers = first.shape[0]
    levels = velocity.shape[1]
    padded = []
    for which in range(2):
        at = 3 * tracers + which * levels
        padded.append(jnp.concatenate([before_v[at], velocity[which, 0], after_v[at]], axis=0))

    def body(tracer, carry):
        value = jnp.concatenate([before[tracer], first[tracer], last[tracer], after[tracer]], axis=0)
        for _ in range(2):
            value = substep(value, *padded)
        out[tracer, 0] = value[2:6]
        return carry

    lax.fori_loop(0, tracers, body, 0)


def whole_spec(shape):
    return pl.BlockSpec(shape, lambda *_: (0,) * len(shape))


def upper_levels(field, before, after, velocity):
    tracers, levels, rows, width = field.shape
    block = (tracers, 1, rows, width)
    return pl.pallas_call(
        upper_kernel,
        grid=(levels - 1,),
        out_shape=jax.ShapeDtypeStruct(field.shape, jnp.float32),
        in_specs=[
            pl.BlockSpec(block, lambda level: (0, level + 1, 0, 0)),
            whole_spec(before.shape),
            whole_spec(after.shape),
            whole_spec(velocity.shape),
        ],
        out_specs=pl.BlockSpec(block, lambda level: (0, level + 1, 0, 0)),
        compiler_params=pltpu.CompilerParams(vmem_limit_bytes=VMEM_LIMIT),
        cost_estimate=pl.CostEstimate(flops=10**9, bytes_accessed=3 * 10**6, transcendentals=0),
        name="upper_levels",
    )(field, before, after, velocity)


def surface_level(velocity, before_v, after_v, first, last, before, after, whole):
    tracers, _, rows, width = whole.shape
    values = (velocity, before_v, after_v, first, last, before, after)
    return pl.pallas_call(
        surface_kernel,
        grid=(1,),
        out_shape=jax.ShapeDtypeStruct(whole.shape, jnp.float32),
        in_specs=[whole_spec(v.shape) for v in values] + [pl.BlockSpec(memory_space=pl.ANY)],
        out_specs=pl.BlockSpec((tracers, 1, rows, width), lambda _: (0, 0, 0, 0)),
        input_output_aliases={len(values): 0},
        compiler_params=pltpu.CompilerParams(vmem_limit_bytes=VMEM_LIMIT),
        name="surface_level",
    )(*values, whole)


def per_device(
    tracer,
    velocity,
    coupling,
    sea_mask,
    send_rows,
    send_cols,
    intersection_near,
    intersection_slot,
    intersection_weight,
):
    field = tracer[0]
    speed = velocity[0]
    tracers, levels, rows, width = field.shape
    level0 = field[:, 0]
    packed = pack(level0.reshape(tracers, rows * width), send_rows[0, 0], send_cols[0, 0])
    pieces = [moved(packed[near], 1 - near, True) for near in range(len(packed))]

    def edge(start):
        upper = lax.slice_in_dim(field[:, 1:], start, start + 2, axis=2)
        moving = lax.slice_in_dim(speed, start, start + 2, axis=2)
        return jnp.concatenate(
            [upper.reshape(tracers * (levels - 1), 2, width), moving.reshape(2 * levels, 2, width)], axis=0
        )

    before_v = moved(edge(rows - 2), 1, False)
    after_v = moved(edge(0), -1, False)

    shared = (
        intersection_near[0],
        intersection_slot[0],
        intersection_weight[0],
        level0,
        coupling[0],
        sea_mask[0],
    )
    first = remap((0, 1), pieces, *shared)
    after = moved(first, -1, False)
    last = remap((2, 3), pieces, *shared)
    before = moved(last, 1, False)
    whole = upper_levels(field, before_v, after_v, speed)
    return surface_level(speed, before_v, after_v, first, last, before, after, whole)[None]


def solution(mesh):
    in_specs = (
        P("comp", None, None, "tile", None),
        P("comp", None, None, "tile", None),
        P("comp", None, "tile", None),
        P("comp", "tile", None),
        P("comp", "tile", None, None),
        P("comp", "tile", None, None),
        P("comp", None, "tile", None),
        P("comp", None, "tile", None),
        P("comp", None, "tile", None),
    )
    out_specs = P("comp", None, None, "tile", None)
    return jax.shard_map(
        per_device, mesh=mesh, in_specs=in_specs, out_specs=out_specs, check_vma=False
    )
```

time: 381 us -> 64.4 us (0.17)
  matrix products: 313 us -> 0 us
  Pallas kernels: 0 us -> 38.1 us
  waiting for transfers between devices: 18.3 us -> 0.33 us
  local copies, waits for them, and re-layouts: 11.4 us -> 2.21 us
  other arithmetic: 9.55 us -> 0.4 us
    dot_general x40 -> x0, matrix products: 313 us -> none  [the longest x32 300 us: remap_one_block(): jnp.dot(received[:, near], table, precision=lax.Precision.HIGHEST, prefer...]
    pallas_call x0 -> x5, Pallas kernels: none -> 38.1 us  [the longest x2 19.5 us: remap(): pl.pallas_call(functools.partial(remap_kernel, grid_rows), out_shape=jax....]
    ppermute x9 -> x8, waiting for transfers between devices: 18.3 us -> 0.33 us  [moved(): return lax.ppermute(value, ('comp', 'tile'), pairs)]
    slice x31 -> x3, local copies, waits for them, and re-layouts: 6.56 us -> 1.42 us  [the longest x1 1.07 us: per_device(): level0 = field[:, 0]]
    ppermute x9 -> x8, starting transfers between devices: 26.2 us -> 22.9 us  [moved(): return lax.ppermute(value, ('comp', 'tile'), pairs)]
  transfers between devices with their start and end apart: 9 -> 8, of which waited for: 5 -> 1; matrix products, arithmetic and copies ran while one was open for 1% -> 1% of each run, Pallas kernels for 0% -> 46%
where the time goes in v1:
time: 64.4 us; the launch traced here: 64.2 us
  Pallas kernels  38.1 us (59%)
  starting transfers between devices  22.9 us (36%)
  local copies, waits for them, and re-layouts  2.21 us (3%)
    ppermute x8, starting transfers between devices, moved(): return lax.ppermute(value, ('comp', 'tile'), pairs)  22.9 us
    pallas_call x2, Pallas kernels, remap(): pl.pallas_call(functools.partial(remap_kernel, grid_rows), out_shape=jax....  19.5 us
    pallas_call x1, Pallas kernels, upper_levels(): pl.pallas_call(upper_kernel, grid=(levels - 1,), out_shape=jax.ShapeDtype...  9.85 us
    pallas_call x1, Pallas kernels, pack(): pl.pallas_call(pack_kernel, out_shape=[jax.ShapeDtypeStruct((tracers, cap...  5 us
    pallas_call x1, Pallas kernels, surface_level(): pl.pallas_call(surface_kernel, grid=(1,), out_shape=jax.ShapeDtypeStruct(...  3.75 us
  transfers between devices with their start and end apart: 8, of which 1 were waited for; matrix products, arithmetic and copies ran while one was open for 1% of the time, Pallas kernels for 46%

profile of v1, /device:TPU:1, one launch (start us, length us, event | category | flops | bytes accessed | tf_op | source)
XLA Modules:
  0.0 64.2 jit_solution(3011877100813113263)
XLA Ops:
  0.0 1.1 %fusion = (f32[16,1,4,1024]{3,2,1,0:T(4,128)S(1)}, f32[16,4,1024]{2,1,0:T(4,128)S(1)}) fusion(f32[16,4,4,1024]{3,2,1,0:T(4,128)} %bitcast.19), kind=kLoop, calls=%fused_computation.3 | loop fusion | bytes 786432 | tf_op jit(solution)/shard_map/slice | solution.py:234
  1.1 0.0 copy-start.6
  1.1 0.0 copy-start.7
  1.1 0.2 copy.11
  1.3 0.6 copy-done.6
  1.8 0.0 copy-done.7
  1.9 0.0 copy-start
  1.9 5.0 %pack.1 = (f32[16,2048]{1,0:T(8,128)S(1)}, f32[16,2048]{1,0:T(8,128)S(1)}, f32[16,2048]{1,0:T(8,128)S(1)}, f32[16,2048]{1,0:T(8,128)S(1)}) custom-call(f32[16,4096]{1,0:T(8,128)S(1)} %bitcast.25, s32[4,2048]{1,0:T(4,128)S(1)} %bitcast.34, s32[4,2048]{1,0:T(4,128)S(1)} %bitcast.35), custom_call_target="tpu_custom_call" | custom-call | flops 4000000000 | bytes 1000000 | tf_op jit(solution)/shard_map/pack/pallas_call | solution.py:84
  6.9 3.1 %collective-permute-start.2 = (f32[16,2048]{1,0:T(8,128)S(1)}, f32[16,2048]{1,0:T(8,128)S(1)}, u32[]{:S(2)}, u32[]{:S(2)}) collective-permute-start(f32[16,2048]{1,0:T(8,128)S(1)} %get-tuple-element.9), channel_id=1, source_target_pairs={{0,65},{1,66},{2,67},{3,68},{4,69},{5,70},{6,71},{7,72},{8,73},{9,... | collective-permute-start | bytes 393224 | tf_op jit(solution)/shard_map/ppermute | solution.py:22
  10.0 0.0 collective-permute-start.3
  10.0 6.9 %collective-permute-start.4 = (f32[16,2048]{1,0:T(8,128)S(1)}, f32[16,2048]{1,0:T(8,128)S(1)}, u32[]{:S(2)}, u32[]{:S(2)}) collective-permute-start(f32[16,2048]{1,0:T(8,128)S(1)} %get-tuple-element.11), channel_id=1, source_target_pairs={{0,127},{1,64},{2,65},{3,66},{4,67},{5,68},{6,69},{7,70},{8,71},{9... | collective-permute-start | bytes 393224 | tf_op jit(solution)/shard_map/ppermute | solution.py:22
  16.9 0.0 copy-start.1
  16.9 1.4 %collective-permute-start.5 = (f32[16,2048]{1,0:T(8,128)S(1)}, f32[16,2048]{1,0:T(8,128)S(1)}, u32[]{:S(2)}, u32[]{:S(2)}) collective-permute-start(f32[16,2048]{1,0:T(8,128)S(1)} %get-tuple-element.12), channel_id=1, source_target_pairs={{0,126},{1,127},{2,64},{3,65},{4,66},{5,67},{6,68},{7,69},{8,70},{... | collective-permute-start | bytes 393224 | tf_op jit(solution)/shard_map/ppermute | solution.py:22
  18.3 0.0 copy-done
  18.3 0.3 fusion.1
  18.6 0.0 copy-done.1
  18.7 0.1 fusion.2
  18.7 0.2 pad_maximum_fusion
  18.9 0.8 %collective-permute-start = (f32[56,2,1024]{2,1,0:T(2,128)S(1)}, f32[56,2,1024]{2,1,0:T(2,128)S(1)}, u32[]{:S(2)}, u32[]{:S(2)}) collective-permute-start(f32[56,2,1024]{2,1,0:T(2,128)S(1)} %pad_maximum_fusion), channel_id=1, source_target_pairs={{0,1},{1,2},{2,3},{3,4},{4,5},{5,6},{6,7},{7,8},{8,9},{9,10},{10,1... | collective-permute-start | bytes 1376264 | tf_op jit(solution)/shard_map/ppermute | solution.py:22
  19.7 0.0 copy-start.2
  19.7 0.0 copy-start.3
  19.7 0.0 copy-start.4
  19.7 0.0 copy-start.5
  19.7 0.0 copy-start.8
  19.7 0.2 pad_maximum_fusion.1
  19.9 0.0 collective-permute-done.2.rest_0_
  20.0 6.2 %collective-permute-start.1 = (f32[56,2,1024]{2,1,0:T(2,128)S(1)}, f32[56,2,1024]{2,1,0:T(2,128)S(1)}, u32[]{:S(2)}, u32[]{:S(2)}) collective-permute-start(f32[56,2,1024]{2,1,0:T(2,128)S(1)} %pad_maximum_fusion.1), channel_id=1, source_target_pairs={{0,63},{1,0},{2,1},{3,2},{4,3},{5,4},{6,5},{7,6},{8,7},{9,8},{10,9... | collective-permute-start | bytes 1376264 | tf_op jit(solution)/shard_map/ppermute | solution.py:22
  26.2 0.0 collective-permute-done.3.rest_1_
  26.2 0.0 collective-permute-done.4.rest_2_
  26.2 0.0 collective-permute-done.5.rest_3_
  26.2 0.0 copy-done.2
  26.2 0.0 copy-done.3
  26.2 0.0 copy-done.4
  26.2 0.0 copy-done.5
  26.3 0.0 copy-done.8
  26.3 9.8 %remap.2.first = f32[16,2,1024]{2,1,0:T(2,128)S(1)} custom-call(s32[8,4,1024]{2,1,0:T(4,128)S(1)} %bitcast.28, s32[8,4,1024]{2,1,0:T(4,128)S(1)} %bitcast.30, f32[8,4,1024]{2,1,0:T(4,128)S(1)} %bitcast.32, f32[16,4,1024]{2,1,0:T(4,128)S(1)} %get-tuple-element.14.level0, f32[16,4,1024]{2,1,0:T(4,128)S(1)} %bitcast.26, s32[4,1024]{1,0:T(4,128)S(1)} %bitcast.36, ...), custom_call_target="tpu_custom_call" | custom-call | flops 15000000512 | bytes 1000000 | tf_op jit(solution)/shard_map/remap/pallas_call | solution.py:119
  36.0 4.4 %collective-permute-start.7 = (f32[16,2,1024]{2,1,0:T(2,128)S(1)}, f32[16,2,1024]{2,1,0:T(2,128)S(1)}, u32[]{:S(2)}, u32[]{:S(2)}) collective-permute-start(f32[16,2,1024]{2,1,0:T(2,128)S(1)} %remap.2.first), channel_id=1, source_target_pairs={{0,63},{1,0},{2,1},{3,2},{4,3},{5,4},{6,5},{7,6},{8,7},{9,8},{10,9... | collective-permute-start | bytes 393224 | tf_op jit(solution)/shard_map/ppermute | solution.py:22
  40.4 9.8 %remap.3.last = f32[16,2,1024]{2,1,0:T(2,128)S(1)} custom-call(s32[8,4,1024]{2,1,0:T(4,128)S(1)} %bitcast.29, s32[8,4,1024]{2,1,0:T(4,128)S(1)} %bitcast.31, f32[8,4,1024]{2,1,0:T(4,128)S(1)} %bitcast.33, f32[16,4,1024]{2,1,0:T(4,128)S(1)} %get-tuple-element.14.level0, f32[16,4,1024]{2,1,0:T(4,128)S(1)} %bitcast.27, s32[4,1024]{1,0:T(4,128)S(1)} %bitcast.37, ...), custom_call_target="tpu_custom_call" | custom-call | flops 15000000512 | bytes 1000000 | tf_op jit(solution)/shard_map/remap/pallas_call | solution.py:119
  50.2 0.1 collective-permute-start.6
  50.2 0.0 collective-permute-done.before.before_v
  50.3 0.0 collective-permute-done.1.after.after_v
  50.3 9.8 %upper_levels.1.whole = f32[16,4,4,1024]{3,2,1,0:T(4,128)} custom-call(f32[16,4,4,1024]{3,2,1,0:T(4,128)S(1)} %bitcast.21, f32[56,2,1024]{2,1,0:T(2,128)S(1)} %collective-permute-done.before.before_v, f32[56,2,1024]{2,1,0:T(2,128)S(1)} %collective-permute-done.1.after.after_v, f32[2,4,4,1024]{3,2,1,0:T(4,128)S(1)} %bitcast.23), custom_call_target="tpu_custom_call" | custom-call | flops 1000000000 | bytes 3000000 | tf_op jit(solution)/shard_map/upper_levels/pallas_call | solution.py:188
  60.1 0.0 collective-permute-done.7.after
  60.1 0.3 collective-permute-done.6.before
  60.4 3.7 %surface_level.1 = f32[16,4,4,1024]{3,2,1,0:T(4,128)} custom-call(f32[2,4,4,1024]{3,2,1,0:T(4,128)S(1)} %bitcast.24, f32[56,2,1024]{2,1,0:T(2,128)S(1)} %collective-permute-done.before.before_v, f32[56,2,1024]{2,1,0:T(2,128)S(1)} %collective-permute-done.1.after.after_v, f32[16,2,1024]{2,1,0:T(2,128)S(1)} %remap.2.first, ...), custom_call_target="tpu_custom_call", output_to_operand_aliasing={{}: (7, {})} | custom-call | tf_op jit(solution)/shard_map/surface_level/pallas_call | solution.py:208
Async XLA Ops:
  1.1 0.8 %copy-start.6 = (s32[1,1,4,2048]{3,2,1,0:T(4,128)S(1)}, s32[1,1,4,2048]{3,2,1,0:T(4,128)}, u32[]{:S(2)}) copy-start(s32[1,1,4,2048]{3,2,1,0:T(4,128)} %param.13) | copy-start | bytes 98308
  1.1 0.8 %copy-start.7 = (s32[1,1,4,2048]{3,2,1,0:T(4,128)S(1)}, s32[1,1,4,2048]{3,2,1,0:T(4,128)}, u32[]{:S(2)}) copy-start(s32[1,1,4,2048]{3,2,1,0:T(4,128)} %param.14) | copy-start | bytes 98308
  1.9 16.5 %copy-start = (f32[1,16,4,4,1024]{4,3,2,1,0:T(4,128)S(1)}, f32[1,16,4,4,1024]{4,3,2,1,0:T(4,128)}, u32[]{:S(2)}) copy-start(f32[1,16,4,4,1024]{4,3,2,1,0:T(4,128)} %param.9) | copy-start | bytes 3145732
  6.9 13.1 %collective-permute-start.2 = (f32[16,2048]{1,0:T(8,128)S(1)}, f32[16,2048]{1,0:T(8,128)S(1)}, u32[]{:S(2)}, u32[]{:S(2)}) collective-permute-start(f32[16,2048]{1,0:T(8,128)S(1)} %get-tuple-element.9), channel_id=1, source_target_pairs={{0,65},{1,66},{2,67},{3,68},{4,69},{5,70},{6,71},{7,72},{8,73},{9,... | collective-permute-start | bytes 393224 | tf_op jit(solution)/shard_map/ppermute | solution.py:22
  10.0 16.2 %collective-permute-start.3 = (f32[16,2048]{1,0:T(8,128)S(1)}, f32[16,2048]{1,0:T(8,128)S(1)}, u32[]{:S(2)}, u32[]{:S(2)}) collective-permute-start(f32[16,2048]{1,0:T(8,128)S(1)} %get-tuple-element.10), channel_id=1, source_target_pairs={{0,64},{1,65},{2,66},{3,67},{4,68},{5,69},{6,70},{7,71},{8,72},{9,... | collective-permute-start | bytes 393224 | tf_op jit(solution)/shard_map/ppermute | solution.py:22
  10.0 16.2 %collective-permute-start.4 = (f32[16,2048]{1,0:T(8,128)S(1)}, f32[16,2048]{1,0:T(8,128)S(1)}, u32[]{:S(2)}, u32[]{:S(2)}) collective-permute-start(f32[16,2048]{1,0:T(8,128)S(1)} %get-tuple-element.11), channel_id=1, source_target_pairs={{0,127},{1,64},{2,65},{3,66},{4,67},{5,68},{6,69},{7,70},{8,71},{9... | collective-permute-start | bytes 393224 | tf_op jit(solution)/shard_map/ppermute | solution.py:22
  16.9 1.7 %copy-start.1 = (f32[1,2,4,4,1024]{4,3,2,1,0:T(4,128)S(1)}, f32[1,2,4,4,1024]{4,3,2,1,0:T(4,128)}, u32[]{:S(2)}) copy-start(f32[1,2,4,4,1024]{4,3,2,1,0:T(4,128)} %param.10) | copy-start | bytes 393220
  16.9 9.3 %collective-permute-start.5 = (f32[16,2048]{1,0:T(8,128)S(1)}, f32[16,2048]{1,0:T(8,128)S(1)}, u32[]{:S(2)}, u32[]{:S(2)}) collective-permute-start(f32[16,2048]{1,0:T(8,128)S(1)} %get-tuple-element.12), channel_id=1, source_target_pairs={{0,126},{1,127},{2,64},{3,65},{4,66},{5,67},{6,68},{7,69},{8,70},{... | collective-permute-start | bytes 393224 | tf_op jit(solution)/shard_map/ppermute | solution.py:22
  18.9 31.3 %collective-permute-start = (f32[56,2,1024]{2,1,0:T(2,128)S(1)}, f32[56,2,1024]{2,1,0:T(2,128)S(1)}, u32[]{:S(2)}, u32[]{:S(2)}) collective-permute-start(f32[56,2,1024]{2,1,0:T(2,128)S(1)} %pad_maximum_fusion), channel_id=1, source_target_pairs={{0,1},{1,2},{2,3},{3,4},{4,5},{5,6},{6,7},{7,8},{8,9},{9,10},{10,1... | collective-permute-start | bytes 1376264 | tf_op jit(solution)/shard_map/ppermute | solution.py:22
  19.7 6.5 %copy-start.2 = (f32[1,16,4,1024]{3,2,1,0:T(4,128)S(1)}, f32[1,16,4,1024]{3,2,1,0:T(4,128)}, u32[]{:S(2)}) copy-start(f32[1,16,4,1024]{3,2,1,0:T(4,128)} %param.11) | copy-start | bytes 786436
  19.7 6.5 %copy-start.3 = (s32[1,8,4,1024]{3,2,1,0:T(4,128)S(1)}, s32[1,8,4,1024]{3,2,1,0:T(4,128)}, u32[]{:S(2)}) copy-start(s32[1,8,4,1024]{3,2,1,0:T(4,128)} %param.15) | copy-start | bytes 393220
  19.7 6.5 %copy-start.4 = (s32[1,8,4,1024]{3,2,1,0:T(4,128)S(1)}, s32[1,8,4,1024]{3,2,1,0:T(4,128)}, u32[]{:S(2)}) copy-start(s32[1,8,4,1024]{3,2,1,0:T(4,128)} %param.16) | copy-start | bytes 393220
  19.7 6.5 %copy-start.5 = (f32[1,8,4,1024]{3,2,1,0:T(4,128)S(1)}, f32[1,8,4,1024]{3,2,1,0:T(4,128)}, u32[]{:S(2)}) copy-start(f32[1,8,4,1024]{3,2,1,0:T(4,128)} %param.17) | copy-start | bytes 393220
  19.7 6.5 %copy-start.8 = (s32[1,4,1024]{2,1,0:T(4,128)S(1)}, s32[1,4,1024]{2,1,0:T(4,128)}, u32[]{:S(2)}) copy-start(s32[1,4,1024]{2,1,0:T(4,128)} %param.12) | copy-start | bytes 49156
  20.0 30.3 %collective-permute-start.1 = (f32[56,2,1024]{2,1,0:T(2,128)S(1)}, f32[56,2,1024]{2,1,0:T(2,128)S(1)}, u32[]{:S(2)}, u32[]{:S(2)}) collective-permute-start(f32[56,2,1024]{2,1,0:T(2,128)S(1)} %pad_maximum_fusion.1), channel_id=1, source_target_pairs={{0,63},{1,0},{2,1},{3,2},{4,3},{5,4},{6,5},{7,6},{8,7},{9,8},{10,9... | collective-permute-start | bytes 1376264 | tf_op jit(solution)/shard_map/ppermute | solution.py:22
  36.0 24.1 %collective-permute-start.7 = (f32[16,2,1024]{2,1,0:T(2,128)S(1)}, f32[16,2,1024]{2,1,0:T(2,128)S(1)}, u32[]{:S(2)}, u32[]{:S(2)}) collective-permute-start(f32[16,2,1024]{2,1,0:T(2,128)S(1)} %remap.2.first), channel_id=1, source_target_pairs={{0,63},{1,0},{2,1},{3,2},{4,3},{5,4},{6,5},{7,6},{8,7},{9,8},{10,9... | collective-permute-start | bytes 393224 | tf_op jit(solution)/shard_map/ppermute | solution.py:22
  50.2 10.3 %collective-permute-start.6 = (f32[16,2,1024]{2,1,0:T(2,128)S(1)}, f32[16,2,1024]{2,1,0:T(2,128)S(1)}, u32[]{:S(2)}, u32[]{:S(2)}) collective-permute-start(f32[16,2,1024]{2,1,0:T(2,128)S(1)} %remap.3.last), channel_id=1, source_target_pairs={{0,1},{1,2},{2,3},{3,4},{4,5},{5,6},{6,7},{7,8},{8,9},{9,10},{10,1... | collective-permute-start | bytes 393224 | tf_op jit(solution)/shard_map/ppermute | solution.py:22

commit v2 on v1

--- a/solution.py
+++ b/solution.py
@@ -10,6 +10,8 @@
 diffusion = 0.12
 LOW = 128
 VMEM_LIMIT = 48 * 2**20
+PACK_ORDER = (3, 0, 2, 1)
+UNROLL = 4
 
 
 def moved(value, steps, swap):
@@ -22,10 +24,9 @@
     return lax.ppermute(value, ("comp", "tile"), pairs)
 
 
-def put_table(table, source, first, count):
-    tracers = source.shape[0]
+def put_table(table, tracers, first, count, part):
     for high in range(count):
-        value = source[:, high * LOW : (high + 1) * LOW]
+        value = part(high)
         leading = value.astype(jnp.bfloat16)
         rest = (value - leading.astype(jnp.float32)).astype(jnp.bfloat16)
         row = (first + high) * tracers
@@ -59,44 +60,58 @@
     return chosen([product[tracers * h : tracers * (h + 1)] for h in range(highs)], high)
 
 
-def pack_kernel(surface, rows, cols, *rest):
+def pack_kernel(field, rows, cols, *rest):
     outs, table = rest[:-1], rest[-1]
-    tracers, cells = surface.shape
-    capacity = rows.shape[1]
-    width = cells // 4
-    put_table(table, surface, 0, cells // LOW)
+    tracers, _, grid_rows, width = field.shape
+    per_row = width // LOW
+
+    def part(high):
+        low = high % per_row * LOW
+        return field[:, 0, high // per_row, low : low + LOW]
+
+    put_table(table, tracers, 0, grid_rows * per_row, part)
     block = 512
-
-    for near, out in enumerate(outs):
-
-        def body(step, carry, near=near, out=out):
-            at = pl.ds(pl.multiple_of(step * block, block), block)
+    for near in PACK_ORDER:
+        for start in range(0, rows.shape[1], block):
+            at = slice(start, start + block)
             entry = rows[near : near + 1, at] * width + cols[near : near + 1, at]
-            out[:, at] = looked_up(table, entry, tracers)
-            return carry
-
-        lax.fori_loop(0, capacity // block, body, 0)
-
-
-def pack(surface, rows, cols):
-    tracers, cells = surface.shape
+            outs[near][:, at] = looked_up(table, entry, tracers)
+
+
+def level_spec(field):
+    tracers, _, rows, width = field.shape
+    return pl.BlockSpec((tracers, 1, rows, width), lambda *_: (0, 0, 0, 0))
+
+
+def pack(field, rows, cols):
+    tracers, _, grid_rows, width = field.shape
     neighbours, capacity = rows.shape
+    piece = (tracers, capacity)
     return pl.pallas_call(
         pack_kernel,
-        out_shape=[jax.ShapeDtypeStruct((tracers, capacity), jnp.float32)] * neighbours,
-        scratch_shapes=[pltpu.VMEM((cells // LOW * tracers, 2 * LOW), jnp.bfloat16)],
+        grid=(1,),
+        in_specs=[level_spec(field), whole_spec(rows.shape), whole_spec(cols.shape)],
+        out_specs=[whole_spec(piece)] * neighbours,
+        out_shape=[jax.ShapeDtypeStruct(piece, jnp.float32)] * neighbours,
+        scratch_shapes=[pltpu.VMEM((grid_rows * width // LOW * tracers, 2 * LOW), jnp.bfloat16)],
         compiler_params=pltpu.CompilerParams(vmem_limit_bytes=VMEM_LIMIT),
         cost_estimate=pl.CostEstimate(flops=4 * 10**9, bytes_accessed=10**6, transcendentals=0),
         name="pack",
-    )(surface, rows, cols)
-
-
-def remap_kernel(grid_rows, near, slot, weight, level0, coupling, mask, *rest):
+    )(field, rows, cols)
+
+
+def remap_kernel(grid_rows, near, slot, weight, field, coupling, mask, *rest):
     pieces, out, table = rest[:-2], rest[-2], rest[-1]
     tracers, capacity = pieces[0].shape
-    width = level0.shape[2]
+    width = field.shape[3]
     for index, piece in enumerate(pieces):
-        put_table(table, piece, index * (capacity // LOW), capacity // LOW)
+        put_table(
+            table,
+            tracers,
+            index * (capacity // LOW),
+            capacity // LOW,
+            lambda high, piece=piece: piece[:, high * LOW : (high + 1) * LOW],
+        )
     block = 512
     for place, row in enumerate(grid_rows):
 
@@ -106,7 +121,7 @@
             for k in range(near.shape[0]):
                 entry = near[k, row : row + 1, at] * capacity + slot[k, row : row + 1, at]
                 total = total + weight[k, row : row + 1, at] * looked_up(table, entry, tracers)
-            own = level0[:, row, at]
+            own = field[:, 0, row, at]
             wet = mask[row : row + 1, at].astype(jnp.float32)
             out[:, place, at] = own + coupling[:, row, at] * wet * (total - own)
             return carry
@@ -114,68 +129,91 @@
         lax.fori_loop(0, width // block, body, 0)
 
 
-def remap(grid_rows, pieces, near, slot, weight, level0, coupling, mask):
+def remap(grid_rows, pieces, near, slot, weight, field, coupling, mask):
     tracers, capacity = pieces[0].shape
+    out = (tracers, len(grid_rows), field.shape[3])
+    specs = [whole_spec(v.shape) for v in (near, slot, weight, coupling, mask, *pieces)]
+    specs.insert(3, level_spec(field))
     return pl.pallas_call(
         functools.partial(remap_kernel, grid_rows),
-        out_shape=jax.ShapeDtypeStruct((tracers, len(grid_rows), level0.shape[2]), jnp.float32),
+        grid=(1,),
+        in_specs=specs,
+        out_specs=whole_spec(out),
+        out_shape=jax.ShapeDtypeStruct(out, jnp.float32),
         scratch_shapes=[pltpu.VMEM((len(pieces) * capacity // LOW * tracers, 2 * LOW), jnp.bfloat16)],
         compiler_params=pltpu.CompilerParams(vmem_limit_bytes=VMEM_LIMIT),
         cost_estimate=pl.CostEstimate(flops=15 * 10**9, bytes_accessed=10**6, transcendentals=0),
         name="remap",
-    )(near, slot, weight, level0, coupling, mask, *pieces)
-
-
-def substep(field, speed_x, speed_y):
-    east = jnp.roll(field, -1, axis=0)
-    west = jnp.roll(field, 1, axis=0)
-    north = jnp.roll(field, -1, axis=1)
-    south = jnp.roll(field, 1, axis=1)
+    )(near, slot, weight, field, coupling, mask, *pieces)
+
+
+def set_factors(factors, speed_x, speed_y):
+    factors[0] = diffusion - 0.5 * speed_x
+    factors[1] = diffusion + 0.5 * speed_x
+    factors[2] = diffusion - 0.5 * speed_y
+    factors[3] = diffusion + 0.5 * speed_y
+
+
+def substep(field, factors):
+    rows, width = field.shape
+    east = pltpu.roll(field, rows - 1, axis=0)
+    west = pltpu.roll(field, 1, axis=0)
+    north = pltpu.roll(field, width - 1, axis=1)
+    south = pltpu.roll(field, 1, axis=1)
     return (
-        field
-        - 0.5 * speed_x * (east - west)
-        - 0.5 * speed_y * (north - south)
-        + diffusion * (east + west + north + south - 4.0 * field)
+        (1 - 4 * diffusion) * field
+        + (factors[0] * east + factors[1] * west)
+        + (factors[2] * north + factors[3] * south)
     )
 
 
-def upper_kernel(field, before, after, velocity, out):
+def transported(tracers, factors, padded, store):
+    def body(step, carry):
+        for offset in range(UNROLL):
+            tracer = step * UNROLL + offset
+            store(tracer, substep(substep(padded(tracer), factors), factors)[:4])
+        return carry
+
+    lax.fori_loop(0, tracers // UNROLL, body, 0)
+
+
+def upper_kernel(field, before, after, velocity, out, factors):
     level = pl.program_id(0)
     tracers = field.shape[0]
     levels = velocity.shape[1]
-    padded = []
+    speeds = []
     for which in range(2):
         at = 3 * tracers + which * levels + 1 + level
-        padded.append(jnp.concatenate([before[at], velocity[which, 1 + level], after[at]], axis=0))
-
-    def body(tracer, carry):
+        speeds.append(jnp.concatenate([velocity[which, 1 + level], after[at], before[at]], axis=0))
+    set_factors(factors, *speeds)
+
+    def padded(tracer):
         at = 3 * tracer + level
-        value = jnp.concatenate([before[at], field[tracer, 0], after[at]], axis=0)
-        for _ in range(2):
-            value = substep(value, *padded)
-        out[tracer, 0] = value[2:6]
-        return carry
-
-    lax.fori_loop(0, tracers, body, 0)
-
-
-def surface_kernel(velocity, before_v, after_v, first, last, before, after, whole, out):
+        return jnp.concatenate([field[tracer, 0], after[at], before[at]], axis=0)
+
+    def store(tracer, value):
+        out[tracer, 0] = value
+
+    transported(tracers, factors, padded, store)
+
+
+def surface_kernel(velocity, before_v, after_v, first, last, before, after, whole, out, factors):
     del whole
     tracers = first.shape[0]
     levels = velocity.shape[1]
-    padded = []
+    speeds = []
     for which in range(2):
         at = 3 * tracers + which * levels
-        padded.append(jnp.concatenate([before_v[at], velocity[which, 0], after_v[at]], axis=0))
-
-    def body(tracer, carry):
-        value = jnp.concatenate([before[tracer], first[tracer], last[tracer], after[tracer]], axis=0)
-        for _ in range(2):
-            value = substep(value, *padded)
-        out[tracer, 0] = value[2:6]
-        return carry
-
-    lax.fori_loop(0, tracers, body, 0)
+        speeds.append(jnp.concatenate([velocity[which, 0], after_v[at], before_v[at]], axis=0))
+    set_factors(factors, *speeds)
+
+    def padded(tracer):
+        return jnp.concatenate([first[tracer], last[tracer], after[tracer], before[tracer]], axis=0)
+
+    def store(tracer, value):
+        out[tracer, 0] = value
+
+    transported(tracers, factors, padded, store)
 
 
 def whole_spec(shape):
@@ -196,6 +234,7 @@
             whole_spec(velocity.shape),
         ],
         out_specs=pl.BlockSpec(block, lambda level: (0, level + 1, 0, 0)),
+        scratch_shapes=[pltpu.VMEM((4, 8, width), jnp.float32)],
         compiler_params=pltpu.CompilerParams(vmem_limit_bytes=VMEM_LIMIT),
         cost_estimate=pl.CostEstimate(flops=10**9, bytes_accessed=3 * 10**6, transcendentals=0),
         name="upper_levels",
@@ -212,6 +251,7 @@
         in_specs=[whole_spec(v.shape) for v in values] + [pl.BlockSpec(memory_space=pl.ANY)],
         out_specs=pl.BlockSpec((tracers, 1, rows, width), lambda _: (0, 0, 0, 0)),
         input_output_aliases={len(values): 0},
+        scratch_shapes=[pltpu.VMEM((4, 8, width), jnp.float32)],
         compiler_params=pltpu.CompilerParams(vmem_limit_bytes=VMEM_LIMIT),
         name="surface_level",
     )(*values, whole)
@@ -231,8 +271,7 @@
     field = tracer[0]
     speed = velocity[0]
     tracers, levels, rows, width = field.shape
-    level0 = field[:, 0]
-    packed = pack(level0.reshape(tracers, rows * width), send_rows[0, 0], send_cols[0, 0])
+    packed = pack(field, send_rows[0, 0], send_cols[0, 0])
     pieces = [moved(packed[near], 1 - near, True) for near in range(len(packed))]
 
     def edge(start):
@@ -249,7 +288,7 @@
         intersection_near[0],
         intersection_slot[0],
         intersection_weight[0],
-        level0,
+        field,
         coupling[0],
         sea_mask[0],
     )

time: 64.4 us -> 61.4 us (0.953)
  Pallas kernels: 38.1 us -> 28.7 us
  waiting for transfers between devices: 0.33 us -> 5.75 us
  local copies, waits for them, and re-layouts: 2.21 us -> 3.12 us
    ppermute x8, waiting for transfers between devices: 0.33 us -> 5.75 us  [moved(): return lax.ppermute(value, ('comp', 'tile'), pairs)]
    pallas_call x1, Pallas kernels: 9.85 us -> 4.42 us  [upper_levels(): pl.pallas_call(upper_kernel, grid=(levels - 1,), out_shape=jax.ShapeDtype...]
    pallas_call x3, Pallas kernels: 24.5 us -> 22.5 us  [the longest x2 19.5 us: remap(): pl.pallas_call(functools.partial(remap_kernel, grid_rows), grid=(1,), in_...]
    unnamed x19 -> x18, local copies, waits for them, and re-layouts: 0.79 us -> 2.76 us
    pallas_call x1, Pallas kernels: 3.75 us -> 1.87 us  [surface_level(): pl.pallas_call(surface_kernel, grid=(1,), out_shape=jax.ShapeDtypeStruct(...]
    slice x1 -> x0, local copies, waits for them, and re-layouts: 1.07 us -> none  [per_device(): level0 = field[:, 0]]
  transfers between devices with their start and end apart: 8 -> 8, of which waited for: 1 -> 1; matrix products, arithmetic and copies ran while one was open for 1% -> 1% of each run, Pallas kernels for 46% -> 39%
where the time goes in v2:
time: 61.4 us; the launch traced here: 61.1 us
  Pallas kernels  28.7 us (47%)
  starting transfers between devices  23 us (37%)
  waiting for transfers between devices  5.75 us (9%)
  local copies, waits for them, and re-layouts  3.12 us (5%)
    ppermute x8, starting transfers between devices, moved(): return lax.ppermute(value, ('comp', 'tile'), pairs)  23 us
    pallas_call x2, Pallas kernels, remap(): pl.pallas_call(functools.partial(remap_kernel, grid_rows), grid=(1,), in_...  19.5 us
    ppermute x8, waiting for transfers between devices, moved(): return lax.ppermute(value, ('comp', 'tile'), pairs)  5.75 us
    pallas_call x1, Pallas kernels, upper_levels(): pl.pallas_call(upper_kernel, grid=(levels - 1,), out_shape=jax.ShapeDtype...  4.42 us
    pallas_call x1, Pallas kernels, pack(): pl.pallas_call(pack_kernel, grid=(1,), in_specs=[level_spec(field), whole...  2.91 us
    unnamed x18, local copies, waits for them, and re-layouts  2.76 us
    pallas_call x1, Pallas kernels, surface_level(): pl.pallas_call(surface_kernel, grid=(1,), out_shape=jax.ShapeDtypeStruct(...  1.87 us
  transfers between devices with their start and end apart: 8, of which 1 were waited for; matrix products, arithmetic and copies ran while one was open for 1% of the time, Pallas kernels for 39%

profile of v2, /device:TPU:1, one launch (start us, length us, event | category | flops | bytes accessed | tf_op | source)
XLA Modules:
  0.0 61.1 jit_solution(2157273958635669898)
XLA Ops:
  0.0 0.0 copy-start
  0.0 1.2 %copy-done = f32[1,16,4,4,1024]{4,3,2,1,0:T(4,128)S(1)} copy-done((f32[1,16,4,4,1024]{4,3,2,1,0:T(4,128)S(1)}, f32[1,16,4,4,1024]{4,3,2,1,0:T(4,128)}, u32[]{:S(2)}) %copy-start) | copy-done | bytes 1048600
  1.2 0.0 copy-start.6
  1.2 0.8 %copy-done.6 = s32[1,1,4,2048]{3,2,1,0:T(4,128)S(1)} copy-done((s32[1,1,4,2048]{3,2,1,0:T(4,128)S(1)}, s32[1,1,4,2048]{3,2,1,0:T(4,128)}, u32[]{:S(2)}) %copy-start.6) | copy-done | bytes 32792
  2.0 0.0 copy-start.7
  2.0 0.8 %copy-done.7 = s32[1,1,4,2048]{3,2,1,0:T(4,128)S(1)} copy-done((s32[1,1,4,2048]{3,2,1,0:T(4,128)S(1)}, s32[1,1,4,2048]{3,2,1,0:T(4,128)}, u32[]{:S(2)}) %copy-start.7) | copy-done | bytes 32792
  2.7 2.9 %pack.1 = (f32[16,2048]{1,0:T(8,128)S(1)}, f32[16,2048]{1,0:T(8,128)S(1)}, f32[16,2048]{1,0:T(8,128)S(1)}, f32[16,2048]{1,0:T(8,128)S(1)}) custom-call(f32[16,4,4,1024]{3,2,1,0:T(4,128)S(1)} %bitcast.14, s32[4,2048]{1,0:T(4,128)S(1)} %bitcast.30, s32[4,2048]{1,0:T(4,128)S(1)} %bitcast.31), custom_call_target="tpu_custom_call" | custom-call | flops 4000000000 | bytes 1000000 | tf_op jit(solution)/shard_map/pack/pallas_call | solution.py:90
  5.7 3.1 %collective-permute-start.2 = (f32[16,2048]{1,0:T(8,128)S(1)}, f32[16,2048]{1,0:T(8,128)S(1)}, u32[]{:S(2)}, u32[]{:S(2)}) collective-permute-start(f32[16,2048]{1,0:T(8,128)S(1)} %get-tuple-element.9), channel_id=1, source_target_pairs={{0,65},{1,66},{2,67},{3,68},{4,69},{5,70},{6,71},{7,72},{8,73},{9,... | collective-permute-start | bytes 393224 | tf_op jit(solution)/shard_map/ppermute | solution.py:24
  8.8 0.0 collective-permute-start.3
  8.8 6.9 %collective-permute-start.4 = (f32[16,2048]{1,0:T(8,128)S(1)}, f32[16,2048]{1,0:T(8,128)S(1)}, u32[]{:S(2)}, u32[]{:S(2)}) collective-permute-start(f32[16,2048]{1,0:T(8,128)S(1)} %get-tuple-element.11), channel_id=1, source_target_pairs={{0,127},{1,64},{2,65},{3,66},{4,67},{5,68},{6,69},{7,70},{8,71},{9... | collective-permute-start | bytes 393224 | tf_op jit(solution)/shard_map/ppermute | solution.py:24
  15.7 0.0 copy-start.1
  15.7 1.4 %collective-permute-start.5 = (f32[16,2048]{1,0:T(8,128)S(1)}, f32[16,2048]{1,0:T(8,128)S(1)}, u32[]{:S(2)}, u32[]{:S(2)}) collective-permute-start(f32[16,2048]{1,0:T(8,128)S(1)} %get-tuple-element.12), channel_id=1, source_target_pairs={{0,126},{1,127},{2,64},{3,65},{4,66},{5,67},{6,68},{7,69},{8,70},{... | collective-permute-start | bytes 393224 | tf_op jit(solution)/shard_map/ppermute | solution.py:24
  17.1 0.3 fusion
  17.4 0.0 copy-done.1
  17.4 0.1 fusion.1
  17.5 0.2 pad_maximum_fusion
  17.7 0.8 %collective-permute-start = (f32[56,2,1024]{2,1,0:T(2,128)S(1)}, f32[56,2,1024]{2,1,0:T(2,128)S(1)}, u32[]{:S(2)}, u32[]{:S(2)}) collective-permute-start(f32[56,2,1024]{2,1,0:T(2,128)S(1)} %pad_maximum_fusion), channel_id=1, source_target_pairs={{0,1},{1,2},{2,3},{3,4},{4,5},{5,6},{6,7},{7,8},{8,9},{9,10},{10,1... | collective-permute-start | bytes 1376264 | tf_op jit(solution)/shard_map/ppermute | solution.py:24
  18.5 0.0 copy-start.2
  18.5 0.0 copy-start.3
  18.5 0.0 copy-start.4
  18.5 0.0 copy-start.5
  18.5 0.0 copy-start.8
  18.5 0.2 pad_maximum_fusion.1
  18.7 0.0 collective-permute-done.2.rest_0_
  18.8 6.2 %collective-permute-start.1 = (f32[56,2,1024]{2,1,0:T(2,128)S(1)}, f32[56,2,1024]{2,1,0:T(2,128)S(1)}, u32[]{:S(2)}, u32[]{:S(2)}) collective-permute-start(f32[56,2,1024]{2,1,0:T(2,128)S(1)} %pad_maximum_fusion.1), channel_id=1, source_target_pairs={{0,63},{1,0},{2,1},{3,2},{4,3},{5,4},{6,5},{7,6},{8,7},{9,8},{10,9... | collective-permute-start | bytes 1376264 | tf_op jit(solution)/shard_map/ppermute | solution.py:24
  25.0 0.0 collective-permute-done.3.rest_1_
  25.0 0.0 collective-permute-done.4.rest_2_
  25.0 0.0 collective-permute-done.5.rest_3_
  25.0 0.0 copy-done.2
  25.0 0.0 copy-done.3
  25.0 0.0 copy-done.4
  25.0 0.0 copy-done.5
  25.0 0.0 copy-done.8
  25.0 9.8 %remap.2.first = f32[16,2,1024]{2,1,0:T(2,128)S(1)} custom-call(s32[8,4,1024]{2,1,0:T(4,128)S(1)} %bitcast.24, s32[8,4,1024]{2,1,0:T(4,128)S(1)} %bitcast.26, f32[8,4,1024]{2,1,0:T(4,128)S(1)} %bitcast.28, f32[16,4,4,1024]{3,2,1,0:T(4,128)S(1)} %bitcast.16, f32[16,4,1024]{2,1,0:T(4,128)S(1)} %bitcast.22, s32[4,1024]{1,0:T(4,128)S(1)} %bitcast.32, ...), custom_call_target="tpu_custom_call" | custom-call | flops 15000000512 | bytes 1000000 | tf_op jit(solution)/shard_map/remap/pallas_call | solution.py:137
  34.8 4.4 %collective-permute-start.7 = (f32[16,2,1024]{2,1,0:T(2,128)S(1)}, f32[16,2,1024]{2,1,0:T(2,128)S(1)}, u32[]{:S(2)}, u32[]{:S(2)}) collective-permute-start(f32[16,2,1024]{2,1,0:T(2,128)S(1)} %remap.2.first), channel_id=1, source_target_pairs={{0,63},{1,0},{2,1},{3,2},{4,3},{5,4},{6,5},{7,6},{8,7},{9,8},{10,9... | collective-permute-start | bytes 393224 | tf_op jit(solution)/shard_map/ppermute | solution.py:24
  39.2 9.8 %remap.3.last = f32[16,2,1024]{2,1,0:T(2,128)S(1)} custom-call(s32[8,4,1024]{2,1,0:T(4,128)S(1)} %bitcast.25, s32[8,4,1024]{2,1,0:T(4,128)S(1)} %bitcast.27, f32[8,4,1024]{2,1,0:T(4,128)S(1)} %bitcast.29, f32[16,4,4,1024]{3,2,1,0:T(4,128)S(1)} %bitcast.17, f32[16,4,1024]{2,1,0:T(4,128)S(1)} %bitcast.23, s32[4,1024]{1,0:T(4,128)S(1)} %bitcast.33, ...), custom_call_target="tpu_custom_call" | custom-call | flops 15000000512 | bytes 1000000 | tf_op jit(solution)/shard_map/remap/pallas_call | solution.py:137
  49.0 0.1 collective-permute-start.6
  49.1 0.0 collective-permute-done.before.before_v
  49.1 0.0 collective-permute-done.1.after.after_v
  49.1 4.4 %upper_levels.1.whole = f32[16,4,4,1024]{3,2,1,0:T(4,128)} custom-call(f32[16,4,4,1024]{3,2,1,0:T(4,128)S(1)} %bitcast.18, f32[56,2,1024]{2,1,0:T(2,128)S(1)} %collective-permute-done.before.before_v, f32[56,2,1024]{2,1,0:T(2,128)S(1)} %collective-permute-done.1.after.after_v, f32[2,4,4,1024]{3,2,1,0:T(4,128)S(1)} %bitcast.20), custom_call_target="tpu_custom_call" | custom-call | flops 1000000000 | bytes 3000000 | tf_op jit(solution)/shard_map/upper_levels/pallas_call | solution.py:226
  53.5 0.0 collective-permute-done.7.after
  53.5 5.7 %collective-permute-done.6.before = f32[16,2,1024]{2,1,0:T(2,128)S(1)} collective-permute-done((f32[16,2,1024]{2,1,0:T(2,128)S(1)}, f32[16,2,1024]{2,1,0:T(2,128)S(1)}, u32[]{:S(2)}, u32[]{:S(2)}) %collective-permute-start.6) | collective-permute-done | bytes 131104 | tf_op jit(solution)/shard_map/ppermute | solution.py:24
  59.3 1.9 %surface_level.1 = f32[16,4,4,1024]{3,2,1,0:T(4,128)} custom-call(f32[2,4,4,1024]{3,2,1,0:T(4,128)S(1)} %bitcast.21, f32[56,2,1024]{2,1,0:T(2,128)S(1)} %collective-permute-done.before.before_v, f32[56,2,1024]{2,1,0:T(2,128)S(1)} %collective-permute-done.1.after.after_v, f32[16,2,1024]{2,1,0:T(2,128)S(1)} %remap.2.first, ...), custom_call_target="tpu_custom_call", output_to_operand_aliasing={{}: (7, {})} | custom-call | tf_op jit(solution)/shard_map/surface_level/pallas_call | solution.py:247
Async XLA Ops:
  0.0 1.2 %copy-start = (f32[1,16,4,4,1024]{4,3,2,1,0:T(4,128)S(1)}, f32[1,16,4,4,1024]{4,3,2,1,0:T(4,128)}, u32[]{:S(2)}) copy-start(f32[1,16,4,4,1024]{4,3,2,1,0:T(4,128)} %param.9) | copy-start | bytes 3145732
  1.2 0.8 %copy-start.6 = (s32[1,1,4,2048]{3,2,1,0:T(4,128)S(1)}, s32[1,1,4,2048]{3,2,1,0:T(4,128)}, u32[]{:S(2)}) copy-start(s32[1,1,4,2048]{3,2,1,0:T(4,128)} %param.13) | copy-start | bytes 98308
  2.0 0.8 %copy-start.7 = (s32[1,1,4,2048]{3,2,1,0:T(4,128)S(1)}, s32[1,1,4,2048]{3,2,1,0:T(4,128)}, u32[]{:S(2)}) copy-start(s32[1,1,4,2048]{3,2,1,0:T(4,128)} %param.14) | copy-start | bytes 98308
  5.7 13.1 %collective-permute-start.2 = (f32[16,2048]{1,0:T(8,128)S(1)}, f32[16,2048]{1,0:T(8,128)S(1)}, u32[]{:S(2)}, u32[]{:S(2)}) collective-permute-start(f32[16,2048]{1,0:T(8,128)S(1)} %get-tuple-element.9), channel_id=1, source_target_pairs={{0,65},{1,66},{2,67},{3,68},{4,69},{5,70},{6,71},{7,72},{8,73},{9,... | collective-permute-start | bytes 393224 | tf_op jit(solution)/shard_map/ppermute | solution.py:24
  8.8 16.2 %collective-permute-start.3 = (f32[16,2048]{1,0:T(8,128)S(1)}, f32[16,2048]{1,0:T(8,128)S(1)}, u32[]{:S(2)}, u32[]{:S(2)}) collective-permute-start(f32[16,2048]{1,0:T(8,128)S(1)} %get-tuple-element.10), channel_id=1, source_target_pairs={{0,64},{1,65},{2,66},{3,67},{4,68},{5,69},{6,70},{7,71},{8,72},{9,... | collective-permute-start | bytes 393224 | tf_op jit(solution)/shard_map/ppermute | solution.py:24
  8.8 16.2 %collective-permute-start.4 = (f32[16,2048]{1,0:T(8,128)S(1)}, f32[16,2048]{1,0:T(8,128)S(1)}, u32[]{:S(2)}, u32[]{:S(2)}) collective-permute-start(f32[16,2048]{1,0:T(8,128)S(1)} %get-tuple-element.11), channel_id=1, source_target_pairs={{0,127},{1,64},{2,65},{3,66},{4,67},{5,68},{6,69},{7,70},{8,71},{9... | collective-permute-start | bytes 393224 | tf_op jit(solution)/shard_map/ppermute | solution.py:24
  15.7 1.7 %copy-start.1 = (f32[1,2,4,4,1024]{4,3,2,1,0:T(4,128)S(1)}, f32[1,2,4,4,1024]{4,3,2,1,0:T(4,128)}, u32[]{:S(2)}) copy-start(f32[1,2,4,4,1024]{4,3,2,1,0:T(4,128)} %param.10) | copy-start | bytes 393220
  15.7 9.3 %collective-permute-start.5 = (f32[16,2048]{1,0:T(8,128)S(1)}, f32[16,2048]{1,0:T(8,128)S(1)}, u32[]{:S(2)}, u32[]{:S(2)}) collective-permute-start(f32[16,2048]{1,0:T(8,128)S(1)} %get-tuple-element.12), channel_id=1, source_target_pairs={{0,126},{1,127},{2,64},{3,65},{4,66},{5,67},{6,68},{7,69},{8,70},{... | collective-permute-start | bytes 393224 | tf_op jit(solution)/shard_map/ppermute | solution.py:24
  17.7 31.4 %collective-permute-start = (f32[56,2,1024]{2,1,0:T(2,128)S(1)}, f32[56,2,1024]{2,1,0:T(2,128)S(1)}, u32[]{:S(2)}, u32[]{:S(2)}) collective-permute-start(f32[56,2,1024]{2,1,0:T(2,128)S(1)} %pad_maximum_fusion), channel_id=1, source_target_pairs={{0,1},{1,2},{2,3},{3,4},{4,5},{5,6},{6,7},{7,8},{8,9},{9,10},{10,1... | collective-permute-start | bytes 1376264 | tf_op jit(solution)/shard_map/ppermute | solution.py:24
  18.5 6.5 %copy-start.2 = (f32[1,16,4,1024]{3,2,1,0:T(4,128)S(1)}, f32[1,16,4,1024]{3,2,1,0:T(4,128)}, u32[]{:S(2)}) copy-start(f32[1,16,4,1024]{3,2,1,0:T(4,128)} %param.11) | copy-start | bytes 786436
  18.5 6.5 %copy-start.3 = (s32[1,8,4,1024]{3,2,1,0:T(4,128)S(1)}, s32[1,8,4,1024]{3,2,1,0:T(4,128)}, u32[]{:S(2)}) copy-start(s32[1,8,4,1024]{3,2,1,0:T(4,128)} %param.15) | copy-start | bytes 393220
  18.5 6.5 %copy-start.4 = (s32[1,8,4,1024]{3,2,1,0:T(4,128)S(1)}, s32[1,8,4,1024]{3,2,1,0:T(4,128)}, u32[]{:S(2)}) copy-start(s32[1,8,4,1024]{3,2,1,0:T(4,128)} %param.16) | copy-start | bytes 393220
  18.5 6.5 %copy-start.5 = (f32[1,8,4,1024]{3,2,1,0:T(4,128)S(1)}, f32[1,8,4,1024]{3,2,1,0:T(4,128)}, u32[]{:S(2)}) copy-start(f32[1,8,4,1024]{3,2,1,0:T(4,128)} %param.17) | copy-start | bytes 393220
  18.5 6.5 %copy-start.8 = (s32[1,4,1024]{2,1,0:T(4,128)S(1)}, s32[1,4,1024]{2,1,0:T(4,128)}, u32[]{:S(2)}) copy-start(s32[1,4,1024]{2,1,0:T(4,128)} %param.12) | copy-start | bytes 49156
  18.8 30.3 %collective-permute-start.1 = (f32[56,2,1024]{2,1,0:T(2,128)S(1)}, f32[56,2,1024]{2,1,0:T(2,128)S(1)}, u32[]{:S(2)}, u32[]{:S(2)}) collective-permute-start(f32[56,2,1024]{2,1,0:T(2,128)S(1)} %pad_maximum_fusion.1), channel_id=1, source_target_pairs={{0,63},{1,0},{2,1},{3,2},{4,3},{5,4},{6,5},{7,6},{8,7},{9,8},{10,9... | collective-permute-start | bytes 1376264 | tf_op jit(solution)/shard_map/ppermute | solution.py:24
  34.8 18.7 %collective-permute-start.7 = (f32[16,2,1024]{2,1,0:T(2,128)S(1)}, f32[16,2,1024]{2,1,0:T(2,128)S(1)}, u32[]{:S(2)}, u32[]{:S(2)}) collective-permute-start(f32[16,2,1024]{2,1,0:T(2,128)S(1)} %remap.2.first), channel_id=1, source_target_pairs={{0,63},{1,0},{2,1},{3,2},{4,3},{5,4},{6,5},{7,6},{8,7},{9,8},{10,9... | collective-permute-start | bytes 393224 | tf_op jit(solution)/shard_map/ppermute | solution.py:24
  49.0 10.3 %collective-permute-start.6 = (f32[16,2,1024]{2,1,0:T(2,128)S(1)}, f32[16,2,1024]{2,1,0:T(2,128)S(1)}, u32[]{:S(2)}, u32[]{:S(2)}) collective-permute-start(f32[16,2,1024]{2,1,0:T(2,128)S(1)} %remap.3.last), channel_id=1, source_target_pairs={{0,1},{1,2},{2,3},{3,4},{4,5},{5,6},{6,7},{7,8},{8,9},{9,10},{10,1... | collective-permute-start | bytes 393224 | tf_op jit(solution)/shard_map/ppermute | solution.py:24

commit v3 on v2

--- a/solution.py
+++ b/solution.py
@@ -10,7 +10,6 @@
 diffusion = 0.12
 LOW = 128
 VMEM_LIMIT = 48 * 2**20
-PACK_ORDER = (3, 0, 2, 1)
 UNROLL = 4
 
 
@@ -60,22 +59,54 @@
     return chosen([product[tracers * h : tracers * (h + 1)] for h in range(highs)], high)
 
 
-def pack_kernel(field, rows, cols, *rest):
-    outs, table = rest[:-1], rest[-1]
-    tracers, _, grid_rows, width = field.shape
+def pack_kernel(field, speed, rows, cols, before_v, after_v, *rest):
+    outs, (table, level0, upper, moving, row_list, col_list, sems) = rest[:-7], rest[-7:]
+    tracers, levels, grid_rows, width = field.shape
+    copies = [
+        pltpu.make_async_copy(source, target, sems.at[i])
+        for i, (source, target) in enumerate(
+            (
+                (field.at[:, 0], level0),
+                (rows, row_list),
+                (cols, col_list),
+                (speed, moving),
+                (field.at[:, pl.ds(1, levels - 1)], upper),
+            )
+        )
+    ]
+    for copy in copies:
+        copy.start()
+    for copy in copies[:3]:
+        copy.wait()
     per_row = width // LOW
 
     def part(high):
         low = high % per_row * LOW
-        return field[:, 0, high // per_row, low : low + LOW]
+        return level0[:, high // per_row, low : low + LOW]
 
     put_table(table, tracers, 0, grid_rows * per_row, part)
     block = 512
-    for near in PACK_ORDER:
+    for near in range(rows.shape[0]):
         for start in range(0, rows.shape[1], block):
             at = slice(start, start + block)
-            entry = rows[near : near + 1, at] * width + cols[near : near + 1, at]
+            entry = row_list[near : near + 1, at] * width + col_list[near : near + 1, at]
             outs[near][:, at] = looked_up(table, entry, tracers)
+    for copy in copies[3:]:
+        copy.wait()
+    for which in range(2):
+        for level in range(levels):
+            at = (levels - 1) * tracers + which * levels + level
+            after_v[at] = moving[which, level, :2]
+            before_v[at] = moving[which, level, grid_rows - 2 :]
+
+    def body(tracer, carry):
+        for level in range(levels - 1):
+            at = (levels - 1) * tracer + level
+            after_v[at] = upper[tracer, level, :2]
+            before_v[at] = upper[tracer, level, grid_rows - 2 :]
+        return carry
+
+    lax.fori_loop(0, tracers, body, 0, unroll=4)
 
 
 def level_spec(field):
@@ -83,26 +114,35 @@
     return pl.BlockSpec((tracers, 1, rows, width), lambda *_: (0, 0, 0, 0))
 
 
-def pack(field, rows, cols):
-    tracers, _, grid_rows, width = field.shape
+def pack(field, speed, rows, cols):
+    tracers, levels, grid_rows, width = field.shape
     neighbours, capacity = rows.shape
-    piece = (tracers, capacity)
+    edge = jax.ShapeDtypeStruct(((levels - 1) * tracers + 2 * levels, 2, width), jnp.float32)
+    piece = jax.ShapeDtypeStruct((tracers, capacity), jnp.float32)
     return pl.pallas_call(
         pack_kernel,
-        grid=(1,),
-        in_specs=[level_spec(field), whole_spec(rows.shape), whole_spec(cols.shape)],
-        out_specs=[whole_spec(piece)] * neighbours,
-        out_shape=[jax.ShapeDtypeStruct(piece, jnp.float32)] * neighbours,
-        scratch_shapes=[pltpu.VMEM((grid_rows * width // LOW * tracers, 2 * LOW), jnp.bfloat16)],
-        compiler_params=pltpu.CompilerParams(vmem_limit_bytes=VMEM_LIMIT),
+        in_specs=[pl.BlockSpec(memory_space=pltpu.HBM)] * 4,
+        out_shape=[edge, edge] + [piece] * neighbours,
+        scratch_shapes=[
+            pltpu.VMEM((grid_rows * width // LOW * tracers, 2 * LOW), jnp.bfloat16),
+            pltpu.VMEM((tracers, grid_rows, width), jnp.float32),
+            pltpu.VMEM((tracers, levels - 1, grid_rows, width), jnp.float32),
+            pltpu.VMEM(speed.shape, jnp.float32),
+            pltpu.VMEM(rows.shape, jnp.int32),
+            pltpu.VMEM(cols.shape, jnp.int32),
+            pltpu.SemaphoreType.DMA((5,)),
+        ],
+        compiler_params=pltpu.CompilerParams(vmem_limit_bytes=60 * 2**20),
         cost_estimate=pl.CostEstimate(flops=4 * 10**9, bytes_accessed=10**6, transcendentals=0),
         name="pack",
-    )(field, rows, cols)
+    )(field, speed, rows, cols)
 
 
 def remap_kernel(grid_rows, near, slot, weight, field, coupling, mask, *rest):
-    pieces, out, table = rest[:-2], rest[-2], rest[-1]
+    pieces, edges, out, table = rest[:4], rest[4:-2], rest[-2], rest[-1]
     tracers, capacity = pieces[0].shape
+    for edge in edges:
+        out[tracers:] = edge[...]
     width = field.shape[3]
     for index, piece in enumerate(pieces):
         put_table(
@@ -123,16 +163,16 @@
                 total = total + weight[k, row : row + 1, at] * looked_up(table, entry, tracers)
             own = field[:, 0, row, at]
             wet = mask[row : row + 1, at].astype(jnp.float32)
-            out[:, place, at] = own + coupling[:, row, at] * wet * (total - own)
+            out[:tracers, place, at] = own + coupling[:, row, at] * wet * (total - own)
             return carry
 
         lax.fori_loop(0, width // block, body, 0)
 
 
-def remap(grid_rows, pieces, near, slot, weight, field, coupling, mask):
+def remap(grid_rows, pieces, edges, near, slot, weight, field, coupling, mask):
     tracers, capacity = pieces[0].shape
-    out = (tracers, len(grid_rows), field.shape[3])
-    specs = [whole_spec(v.shape) for v in (near, slot, weight, coupling, mask, *pieces)]
+    out = (tracers + sum(edge.shape[0] for edge in edges), len(grid_rows), field.shape[3])
+    specs = [whole_spec(v.shape) for v in (near, slot, weight, coupling, mask, *pieces, *edges)]
     specs.insert(3, level_spec(field))
     return pl.pallas_call(
         functools.partial(remap_kernel, grid_rows),
@@ -144,7 +184,7 @@
         compiler_params=pltpu.CompilerParams(vmem_limit_bytes=VMEM_LIMIT),
         cost_estimate=pl.CostEstimate(flops=15 * 10**9, bytes_accessed=10**6, transcendentals=0),
         name="remap",
-    )(near, slot, weight, field, coupling, mask, *pieces)
+    )(near, slot, weight, field, coupling, mask, *pieces, *edges)
 
 
 def set_factors(factors, speed_x, speed_y):
@@ -184,12 +224,14 @@
     speeds = []
     for which in range(2):
         at = 3 * tracers + which * levels + 1 + level
-        speeds.append(jnp.concatenate([velocity[which, 1 + level], after[at], before[at]], axis=0))
+        speeds.append(
+            jnp.concatenate([velocity[which, 1 + level], after[at], before[tracers + at]], axis=0)
+        )
     set_factors(factors, *speeds)
 
     def padded(tracer):
         at = 3 * tracer + level
-        return jnp.concatenate([field[tracer, 0], after[at], before[at]], axis=0)
+        return jnp.concatenate([field[tracer, 0], after[at], before[tracers + at]], axis=0)
 
     def store(tracer, value):
         out[tracer, 0] = value
@@ -197,14 +239,16 @@
     transported(tracers, factors, padded, store)
 
 
-def surface_kernel(velocity, before_v, after_v, first, last, before, after, whole, out, factors):
+def surface_kernel(velocity, after_v, first, last, before, after, whole, out, factors):
     del whole
     tracers = first.shape[0]
     levels = velocity.shape[1]
     speeds = []
     for which in range(2):
         at = 3 * tracers + which * levels
-        speeds.append(jnp.concatenate([velocity[which, 0], after_v[at], before_v[at]], axis=0))
+        speeds.append(
+            jnp.concatenate([velocity[which, 0], after_v[at], before[tracers + at]], axis=0)
+        )
     set_factors(factors, *speeds)
 
     def padded(tracer):
@@ -236,14 +280,14 @@
         out_specs=pl.BlockSpec(block, lambda level: (0, level + 1, 0, 0)),
         scratch_shapes=[pltpu.VMEM((4, 8, width), jnp.float32)],
         compiler_params=pltpu.CompilerParams(vmem_limit_bytes=VMEM_LIMIT),
-        cost_estimate=pl.CostEstimate(flops=10**9, bytes_accessed=3 * 10**6, transcendentals=0),
+        cost_estimate=pl.CostEstimate(flops=10**6, bytes_accessed=10**5, transcendentals=0),
         name="upper_levels",
     )(field, before, after, velocity)
 
 
-def surface_level(velocity, before_v, after_v, first, last, before, after, whole):
+def surface_level(velocity, after_v, first, last, before, after, whole):
     tracers, _, rows, width = whole.shape
-    values = (velocity, before_v, after_v, first, last, before, after)
+    values = (velocity, after_v, first, last, before, after)
     return pl.pallas_call(
         surface_kernel,
         grid=(1,),
@@ -271,19 +315,9 @@
     field = tracer[0]
     speed = velocity[0]
     tracers, levels, rows, width = field.shape
-    packed = pack(field, send_rows[0, 0], send_cols[0, 0])
+    before_v, after_v, *packed = pack(field, speed, send_rows[0, 0], send_cols[0, 0])
     pieces = [moved(packed[near], 1 - near, True) for near in range(len(packed))]
-
-    def edge(start):
-        upper = lax.slice_in_dim(field[:, 1:], start, start + 2, axis=2)
-        moving = lax.slice_in_dim(speed, start, start + 2, axis=2)
-        return jnp.concatenate(
-            [upper.reshape(tracers * (levels - 1), 2, width), moving.reshape(2 * levels, 2, width)], axis=0
-        )
-
-    before_v = moved(edge(rows - 2), 1, False)
-    after_v = moved(edge(0), -1, False)
-
+    after_v = moved(after_v, -1, False)
     shared = (
         intersection_near[0],
         intersection_slot[0],
@@ -292,12 +326,13 @@
         coupling[0],
         sea_mask[0],
     )
-    first = remap((0, 1), pieces, *shared)
+    last = remap((2, 3), pieces, [before_v], *shared)
+    before = moved(last, 1, False)
+    pieces, last = lax.optimization_barrier((pieces, last))
+    first = remap((0, 1), pieces, [], *shared)
     after = moved(first, -1, False)
-    last = remap((2, 3), pieces, *shared)
-    before = moved(last, 1, False)
-    whole = upper_levels(field, before_v, after_v, speed)
-    return surface_level(speed, before_v, after_v, first, last, before, after, whole)[None]
+    whole = upper_levels(field, before, after_v, speed)
+    return surface_level(speed, after_v, first, last, before, after, whole)[None]
 
 
 def solution(mesh):

time: 61.4 us -> 60.3 us (0.982)
  starting transfers between devices: 23 us -> 19.4 us
  waiting for transfers between devices: 5.75 us -> 8.38 us
  Pallas kernels: 28.7 us -> 31.2 us
  local copies, waits for them, and re-layouts: 3.12 us -> 1.05 us
    ppermute x8 -> x7, starting transfers between devices: 23 us -> 19.4 us  [moved(): return lax.ppermute(value, ('comp', 'tile'), pairs)]
    ppermute x8 -> x7, waiting for transfers between devices: 5.75 us -> 8.38 us  [moved(): return lax.ppermute(value, ('comp', 'tile'), pairs)]
    pallas_call x1, Pallas kernels: 2.91 us -> 5.36 us  [pack(): pl.pallas_call(pack_kernel, in_specs=[pl.BlockSpec(memory_space=pltpu.HBM...]
    unnamed x18 -> x16, local copies, waits for them, and re-layouts: 2.76 us -> 1.05 us
  transfers between devices with their start and end apart: 8 -> 7, of which waited for: 1 -> 3; matrix products, arithmetic and copies ran while one was open for 1% -> 0% of each run, Pallas kernels for 39% -> 40%
where the time goes in v3:
time: 60.3 us; the launch traced here: 60.1 us
  Pallas kernels  31.2 us (52%)
  starting transfers between devices  19.4 us (32%)
  waiting for transfers between devices  8.38 us (14%)
  local copies, waits for them, and re-layouts  1.05 us (2%)
    pallas_call x2, Pallas kernels, remap(): pl.pallas_call(functools.partial(remap_kernel, grid_rows), grid=(1,), in_...  19.6 us
    ppermute x7, starting transfers between devices, moved(): return lax.ppermute(value, ('comp', 'tile'), pairs)  19.4 us
    ppermute x7, waiting for transfers between devices, moved(): return lax.ppermute(value, ('comp', 'tile'), pairs)  8.38 us
    pallas_call x1, Pallas kernels, pack(): pl.pallas_call(pack_kernel, in_specs=[pl.BlockSpec(memory_space=pltpu.HBM...  5.36 us
    pallas_call x1, Pallas kernels, upper_levels(): pl.pallas_call(upper_kernel, grid=(levels - 1,), out_shape=jax.ShapeDtype...  4.41 us
    pallas_call x1, Pallas kernels, surface_level(): pl.pallas_call(surface_kernel, grid=(1,), out_shape=jax.ShapeDtypeStruct(...  1.87 us
  transfers between devices with their start and end apart: 7, of which 3 were waited for; matrix products, arithmetic and copies ran while one was open for 0% of the time, Pallas kernels for 40%

profile of v3, /device:TPU:1, one launch (start us, length us, event | category | flops | bytes accessed | tf_op | source)
XLA Modules:
  0.0 60.1 jit_solution(3911267296116211346)
XLA Ops:
  0.0 0.0 copy-start
  0.0 0.0 copy-start.2
  0.0 0.0 copy-start.3
  0.0 0.0 copy-start.4
  0.0 0.0 copy-start.5
  0.0 5.4 %pack.1 = (f32[56,2,1024]{2,1,0:T(2,128)}, f32[56,2,1024]{2,1,0:T(2,128)}, f32[16,2048]{1,0:T(8,128)}, f32[16,2048]{1,0:T(8,128)}, f32[16,2048]{1,0:T(8,128)}, /*index=5*/f32[16,2048]{1,0:T(8,128)}) custom-call(f32[16,4,4,1024]{3,2,1,0:T(4,128)} %bitcast.10, f32[2,4,4,1024]{3,2,1,0:T(4,128)} %bitcast.14, s32[4,2048]{1,0:T(4,128)} %bitcast.27, s32[4,2048]{1,0:T(4,128)} %bitcast.28), custom_call_target="tpu_custom_call" | custom-call | flops 4000000000 | bytes 1000000 | tf_op jit(solution)/shard_map/pack/pallas_call | solution.py:122
  5.4 0.0 copy-start.6
  5.4 3.1 %collective-permute-start.1 = (f32[16,2048]{1,0:T(8,128)}, f32[16,2048]{1,0:T(8,128)S(1)}, u32[]{:S(2)}, u32[]{:S(2)}) collective-permute-start(f32[16,2048]{1,0:T(8,128)} %get-tuple-element.17), channel_id=1, source_target_pairs={{0,65},{1,66},{2,67},{3,68},{4,69},{5,70},{6,71},{7,72},{8,73},{9,... | collective-permute-start | bytes 393224 | tf_op jit(solution)/shard_map/ppermute | solution.py:23
  8.5 0.0 collective-permute-start.2
  8.5 6.9 %collective-permute-start.3 = (f32[16,2048]{1,0:T(8,128)}, f32[16,2048]{1,0:T(8,128)S(1)}, u32[]{:S(2)}, u32[]{:S(2)}) collective-permute-start(f32[16,2048]{1,0:T(8,128)} %get-tuple-element.19), channel_id=1, source_target_pairs={{0,127},{1,64},{2,65},{3,66},{4,67},{5,68},{6,69},{7,70},{8,71},{9... | collective-permute-start | bytes 393224 | tf_op jit(solution)/shard_map/ppermute | solution.py:23
  15.4 1.4 %collective-permute-start.4 = (f32[16,2048]{1,0:T(8,128)}, f32[16,2048]{1,0:T(8,128)S(1)}, u32[]{:S(2)}, u32[]{:S(2)}) collective-permute-start(f32[16,2048]{1,0:T(8,128)} %get-tuple-element.20), channel_id=1, source_target_pairs={{0,126},{1,127},{2,64},{3,65},{4,66},{5,67},{6,68},{7,69},{8,70},{... | collective-permute-start | bytes 393224 | tf_op jit(solution)/shard_map/ppermute | solution.py:23
  16.9 0.7 %collective-permute-start = (f32[56,2,1024]{2,1,0:T(2,128)}, f32[56,2,1024]{2,1,0:T(2,128)S(1)}, u32[]{:S(2)}, u32[]{:S(2)}) collective-permute-start(f32[56,2,1024]{2,1,0:T(2,128)} %get-tuple-element.16), channel_id=1, source_target_pairs={{0,63},{1,0},{2,1},{3,2},{4,3},{5,4},{6,5},{7,6},{8,7},{9,8},{10,9... | collective-permute-start | bytes 1376264 | tf_op jit(solution)/shard_map/ppermute | solution.py:23
  17.6 1.1 %collective-permute-done.1.rest_0_ = f32[16,2048]{1,0:T(8,128)S(1)} collective-permute-done((f32[16,2048]{1,0:T(8,128)}, f32[16,2048]{1,0:T(8,128)S(1)}, u32[]{:S(2)}, u32[]{:S(2)}) %collective-permute-start.1) | collective-permute-done | bytes 131104 | tf_op jit(solution)/shard_map/ppermute | solution.py:23
  18.7 0.0 collective-permute-done.2.rest_1_
  18.7 0.0 collective-permute-done.3.rest_2_
  18.7 4.1 %collective-permute-done.4.rest_3_ = f32[16,2048]{1,0:T(8,128)S(1)} collective-permute-done((f32[16,2048]{1,0:T(8,128)}, f32[16,2048]{1,0:T(8,128)S(1)}, u32[]{:S(2)}, u32[]{:S(2)}) %collective-permute-start.4) | collective-permute-done | bytes 131104 | tf_op jit(solution)/shard_map/ppermute | solution.py:23
  22.8 0.0 copy-done
  22.8 0.0 copy-done.2
  22.8 0.0 copy-done.3
  22.8 0.0 copy-done.4
  22.8 0.0 copy-done.5
  22.8 0.0 copy-done.6
  22.8 0.0 copy-start.7
  22.8 1.0 %copy-done.7 = f32[56,2,1024]{2,1,0:T(2,128)S(1)} copy-done((f32[56,2,1024]{2,1,0:T(2,128)S(1)}, f32[56,2,1024]{2,1,0:T(2,128)}, u32[]{:S(2)}) %copy-start.7) | copy-done | bytes 458776
  23.8 9.8 %remap.2.last = f32[72,2,1024]{2,1,0:T(2,128)S(1)} custom-call(s32[8,4,1024]{2,1,0:T(4,128)S(1)} %bitcast.19, s32[8,4,1024]{2,1,0:T(4,128)S(1)} %bitcast.21, f32[8,4,1024]{2,1,0:T(4,128)S(1)} %bitcast.23, f32[16,4,4,1024]{3,2,1,0:T(4,128)S(1)} %bitcast.11, f32[16,4,1024]{2,1,0:T(4,128)S(1)} %bitcast.17, s32[4,1024]{1,0:T(4,128)S(1)} %bitcast.25, ...), custom_call_target="tpu_custom_call" | custom-call | flops 15000000512 | bytes 1000000 | tf_op jit(solution)/shard_map/remap/pallas_call | solution.py:177
  33.6 0.0 copy-start.1
  33.6 0.3 collective-permute-start.5
  33.9 9.8 %remap.3.first = f32[16,2,1024]{2,1,0:T(2,128)S(1)} custom-call(s32[8,4,1024]{2,1,0:T(4,128)S(1)} %bitcast.20, s32[8,4,1024]{2,1,0:T(4,128)S(1)} %bitcast.22, f32[8,4,1024]{2,1,0:T(4,128)S(1)} %bitcast.24, f32[16,4,4,1024]{3,2,1,0:T(4,128)S(1)} %bitcast.12, f32[16,4,1024]{2,1,0:T(4,128)S(1)} %bitcast.18, s32[4,1024]{1,0:T(4,128)S(1)} %bitcast.26, ...), custom_call_target="tpu_custom_call" | custom-call | flops 15000000512 | bytes 1000000 | tf_op jit(solution)/shard_map/remap/pallas_call | solution.py:177
  43.7 6.9 %collective-permute-start.6 = (f32[16,2,1024]{2,1,0:T(2,128)S(1)}, f32[16,2,1024]{2,1,0:T(2,128)S(1)}, u32[]{:S(2)}, u32[]{:S(2)}) collective-permute-start(f32[16,2,1024]{2,1,0:T(2,128)S(1)} %remap.3.first), channel_id=1, source_target_pairs={{0,63},{1,0},{2,1},{3,2},{4,3},{5,4},{6,5},{7,6},{8,7},{9,8},{10,9... | collective-permute-start | bytes 393224 | tf_op jit(solution)/shard_map/ppermute | solution.py:23
  50.6 0.0 collective-permute-done.after.after_v
  50.6 3.2 %collective-permute-done.5.before = f32[72,2,1024]{2,1,0:T(2,128)S(1)} collective-permute-done((f32[72,2,1024]{2,1,0:T(2,128)S(1)}, f32[72,2,1024]{2,1,0:T(2,128)S(1)}, u32[]{:S(2)}, u32[]{:S(2)}) %collective-permute-start.5) | collective-permute-done | bytes 589856 | tf_op jit(solution)/shard_map/ppermute | solution.py:23
  53.8 0.0 copy-done.1
  53.8 4.4 %upper_levels.1.whole = f32[16,4,4,1024]{3,2,1,0:T(4,128)} custom-call(f32[16,4,4,1024]{3,2,1,0:T(4,128)S(1)} %bitcast.13, f32[72,2,1024]{2,1,0:T(2,128)S(1)} %collective-permute-done.5.before, f32[56,2,1024]{2,1,0:T(2,128)S(1)} %collective-permute-done.after.after_v, f32[2,4,4,1024]{3,2,1,0:T(4,128)S(1)} %bitcast.15), custom_call_target="tpu_custom_call" | custom-call | flops 1000000 | bytes 100000 | tf_op jit(solution)/shard_map/upper_levels/pallas_call | solution.py:270
  58.2 0.0 collective-permute-done.6.after
  58.2 1.9 %surface_level.1 = f32[16,4,4,1024]{3,2,1,0:T(4,128)} custom-call(f32[2,4,4,1024]{3,2,1,0:T(4,128)S(1)} %bitcast.16, f32[56,2,1024]{2,1,0:T(2,128)S(1)} %collective-permute-done.after.after_v, f32[16,2,1024]{2,1,0:T(2,128)S(1)} %remap.3.first, f32[72,2,1024]{2,1,0:T(2,128)S(1)} %remap.2.last, ...), custom_call_target="tpu_custom_call", output_to_operand_aliasing={{}: (6, {})} | custom-call | tf_op jit(solution)/shard_map/surface_level/pallas_call | solution.py:291
Async XLA Ops:
  0.0 22.8 %copy-start = (f32[1,16,4,4,1024]{4,3,2,1,0:T(4,128)S(1)}, f32[1,16,4,4,1024]{4,3,2,1,0:T(4,128)}, u32[]{:S(2)}) copy-start(f32[1,16,4,4,1024]{4,3,2,1,0:T(4,128)} %param.9) | copy-start | bytes 3145732
  0.0 22.8 %copy-start.2 = (f32[1,16,4,1024]{3,2,1,0:T(4,128)S(1)}, f32[1,16,4,1024]{3,2,1,0:T(4,128)}, u32[]{:S(2)}) copy-start(f32[1,16,4,1024]{3,2,1,0:T(4,128)} %param.11) | copy-start | bytes 786436
  0.0 22.8 %copy-start.3 = (s32[1,8,4,1024]{3,2,1,0:T(4,128)S(1)}, s32[1,8,4,1024]{3,2,1,0:T(4,128)}, u32[]{:S(2)}) copy-start(s32[1,8,4,1024]{3,2,1,0:T(4,128)} %param.15) | copy-start | bytes 393220
  0.0 22.8 %copy-start.4 = (s32[1,8,4,1024]{3,2,1,0:T(4,128)S(1)}, s32[1,8,4,1024]{3,2,1,0:T(4,128)}, u32[]{:S(2)}) copy-start(s32[1,8,4,1024]{3,2,1,0:T(4,128)} %param.16) | copy-start | bytes 393220
  0.0 22.8 %copy-start.5 = (f32[1,8,4,1024]{3,2,1,0:T(4,128)S(1)}, f32[1,8,4,1024]{3,2,1,0:T(4,128)}, u32[]{:S(2)}) copy-start(f32[1,8,4,1024]{3,2,1,0:T(4,128)} %param.17) | copy-start | bytes 393220
  5.4 17.4 %copy-start.6 = (s32[1,4,1024]{2,1,0:T(4,128)S(1)}, s32[1,4,1024]{2,1,0:T(4,128)}, u32[]{:S(2)}) copy-start(s32[1,4,1024]{2,1,0:T(4,128)} %param.12) | copy-start | bytes 49156
  5.4 13.3 %collective-permute-start.1 = (f32[16,2048]{1,0:T(8,128)}, f32[16,2048]{1,0:T(8,128)S(1)}, u32[]{:S(2)}, u32[]{:S(2)}) collective-permute-start(f32[16,2048]{1,0:T(8,128)} %get-tuple-element.17), channel_id=1, source_target_pairs={{0,65},{1,66},{2,67},{3,68},{4,69},{5,70},{6,71},{7,72},{8,73},{9,... | collective-permute-start | bytes 393224 | tf_op jit(solution)/shard_map/ppermute | solution.py:23
  8.5 10.2 %collective-permute-start.2 = (f32[16,2048]{1,0:T(8,128)}, f32[16,2048]{1,0:T(8,128)S(1)}, u32[]{:S(2)}, u32[]{:S(2)}) collective-permute-start(f32[16,2048]{1,0:T(8,128)} %get-tuple-element.18), channel_id=1, source_target_pairs={{0,64},{1,65},{2,66},{3,67},{4,68},{5,69},{6,70},{7,71},{8,72},{9,... | collective-permute-start | bytes 393224 | tf_op jit(solution)/shard_map/ppermute | solution.py:23
  8.5 10.2 %collective-permute-start.3 = (f32[16,2048]{1,0:T(8,128)}, f32[16,2048]{1,0:T(8,128)S(1)}, u32[]{:S(2)}, u32[]{:S(2)}) collective-permute-start(f32[16,2048]{1,0:T(8,128)} %get-tuple-element.19), channel_id=1, source_target_pairs={{0,127},{1,64},{2,65},{3,66},{4,67},{5,68},{6,69},{7,70},{8,71},{9... | collective-permute-start | bytes 393224 | tf_op jit(solution)/shard_map/ppermute | solution.py:23
  15.4 7.3 %collective-permute-start.4 = (f32[16,2048]{1,0:T(8,128)}, f32[16,2048]{1,0:T(8,128)S(1)}, u32[]{:S(2)}, u32[]{:S(2)}) collective-permute-start(f32[16,2048]{1,0:T(8,128)} %get-tuple-element.20), channel_id=1, source_target_pairs={{0,126},{1,127},{2,64},{3,65},{4,66},{5,67},{6,68},{7,69},{8,70},{... | collective-permute-start | bytes 393224 | tf_op jit(solution)/shard_map/ppermute | solution.py:23
  16.9 33.8 %collective-permute-start = (f32[56,2,1024]{2,1,0:T(2,128)}, f32[56,2,1024]{2,1,0:T(2,128)S(1)}, u32[]{:S(2)}, u32[]{:S(2)}) collective-permute-start(f32[56,2,1024]{2,1,0:T(2,128)} %get-tuple-element.16), channel_id=1, source_target_pairs={{0,63},{1,0},{2,1},{3,2},{4,3},{5,4},{6,5},{7,6},{8,7},{9,8},{10,9... | collective-permute-start | bytes 1376264 | tf_op jit(solution)/shard_map/ppermute | solution.py:23
  22.8 1.0 %copy-start.7 = (f32[56,2,1024]{2,1,0:T(2,128)S(1)}, f32[56,2,1024]{2,1,0:T(2,128)}, u32[]{:S(2)}) copy-start(f32[56,2,1024]{2,1,0:T(2,128)} %get-tuple-element.21.rest_4_) | copy-start | bytes 1376260
  33.6 20.2 %copy-start.1 = (f32[1,2,4,4,1024]{4,3,2,1,0:T(4,128)S(1)}, f32[1,2,4,4,1024]{4,3,2,1,0:T(4,128)}, u32[]{:S(2)}) copy-start(f32[1,2,4,4,1024]{4,3,2,1,0:T(4,128)} %param.10) | copy-start | bytes 393220
  33.6 20.2 %collective-permute-start.5 = (f32[72,2,1024]{2,1,0:T(2,128)S(1)}, f32[72,2,1024]{2,1,0:T(2,128)S(1)}, u32[]{:S(2)}, u32[]{:S(2)}) collective-permute-start(f32[72,2,1024]{2,1,0:T(2,128)S(1)} %remap.2.last), channel_id=1, source_target_pairs={{0,1},{1,2},{2,3},{3,4},{4,5},{5,6},{6,7},{7,8},{8,9},{9,10},{10,1... | collective-permute-start | bytes 1769480 | tf_op jit(solution)/shard_map/ppermute | solution.py:23
  43.7 14.6 %collective-permute-start.6 = (f32[16,2,1024]{2,1,0:T(2,128)S(1)}, f32[16,2,1024]{2,1,0:T(2,128)S(1)}, u32[]{:S(2)}, u32[]{:S(2)}) collective-permute-start(f32[16,2,1024]{2,1,0:T(2,128)S(1)} %remap.3.first), channel_id=1, source_target_pairs={{0,63},{1,0},{2,1},{3,2},{4,3},{5,4},{6,5},{7,6},{8,7},{9,8},{10,9... | collective-permute-start | bytes 393224 | tf_op jit(solution)/shard_map/ppermute | solution.py:23

commit v4 on v2

--- a/solution.py
+++ b/solution.py
@@ -9,9 +9,11 @@
 
 diffusion = 0.12
 LOW = 128
+BLOCK = 512
+UNROLL = 4
 VMEM_LIMIT = 48 * 2**20
-PACK_ORDER = (3, 0, 2, 1)
-UNROLL = 4
+FULL_VMEM = 60 * 2**20
+SMALL_COST = pl.CostEstimate(flops=10**6, bytes_accessed=10**5, transcendentals=0)
 
 
 def moved(value, steps, swap):
@@ -50,32 +52,80 @@
     return values[0]
 
 
-def looked_up(table, entry, tracers):
-    width = entry.shape[1]
-    highs = table.shape[0] // tracers
+def low_product(table, entry, tracers):
     hot = one_hot(entry & (LOW - 1))
     hot = jnp.concatenate([hot, hot], axis=0)
     product = jnp.dot(table[...], hot, preferred_element_type=jnp.float32)
-    high = jnp.broadcast_to(entry // LOW, (tracers, width))
-    return chosen([product[tracers * h : tracers * (h + 1)] for h in range(highs)], high)
+    return [product[at : at + tracers] for at in range(0, table.shape[0], tracers)]
+
+
+def high_part(entry, tracers):
+    return jnp.broadcast_to(entry // LOW, (tracers, entry.shape[1]))
+
+
+def started(pairs, sems):
+    copies = [pltpu.make_async_copy(source, target, sems.at[i]) for i, (source, target) in enumerate(pairs)]
+    for copy in copies:
+        copy.start()
+    return copies
+
+
+def edges_kernel(field, speed, before_v, after_v, upper, moving, sems):
+    tracers, levels, grid_rows, _ = field.shape
+    for copy in started(((speed, moving), (field.at[:, pl.ds(1, levels - 1)], upper)), sems):
+        copy.wait()
+    for which in range(2):
+        for level in range(levels):
+            at = (levels - 1) * tracers + which * levels + level
+            after_v[at] = moving[which, level, :2]
+            before_v[at] = moving[which, level, grid_rows - 2 :]
+
+    def body(tracer, carry):
+        for level in range(levels - 1):
+            at = (levels - 1) * tracer + level
+            after_v[at] = upper[tracer, level, :2]
+            before_v[at] = upper[tracer, level, grid_rows - 2 :]
+        return carry
+
+    lax.fori_loop(0, tracers, body, 0, unroll=4)
+
+
+def edges(field, speed):
+    tracers, levels, grid_rows, width = field.shape
+    edge = jax.ShapeDtypeStruct(((levels - 1) * tracers + 2 * levels, 2, width), jnp.float32)
+    return pl.pallas_call(
+        edges_kernel,
+        in_specs=[pl.BlockSpec(memory_space=pltpu.HBM)] * 2,
+        out_shape=[edge, edge],
+        scratch_shapes=[
+            pltpu.VMEM((tracers, levels - 1, grid_rows, width), jnp.float32),
+            pltpu.VMEM(speed.shape, jnp.float32),
+            pltpu.SemaphoreType.DMA((2,)),
+        ],
+        compiler_params=pltpu.CompilerParams(vmem_limit_bytes=FULL_VMEM),
+        cost_estimate=SMALL_COST,
+        name="edges",
+    )(field, speed)
 
 
 def pack_kernel(field, rows, cols, *rest):
-    outs, table = rest[:-1], rest[-1]
+    outs, (table, level0, row_list, col_list, sems) = rest[:-5], rest[-5:]
     tracers, _, grid_rows, width = field.shape
+    for copy in started(((field.at[:, 0], level0), (rows, row_list), (cols, col_list)), sems):
+        copy.wait()
     per_row = width // LOW
 
     def part(high):
         low = high % per_row * LOW
-        return field[:, 0, high // per_row, low : low + LOW]
+        return level0[:, high // per_row, low : low + LOW]
 
     put_table(table, tracers, 0, grid_rows * per_row, part)
-    block = 512
-    for near in PACK_ORDER:
-        for start in range(0, rows.shape[1], block):
-            at = slice(start, start + block)
-            entry = rows[near : near + 1, at] * width + cols[near : near + 1, at]
-            outs[near][:, at] = looked_up(table, entry, tracers)
+    for near in range(rows.shape[0]):
+        for start in range(0, rows.shape[1], BLOCK):
+            at = slice(start, start + BLOCK)
+            entry = row_list[near : near + 1, at] * width + col_list[near : near + 1, at]
+            product = low_product(table, entry, tracers)
+            outs[near][:, at] = chosen(product, high_part(entry, tracers))
 
 
 def level_spec(field):
@@ -86,56 +136,105 @@
 def pack(field, rows, cols):
     tracers, _, grid_rows, width = field.shape
     neighbours, capacity = rows.shape
-    piece = (tracers, capacity)
+    piece = jax.ShapeDtypeStruct((tracers, capacity), jnp.float32)
     return pl.pallas_call(
         pack_kernel,
-        grid=(1,),
-        in_specs=[level_spec(field), whole_spec(rows.shape), whole_spec(cols.shape)],
-        out_specs=[whole_spec(piece)] * neighbours,
-        out_shape=[jax.ShapeDtypeStruct(piece, jnp.float32)] * neighbours,
-        scratch_shapes=[pltpu.VMEM((grid_rows * width // LOW * tracers, 2 * LOW), jnp.bfloat16)],
-        compiler_params=pltpu.CompilerParams(vmem_limit_bytes=VMEM_LIMIT),
-        cost_estimate=pl.CostEstimate(flops=4 * 10**9, bytes_accessed=10**6, transcendentals=0),
+        in_specs=[pl.BlockSpec(memory_space=pltpu.HBM)] * 3,
+        out_shape=[piece] * neighbours,
+        scratch_shapes=[
+            pltpu.VMEM((grid_rows * width // LOW * tracers, 2 * LOW), jnp.bfloat16),
+            pltpu.VMEM((tracers, grid_rows, width), jnp.float32),
+            pltpu.VMEM(rows.shape, jnp.int32),
+            pltpu.VMEM(cols.shape, jnp.int32),
+            pltpu.SemaphoreType.DMA((3,)),
+        ],
+        compiler_params=pltpu.CompilerParams(vmem_limit_bytes=FULL_VMEM),
+        cost_estimate=SMALL_COST,
         name="pack",
     )(field, rows, cols)
 
 
-def remap_kernel(grid_rows, near, slot, weight, field, coupling, mask, *rest):
-    pieces, out, table = rest[:-2], rest[-2], rest[-1]
+def added_reads(sources, near, slot, weight, table, tracers, row, at):
+    total = None
+    for k in range(near.shape[0]):
+        which = near[k, row : row + 1, at]
+        entry = slot[k, row : row + 1, at]
+        product = low_product(table, entry, tracers)
+        high = high_part(entry, tracers)
+        count = len(product) // len(sources)
+        wide = jnp.broadcast_to(which, high.shape)
+        read = chosen(product[:count], high)
+        inside = which == sources[0]
+        for rank in range(1, len(sources)):
+            part = chosen(product[rank * count : (rank + 1) * count], high)
+            read = jnp.where(wide == sources[rank], part, read)
+            inside = inside | (which == sources[rank])
+        term = jnp.where(inside, weight[k, row : row + 1, at], 0.0) * read
+        total = term if total is None else total + term
+    return total
+
+
+def put_pieces(table, pieces):
     tracers, capacity = pieces[0].shape
-    width = field.shape[3]
+    count = capacity // LOW
     for index, piece in enumerate(pieces):
         put_table(
-            table,
-            tracers,
-            index * (capacity // LOW),
-            capacity // LOW,
-            lambda high, piece=piece: piece[:, high * LOW : (high + 1) * LOW],
+            table, tracers, index * count, count, lambda high, piece=piece: piece[:, high * LOW : (high + 1) * LOW]
         )
-    block = 512
+
+
+def near_kernel(sources, near, slot, weight, piece, out, table):
+    tracers = piece.shape[0]
+    put_pieces(table, [piece])
+    width = near.shape[2]
+    for row in range(near.shape[1]):
+
+        def body(step, carry, row=row):
+            at = pl.ds(pl.multiple_of(step * BLOCK, BLOCK), BLOCK)
+            out[:, row, at] = added_reads(sources, near, slot, weight, table, tracers, row, at)
+            return carry
+
+        lax.fori_loop(0, width // BLOCK, body, 0)
+
+
+def remap_near(source, near, slot, weight, piece):
+    tracers, capacity = piece.shape
+    _, rows, width = near.shape
+    return pl.pallas_call(
+        functools.partial(near_kernel, (source,)),
+        out_shape=jax.ShapeDtypeStruct((tracers, rows, width), jnp.float32),
+        scratch_shapes=[pltpu.VMEM((capacity // LOW * tracers, 2 * LOW), jnp.bfloat16)],
+        compiler_params=pltpu.CompilerParams(vmem_limit_bytes=VMEM_LIMIT),
+        cost_estimate=SMALL_COST,
+        name="remap_near",
+    )(near, slot, weight, piece)
+
+
+def remap_kernel(sources, grid_rows, near, slot, weight, field, coupling, mask, partial, *rest):
+    pieces, (out, table) = rest[:-2], rest[-2:]
+    tracers = field.shape[0]
+    put_pieces(table, pieces)
     for place, row in enumerate(grid_rows):
 
         def body(step, carry, place=place, row=row):
-            at = pl.ds(pl.multiple_of(step * block, block), block)
-            total = jnp.zeros((tracers, block), jnp.float32)
-            for k in range(near.shape[0]):
-                entry = near[k, row : row + 1, at] * capacity + slot[k, row : row + 1, at]
-                total = total + weight[k, row : row + 1, at] * looked_up(table, entry, tracers)
+            at = pl.ds(pl.multiple_of(step * BLOCK, BLOCK), BLOCK)
+            total = added_reads(sources, near, slot, weight, table, tracers, row, at)
+            total = total + partial[:, row, at]
             own = field[:, 0, row, at]
             wet = mask[row : row + 1, at].astype(jnp.float32)
             out[:, place, at] = own + coupling[:, row, at] * wet * (total - own)
             return carry
 
-        lax.fori_loop(0, width // block, body, 0)
-
-
-def remap(grid_rows, pieces, near, slot, weight, field, coupling, mask):
+        lax.fori_loop(0, field.shape[3] // BLOCK, body, 0)
+
+
+def remap(sources, grid_rows, pieces, near, slot, weight, field, coupling, mask, partial):
     tracers, capacity = pieces[0].shape
     out = (tracers, len(grid_rows), field.shape[3])
-    specs = [whole_spec(v.shape) for v in (near, slot, weight, coupling, mask, *pieces)]
+    specs = [whole_spec(v.shape) for v in (near, slot, weight, coupling, mask, partial, *pieces)]
     specs.insert(3, level_spec(field))
     return pl.pallas_call(
-        functools.partial(remap_kernel, grid_rows),
+        functools.partial(remap_kernel, sources, grid_rows),
         grid=(1,),
         in_specs=specs,
         out_specs=whole_spec(out),
@@ -144,7 +243,7 @@
         compiler_params=pltpu.CompilerParams(vmem_limit_bytes=VMEM_LIMIT),
         cost_estimate=pl.CostEstimate(flops=15 * 10**9, bytes_accessed=10**6, transcendentals=0),
         name="remap",
-    )(near, slot, weight, field, coupling, mask, *pieces)
+    )(near, slot, weight, field, coupling, mask, partial, *pieces)
 
 
 def set_factors(factors, speed_x, speed_y):
@@ -177,19 +276,21 @@
     lax.fori_loop(0, tracers // UNROLL, body, 0)
 
 
-def upper_kernel(field, before, after, velocity, out, factors):
+def upper_kernel(field, before_v, after_v, velocity, out, factors):
     level = pl.program_id(0)
     tracers = field.shape[0]
     levels = velocity.shape[1]
     speeds = []
     for which in range(2):
         at = 3 * tracers + which * levels + 1 + level
-        speeds.append(jnp.concatenate([velocity[which, 1 + level], after[at], before[at]], axis=0))
+        speeds.append(
+            jnp.concatenate([velocity[which, 1 + level], after_v[at], before_v[at]], axis=0)
+        )
     set_factors(factors, *speeds)
 
     def padded(tracer):
         at = 3 * tracer + level
-        return jnp.concatenate([field[tracer, 0], after[at], before[at]], axis=0)
+        return jnp.concatenate([field[tracer, 0], after_v[at], before_v[at]], axis=0)
 
     def store(tracer, value):
         out[tracer, 0] = value
@@ -204,7 +305,9 @@
     speeds = []
     for which in range(2):
         at = 3 * tracers + which * levels
-        speeds.append(jnp.concatenate([velocity[which, 0], after_v[at], before_v[at]], axis=0))
+        speeds.append(
+            jnp.concatenate([velocity[which, 0], after_v[at], before_v[at]], axis=0)
+        )
     set_factors(factors, *speeds)
 
     def padded(tracer):
@@ -236,7 +339,7 @@
         out_specs=pl.BlockSpec(block, lambda level: (0, level + 1, 0, 0)),
         scratch_shapes=[pltpu.VMEM((4, 8, width), jnp.float32)],
         compiler_params=pltpu.CompilerParams(vmem_limit_bytes=VMEM_LIMIT),
-        cost_estimate=pl.CostEstimate(flops=10**9, bytes_accessed=3 * 10**6, transcendentals=0),
+        cost_estimate=SMALL_COST,
         name="upper_levels",
     )(field, before, after, velocity)
 
@@ -271,31 +374,23 @@
     field = tracer[0]
     speed = velocity[0]
     tracers, levels, rows, width = field.shape
-    packed = pack(field, send_rows[0, 0], send_cols[0, 0])
-    pieces = [moved(packed[near], 1 - near, True) for near in range(len(packed))]
-
-    def edge(start):
-        upper = lax.slice_in_dim(field[:, 1:], start, start + 2, axis=2)
-        moving = lax.slice_in_dim(speed, start, start + 2, axis=2)
-        return jnp.concatenate(
-            [upper.reshape(tracers * (levels - 1), 2, width), moving.reshape(2 * levels, 2, width)], axis=0
-        )
-
-    before_v = moved(edge(rows - 2), 1, False)
-    after_v = moved(edge(0), -1, False)
-
-    shared = (
-        intersection_near[0],
-        intersection_slot[0],
-        intersection_weight[0],
-        field,
-        coupling[0],
-        sea_mask[0],
-    )
-    first = remap((0, 1), pieces, *shared)
+    near, slot, weight = intersection_near[0], intersection_slot[0], intersection_weight[0]
+    others = (0, 2, 3)
+    before_v, after_v = edges(field, speed)
+    before_v, lists = lax.optimization_barrier((before_v, (send_rows[0, 0], send_cols[0, 0])))
+    packed = pack(field, *lists)
+    before_v = moved(before_v, 1, False)
+    pieces = [moved(packed[j], 1 - j, True) for j in range(len(packed))]
+    after_v = moved(after_v, -1, False)
+    partial = remap_near(1, near, slot, weight, pieces[1])
+    pieces, before_v = lax.optimization_barrier(([pieces[j] for j in others], before_v))
+    shared = (near, slot, weight, field, coupling[0], sea_mask[0], partial)
+    last = remap(others, (2, 3), pieces, *shared)
+    before = moved(last, 1, False)
+    pieces, last = lax.optimization_barrier((pieces, last))
+    first = remap(others, (0, 1), pieces, *shared)
     after = moved(first, -1, False)
-    last = remap((2, 3), pieces, *shared)
-    before = moved(last, 1, False)
+    before_v, before = lax.optimization_barrier((before_v, before))
     whole = upper_levels(field, before_v, after_v, speed)
     return surface_level(speed, before_v, after_v, first, last, before, after, whole)[None]
 

time: 61.4 us -> 57.1 us (0.930)
  Pallas kernels: 28.7 us -> 34.4 us
  waiting for transfers between devices: 5.75 us -> 1.35 us
  local copies, waits for them, and re-layouts: 3.12 us -> 0.03 us
  starting transfers between devices: 23 us -> 21.2 us
    pallas_call x3 -> x5, Pallas kernels: 22.5 us -> 28.1 us  [the longest x2 15.1 us: remap(): pl.pallas_call(functools.partial(remap_kernel, sources, grid_rows), grid=...]
    ppermute x8, waiting for transfers between devices: 5.75 us -> 1.35 us  [moved(): return lax.ppermute(value, ('comp', 'tile'), pairs)]
    unnamed x18 -> x14, local copies, waits for them, and re-layouts: 2.76 us -> 0.03 us
    ppermute x8, starting transfers between devices: 23 us -> 21.2 us  [moved(): return lax.ppermute(value, ('comp', 'tile'), pairs)]
  transfers between devices with their start and end apart: 8 -> 8, of which waited for: 1 -> 2; matrix products, arithmetic and copies ran while one was open for 1% -> 0% of each run, Pallas kernels for 39% -> 53%
where the time goes in v4:
time: 57.1 us; the launch traced here: 57 us
  Pallas kernels  34.4 us (60%)
  starting transfers between devices  21.2 us (37%)
  waiting for transfers between devices  1.35 us (2%)
    ppermute x8, starting transfers between devices, moved(): return lax.ppermute(value, ('comp', 'tile'), pairs)  21.2 us
    pallas_call x2, Pallas kernels, remap(): pl.pallas_call(functools.partial(remap_kernel, sources, grid_rows), grid=...  15.1 us
    pallas_call x1, Pallas kernels, remap_near(): pl.pallas_call(functools.partial(near_kernel, (source,)), out_shape=jax.S...  6.03 us
    pallas_call x1, Pallas kernels, pack(): pl.pallas_call(pack_kernel, in_specs=[pl.BlockSpec(memory_space=pltpu.HBM...  4.54 us
    pallas_call x1, Pallas kernels, upper_levels(): pl.pallas_call(upper_kernel, grid=(levels - 1,), out_shape=jax.ShapeDtype...  4.42 us
    pallas_call x1, Pallas kernels, edges(): pl.pallas_call(edges_kernel, in_specs=[pl.BlockSpec(memory_space=pltpu.HB...  2.43 us
    pallas_call x1, Pallas kernels, surface_level(): pl.pallas_call(surface_kernel, grid=(1,), out_shape=jax.ShapeDtypeStruct(...  1.87 us
    ppermute x8, waiting for transfers between devices, moved(): return lax.ppermute(value, ('comp', 'tile'), pairs)  1.35 us
  transfers between devices with their start and end apart: 8, of which 2 were waited for; matrix products, arithmetic and copies ran while one was open for 0% of the time, Pallas kernels for 53%

profile of v4, /device:TPU:1, one launch (start us, length us, event | category | flops | bytes accessed | tf_op | source)
XLA Modules:
  0.0 57.0 jit_solution(4632662433304616927)
XLA Ops:
  0.0 0.0 copy-start.2
  0.0 0.0 copy-start.3
  0.0 0.0 copy-start.4
  0.0 2.4 %edges.1 = (f32[56,2,1024]{2,1,0:T(2,128)}, f32[56,2,1024]{2,1,0:T(2,128)}) custom-call(f32[16,4,4,1024]{3,2,1,0:T(4,128)} %bitcast.10, f32[2,4,4,1024]{3,2,1,0:T(4,128)} %bitcast.15), custom_call_target="tpu_custom_call" | custom-call | flops 1000000 | bytes 100000 | tf_op jit(solution)/shard_map/edges/pallas_call | solution.py:96
  2.4 0.0 copy-start
  2.5 2.5 %collective-permute-start.3 = (f32[56,2,1024]{2,1,0:T(2,128)}, f32[56,2,1024]{2,1,0:T(2,128)S(1)}, u32[]{:S(2)}, u32[]{:S(2)}) collective-permute-start(f32[56,2,1024]{2,1,0:T(2,128)} %get-tuple-element.30), channel_id=1, source_target_pairs={{0,1},{1,2},{2,3},{3,4},{4,5},{5,6},{6,7},{7,8},{8,9},{9,10},{10,1... | collective-permute-start | bytes 1376264 | tf_op jit(solution)/shard_map/ppermute | solution.py:26
  5.0 4.5 %pack.1 = (f32[16,2048]{1,0:T(8,128)}, f32[16,2048]{1,0:T(8,128)}, f32[16,2048]{1,0:T(8,128)}, f32[16,2048]{1,0:T(8,128)}) custom-call(f32[16,4,4,1024]{3,2,1,0:T(4,128)} %bitcast.11, s32[4,2048]{1,0:T(4,128)} %bitcast.31, s32[4,2048]{1,0:T(4,128)} %bitcast.32), custom_call_target="tpu_custom_call" | custom-call | flops 1000000 | bytes 100000 | tf_op jit(solution)/shard_map/pack/pallas_call | solution.py:140
  9.5 1.0 %collective-permute-start.4 = (f32[16,2048]{1,0:T(8,128)}, f32[16,2048]{1,0:T(8,128)S(1)}, u32[]{:S(2)}, u32[]{:S(2)}) collective-permute-start(f32[16,2048]{1,0:T(8,128)} %get-tuple-element.32), channel_id=1, source_target_pairs={{0,64},{1,65},{2,66},{3,67},{4,68},{5,69},{6,70},{7,71},{8,72},{9,... | collective-permute-start | bytes 393224 | tf_op jit(solution)/shard_map/ppermute | solution.py:26
  10.6 1.6 %collective-permute-start = (f32[16,2048]{1,0:T(8,128)}, f32[16,2048]{1,0:T(8,128)S(1)}, u32[]{:S(2)}, u32[]{:S(2)}) collective-permute-start(f32[16,2048]{1,0:T(8,128)} %get-tuple-element.27), channel_id=1, source_target_pairs={{0,65},{1,66},{2,67},{3,68},{4,69},{5,70},{6,71},{7,72},{8,73},{9,... | collective-permute-start | bytes 393224 | tf_op jit(solution)/shard_map/ppermute | solution.py:26
  12.2 5.6 %collective-permute-start.1 = (f32[16,2048]{1,0:T(8,128)}, f32[16,2048]{1,0:T(8,128)S(1)}, u32[]{:S(2)}, u32[]{:S(2)}) collective-permute-start(f32[16,2048]{1,0:T(8,128)} %get-tuple-element.28), channel_id=1, source_target_pairs={{0,127},{1,64},{2,65},{3,66},{4,67},{5,68},{6,69},{7,70},{8,71},{9... | collective-permute-start | bytes 393224 | tf_op jit(solution)/shard_map/ppermute | solution.py:26
  17.8 2.5 %collective-permute-start.2 = (f32[16,2048]{1,0:T(8,128)}, f32[16,2048]{1,0:T(8,128)S(1)}, u32[]{:S(2)}, u32[]{:S(2)}) collective-permute-start(f32[16,2048]{1,0:T(8,128)} %get-tuple-element.29), channel_id=1, source_target_pairs={{0,126},{1,127},{2,64},{3,65},{4,66},{5,67},{6,68},{7,69},{8,70},{... | collective-permute-start | bytes 393224 | tf_op jit(solution)/shard_map/ppermute | solution.py:26
  20.2 0.0 collective-permute-done.4.piece
  20.2 0.7 %collective-permute-start.6 = (f32[56,2,1024]{2,1,0:T(2,128)}, f32[56,2,1024]{2,1,0:T(2,128)S(1)}, u32[]{:S(2)}, u32[]{:S(2)}) collective-permute-start(f32[56,2,1024]{2,1,0:T(2,128)} %get-tuple-element.37), channel_id=1, source_target_pairs={{0,63},{1,0},{2,1},{3,2},{4,3},{5,4},{6,5},{7,6},{8,7},{9,8},{10,9... | collective-permute-start | bytes 1376264 | tf_op jit(solution)/shard_map/ppermute | solution.py:26
  21.0 0.0 copy-done.2
  21.0 0.0 copy-done.3
  21.0 0.0 copy-done.4
  21.0 0.0 copy-start.5
  21.0 0.0 copy-start.6
  21.0 6.0 %remap_near.1.partial = f32[16,4,1024]{2,1,0:T(4,128)S(1)} custom-call(s32[8,4,1024]{2,1,0:T(4,128)S(1)} %bitcast.18, s32[8,4,1024]{2,1,0:T(4,128)S(1)} %bitcast.21, f32[8,4,1024]{2,1,0:T(4,128)S(1)} %bitcast.24, f32[16,2048]{1,0:T(8,128)S(1)} %collective-permute-done.4.piece), custom_call_target="tpu_custom_call" | custom-call | flops 1000000 | bytes 100000 | tf_op jit(solution)/shard_map/remap_near/pallas_call | solution.py:203
  27.0 0.9 %collective-permute-done.rest_0_ = f32[16,2048]{1,0:T(8,128)S(1)} collective-permute-done((f32[16,2048]{1,0:T(8,128)}, f32[16,2048]{1,0:T(8,128)S(1)}, u32[]{:S(2)}, u32[]{:S(2)}) %collective-permute-start) | collective-permute-done | bytes 131104 | tf_op jit(solution)/shard_map/ppermute | solution.py:26
  27.9 0.0 collective-permute-done.1.rest_1_
  27.9 0.5 collective-permute-done.2.rest_2_
  28.4 0.0 collective-permute-done.3.before_v
  28.4 0.0 copy-done
  28.4 0.0 copy-done.5
  28.4 0.0 copy-done.6
  28.4 7.5 %remap.2.last = f32[16,2,1024]{2,1,0:T(2,128)S(1)} custom-call(s32[8,4,1024]{2,1,0:T(4,128)S(1)} %bitcast.19, s32[8,4,1024]{2,1,0:T(4,128)S(1)} %bitcast.22, f32[8,4,1024]{2,1,0:T(4,128)S(1)} %bitcast.25, f32[16,4,4,1024]{3,2,1,0:T(4,128)S(1)} %bitcast.12, f32[16,4,1024]{2,1,0:T(4,128)S(1)} %bitcast.27, s32[4,1024]{1,0:T(4,128)S(1)} %bitcast.29, ...), custom_call_target="tpu_custom_call" | custom-call | flops 15000000512 | bytes 1000000 | tf_op jit(solution)/shard_map/remap/pallas_call | solution.py:236
  35.9 0.0 copy-start.1
  35.9 0.3 collective-permute-start.5
  36.2 7.5 %remap.3.first = f32[16,2,1024]{2,1,0:T(2,128)S(1)} custom-call(s32[8,4,1024]{2,1,0:T(4,128)S(1)} %bitcast.20, s32[8,4,1024]{2,1,0:T(4,128)S(1)} %bitcast.23, f32[8,4,1024]{2,1,0:T(4,128)S(1)} %bitcast.26, f32[16,4,4,1024]{3,2,1,0:T(4,128)S(1)} %bitcast.13, f32[16,4,1024]{2,1,0:T(4,128)S(1)} %bitcast.28, s32[4,1024]{1,0:T(4,128)S(1)} %bitcast.30, ...), custom_call_target="tpu_custom_call" | custom-call | flops 15000000512 | bytes 1000000 | tf_op jit(solution)/shard_map/remap/pallas_call | solution.py:236
  43.7 6.9 %collective-permute-start.7 = (f32[16,2,1024]{2,1,0:T(2,128)S(1)}, f32[16,2,1024]{2,1,0:T(2,128)S(1)}, u32[]{:S(2)}, u32[]{:S(2)}) collective-permute-start(f32[16,2,1024]{2,1,0:T(2,128)S(1)} %remap.3.first), channel_id=1, source_target_pairs={{0,63},{1,0},{2,1},{3,2},{4,3},{5,4},{6,5},{7,6},{8,7},{9,8},{10,9... | collective-permute-start | bytes 393224 | tf_op jit(solution)/shard_map/ppermute | solution.py:26
  50.7 0.0 collective-permute-done.5.before
  50.7 0.0 collective-permute-done.6.after_v
  50.7 0.0 copy-done.1
  50.7 4.4 %upper_levels.1.whole = f32[16,4,4,1024]{3,2,1,0:T(4,128)} custom-call(f32[16,4,4,1024]{3,2,1,0:T(4,128)S(1)} %bitcast.14, f32[56,2,1024]{2,1,0:T(2,128)S(1)} %collective-permute-done.3.before_v, f32[56,2,1024]{2,1,0:T(2,128)S(1)} %collective-permute-done.6.after_v, f32[2,4,4,1024]{3,2,1,0:T(4,128)S(1)} %bitcast.16), custom_call_target="tpu_custom_call" | custom-call | flops 1000000 | bytes 100000 | tf_op jit(solution)/shard_map/upper_levels/pallas_call | solution.py:329
  55.1 0.0 collective-permute-done.7.after
  55.1 1.9 %surface_level.1 = f32[16,4,4,1024]{3,2,1,0:T(4,128)} custom-call(f32[2,4,4,1024]{3,2,1,0:T(4,128)S(1)} %bitcast.17, f32[56,2,1024]{2,1,0:T(2,128)S(1)} %collective-permute-done.3.before_v, f32[56,2,1024]{2,1,0:T(2,128)S(1)} %collective-permute-done.6.after_v, f32[16,2,1024]{2,1,0:T(2,128)S(1)} %remap.3.first, ...), custom_call_target="tpu_custom_call", output_to_operand_aliasing={{}: (7, {})} | custom-call | tf_op jit(solution)/shard_map/surface_level/pallas_call | solution.py:350
Async XLA Ops:
  0.0 21.0 %copy-start.2 = (s32[1,8,4,1024]{3,2,1,0:T(4,128)S(1)}, s32[1,8,4,1024]{3,2,1,0:T(4,128)}, u32[]{:S(2)}) copy-start(s32[1,8,4,1024]{3,2,1,0:T(4,128)} %param.15) | copy-start | bytes 393220
  0.0 21.0 %copy-start.3 = (s32[1,8,4,1024]{3,2,1,0:T(4,128)S(1)}, s32[1,8,4,1024]{3,2,1,0:T(4,128)}, u32[]{:S(2)}) copy-start(s32[1,8,4,1024]{3,2,1,0:T(4,128)} %param.16) | copy-start | bytes 393220
  0.0 21.0 %copy-start.4 = (f32[1,8,4,1024]{3,2,1,0:T(4,128)S(1)}, f32[1,8,4,1024]{3,2,1,0:T(4,128)}, u32[]{:S(2)}) copy-start(f32[1,8,4,1024]{3,2,1,0:T(4,128)} %param.17) | copy-start | bytes 393220
  2.4 25.9 %copy-start = (f32[1,16,4,4,1024]{4,3,2,1,0:T(4,128)S(1)}, f32[1,16,4,4,1024]{4,3,2,1,0:T(4,128)}, u32[]{:S(2)}) copy-start(f32[1,16,4,4,1024]{4,3,2,1,0:T(4,128)} %param.9) | copy-start | bytes 3145732
  2.5 25.9 %collective-permute-start.3 = (f32[56,2,1024]{2,1,0:T(2,128)}, f32[56,2,1024]{2,1,0:T(2,128)S(1)}, u32[]{:S(2)}, u32[]{:S(2)}) collective-permute-start(f32[56,2,1024]{2,1,0:T(2,128)} %get-tuple-element.30), channel_id=1, source_target_pairs={{0,1},{1,2},{2,3},{3,4},{4,5},{5,6},{6,7},{7,8},{8,9},{9,10},{10,1... | collective-permute-start | bytes 1376264 | tf_op jit(solution)/shard_map/ppermute | solution.py:26
  9.5 10.7 %collective-permute-start.4 = (f32[16,2048]{1,0:T(8,128)}, f32[16,2048]{1,0:T(8,128)S(1)}, u32[]{:S(2)}, u32[]{:S(2)}) collective-permute-start(f32[16,2048]{1,0:T(8,128)} %get-tuple-element.32), channel_id=1, source_target_pairs={{0,64},{1,65},{2,66},{3,67},{4,68},{5,69},{6,70},{7,71},{8,72},{9,... | collective-permute-start | bytes 393224 | tf_op jit(solution)/shard_map/ppermute | solution.py:26
  10.6 17.3 %collective-permute-start = (f32[16,2048]{1,0:T(8,128)}, f32[16,2048]{1,0:T(8,128)S(1)}, u32[]{:S(2)}, u32[]{:S(2)}) collective-permute-start(f32[16,2048]{1,0:T(8,128)} %get-tuple-element.27), channel_id=1, source_target_pairs={{0,65},{1,66},{2,67},{3,68},{4,69},{5,70},{6,71},{7,72},{8,73},{9,... | collective-permute-start | bytes 393224 | tf_op jit(solution)/shard_map/ppermute | solution.py:26
  12.2 15.7 %collective-permute-start.1 = (f32[16,2048]{1,0:T(8,128)}, f32[16,2048]{1,0:T(8,128)S(1)}, u32[]{:S(2)}, u32[]{:S(2)}) collective-permute-start(f32[16,2048]{1,0:T(8,128)} %get-tuple-element.28), channel_id=1, source_target_pairs={{0,127},{1,64},{2,65},{3,66},{4,67},{5,68},{6,69},{7,70},{8,71},{9... | collective-permute-start | bytes 393224 | tf_op jit(solution)/shard_map/ppermute | solution.py:26
  17.8 10.6 %collective-permute-start.2 = (f32[16,2048]{1,0:T(8,128)}, f32[16,2048]{1,0:T(8,128)S(1)}, u32[]{:S(2)}, u32[]{:S(2)}) collective-permute-start(f32[16,2048]{1,0:T(8,128)} %get-tuple-element.29), channel_id=1, source_target_pairs={{0,126},{1,127},{2,64},{3,65},{4,66},{5,67},{6,68},{7,69},{8,70},{... | collective-permute-start | bytes 393224 | tf_op jit(solution)/shard_map/ppermute | solution.py:26
  20.2 30.5 %collective-permute-start.6 = (f32[56,2,1024]{2,1,0:T(2,128)}, f32[56,2,1024]{2,1,0:T(2,128)S(1)}, u32[]{:S(2)}, u32[]{:S(2)}) collective-permute-start(f32[56,2,1024]{2,1,0:T(2,128)} %get-tuple-element.37), channel_id=1, source_target_pairs={{0,63},{1,0},{2,1},{3,2},{4,3},{5,4},{6,5},{7,6},{8,7},{9,8},{10,9... | collective-permute-start | bytes 1376264 | tf_op jit(solution)/shard_map/ppermute | solution.py:26
  21.0 7.4 %copy-start.5 = (f32[1,16,4,1024]{3,2,1,0:T(4,128)S(1)}, f32[1,16,4,1024]{3,2,1,0:T(4,128)}, u32[]{:S(2)}) copy-start(f32[1,16,4,1024]{3,2,1,0:T(4,128)} %param.11) | copy-start | bytes 786436
  21.0 7.4 %copy-start.6 = (s32[1,4,1024]{2,1,0:T(4,128)S(1)}, s32[1,4,1024]{2,1,0:T(4,128)}, u32[]{:S(2)}) copy-start(s32[1,4,1024]{2,1,0:T(4,128)} %param.12) | copy-start | bytes 49156
  35.9 14.8 %copy-start.1 = (f32[1,2,4,4,1024]{4,3,2,1,0:T(4,128)S(1)}, f32[1,2,4,4,1024]{4,3,2,1,0:T(4,128)}, u32[]{:S(2)}) copy-start(f32[1,2,4,4,1024]{4,3,2,1,0:T(4,128)} %param.10) | copy-start | bytes 393220
  35.9 14.8 %collective-permute-start.5 = (f32[16,2,1024]{2,1,0:T(2,128)S(1)}, f32[16,2,1024]{2,1,0:T(2,128)S(1)}, u32[]{:S(2)}, u32[]{:S(2)}) collective-permute-start(f32[16,2,1024]{2,1,0:T(2,128)S(1)} %remap.2.last), channel_id=1, source_target_pairs={{0,1},{1,2},{2,3},{3,4},{4,5},{5,6},{6,7},{7,8},{8,9},{9,10},{10,1... | collective-permute-start | bytes 393224 | tf_op jit(solution)/shard_map/ppermute | solution.py:26
  43.7 11.4 %collective-permute-start.7 = (f32[16,2,1024]{2,1,0:T(2,128)S(1)}, f32[16,2,1024]{2,1,0:T(2,128)S(1)}, u32[]{:S(2)}, u32[]{:S(2)}) collective-permute-start(f32[16,2,1024]{2,1,0:T(2,128)S(1)} %remap.3.first), channel_id=1, source_target_pairs={{0,63},{1,0},{2,1},{3,2},{4,3},{5,4},{6,5},{7,6},{8,7},{9,8},{10,9... | collective-permute-start | bytes 393224 | tf_op jit(solution)/shard_map/ppermute | solution.py:26

commit v5 on v4

--- a/solution.py
+++ b/solution.py
@@ -9,7 +9,8 @@
 
 diffusion = 0.12
 LOW = 128
-BLOCK = 512
+BLOCK = 1024
+PACK_BLOCK = 512
 UNROLL = 4
 VMEM_LIMIT = 48 * 2**20
 FULL_VMEM = 60 * 2**20
@@ -24,6 +25,12 @@
             target = (comp ^ 1 if swap else comp) * tiles + (tile + steps) % tiles
             pairs.append((comp * tiles + tile, target))
     return lax.ppermute(value, ("comp", "tile"), pairs)
+
+
+def swapped(value, odd_step):
+    tiles = lax.axis_size("tile")
+    pairs = [(tile, (tile + (odd_step if tile % 2 else -odd_step)) % tiles) for tile in range(tiles)]
+    return lax.ppermute(value, "tile", pairs)
 
 
 def put_table(table, tracers, first, count, part):
@@ -109,21 +116,19 @@
 
 
 def pack_kernel(field, rows, cols, *rest):
-    outs, (table, level0, row_list, col_list, sems) = rest[:-5], rest[-5:]
+    outs, table = rest[:-1], rest[-1]
     tracers, _, grid_rows, width = field.shape
-    for copy in started(((field.at[:, 0], level0), (rows, row_list), (cols, col_list)), sems):
-        copy.wait()
     per_row = width // LOW
 
     def part(high):
         low = high % per_row * LOW
-        return level0[:, high // per_row, low : low + LOW]
+        return field[:, 0, high // per_row, low : low + LOW]
 
     put_table(table, tracers, 0, grid_rows * per_row, part)
     for near in range(rows.shape[0]):
-        for start in range(0, rows.shape[1], BLOCK):
-            at = slice(start, start + BLOCK)
-            entry = row_list[near : near + 1, at] * width + col_list[near : near + 1, at]
+        for start in range(0, rows.shape[1], PACK_BLOCK):
+            at = slice(start, start + PACK_BLOCK)
+            entry = rows[near : near + 1, at] * width + cols[near : near + 1, at]
             product = low_product(table, entry, tracers)
             outs[near][:, at] = chosen(product, high_part(entry, tracers))
 
@@ -139,16 +144,12 @@
     piece = jax.ShapeDtypeStruct((tracers, capacity), jnp.float32)
     return pl.pallas_call(
         pack_kernel,
-        in_specs=[pl.BlockSpec(memory_space=pltpu.HBM)] * 3,
+        grid=(1,),
+        in_specs=[level_spec(field), whole_spec(rows.shape), whole_spec(cols.shape)],
+        out_specs=[whole_spec(piece.shape)] * neighbours,
         out_shape=[piece] * neighbours,
-        scratch_shapes=[
-            pltpu.VMEM((grid_rows * width // LOW * tracers, 2 * LOW), jnp.bfloat16),
-            pltpu.VMEM((tracers, grid_rows, width), jnp.float32),
-            pltpu.VMEM(rows.shape, jnp.int32),
-            pltpu.VMEM(cols.shape, jnp.int32),
-            pltpu.SemaphoreType.DMA((3,)),
-        ],
-        compiler_params=pltpu.CompilerParams(vmem_limit_bytes=FULL_VMEM),
+        scratch_shapes=[pltpu.VMEM((grid_rows * width // LOW * tracers, 2 * LOW), jnp.bfloat16)],
+        compiler_params=pltpu.CompilerParams(vmem_limit_bytes=VMEM_LIMIT),
         cost_estimate=SMALL_COST,
         name="pack",
     )(field, rows, cols)
@@ -157,8 +158,8 @@
 def added_reads(sources, near, slot, weight, table, tracers, row, at):
     total = None
     for k in range(near.shape[0]):
-        which = near[k, row : row + 1, at]
-        entry = slot[k, row : row + 1, at]
+        which = near[k, pl.ds(row, 1), at]
+        entry = slot[k, pl.ds(row, 1), at]
         product = low_product(table, entry, tracers)
         high = high_part(entry, tracers)
         count = len(product) // len(sources)
@@ -169,7 +170,7 @@
             part = chosen(product[rank * count : (rank + 1) * count], high)
             read = jnp.where(wide == sources[rank], part, read)
             inside = inside | (which == sources[rank])
-        term = jnp.where(inside, weight[k, row : row + 1, at], 0.0) * read
+        term = jnp.where(inside, weight[k, pl.ds(row, 1), at], 0.0) * read
         total = term if total is None else total + term
     return total
 
@@ -210,31 +211,33 @@
     )(near, slot, weight, piece)
 
 
-def remap_kernel(sources, grid_rows, near, slot, weight, field, coupling, mask, partial, *rest):
+def remap_kernel(sources, start, near, slot, weight, field, coupling, mask, partial, *rest):
     pieces, (out, table) = rest[:-2], rest[-2:]
     tracers = field.shape[0]
     put_pieces(table, pieces)
-    for place, row in enumerate(grid_rows):
+    for place in range(out.shape[1]):
+        row = start[0] + place
 
         def body(step, carry, place=place, row=row):
             at = pl.ds(pl.multiple_of(step * BLOCK, BLOCK), BLOCK)
             total = added_reads(sources, near, slot, weight, table, tracers, row, at)
             total = total + partial[:, row, at]
             own = field[:, 0, row, at]
-            wet = mask[row : row + 1, at].astype(jnp.float32)
+            wet = mask[pl.ds(row, 1), at].astype(jnp.float32)
             out[:, place, at] = own + coupling[:, row, at] * wet * (total - own)
             return carry
 
         lax.fori_loop(0, field.shape[3] // BLOCK, body, 0)
 
 
-def remap(sources, grid_rows, pieces, near, slot, weight, field, coupling, mask, partial):
+def remap(sources, start, pieces, near, slot, weight, field, coupling, mask, partial):
     tracers, capacity = pieces[0].shape
-    out = (tracers, len(grid_rows), field.shape[3])
+    out = (tracers, 2, field.shape[3])
     specs = [whole_spec(v.shape) for v in (near, slot, weight, coupling, mask, partial, *pieces)]
     specs.insert(3, level_spec(field))
-    return pl.pallas_call(
-        functools.partial(remap_kernel, sources, grid_rows),
+    specs.insert(0, pl.BlockSpec(memory_space=pltpu.SMEM))
+    return pl.pallas_call(
+        functools.partial(remap_kernel, sources),
         grid=(1,),
         in_specs=specs,
         out_specs=whole_spec(out),
@@ -243,7 +246,7 @@
         compiler_params=pltpu.CompilerParams(vmem_limit_bytes=VMEM_LIMIT),
         cost_estimate=pl.CostEstimate(flops=15 * 10**9, bytes_accessed=10**6, transcendentals=0),
         name="remap",
-    )(near, slot, weight, field, coupling, mask, partial, *pieces)
+    )(start, near, slot, weight, field, coupling, mask, partial, *pieces)
 
 
 def set_factors(factors, speed_x, speed_y):
@@ -298,9 +301,10 @@
     transported(tracers, factors, padded, store)
 
 
-def surface_kernel(velocity, before_v, after_v, first, last, before, after, whole, out, factors):
+def surface_kernel(start, velocity, before_v, after_v, own1, own2, got1, got2, whole, out, factors):
     del whole
-    tracers = first.shape[0]
+    tracers = own1.shape[0]
+    odd = start[0] > 0
     levels = velocity.shape[1]
     speeds = []
     for which in range(2):
@@ -311,7 +315,11 @@
     set_factors(factors, *speeds)
 
     def padded(tracer):
-        return jnp.concatenate([first[tracer], last[tracer], after[tracer], before[tracer]], axis=0)
+        one, two = own1[tracer], own2[tracer]
+        far1, far2 = got1[tracer], got2[tracer]
+        first, last = jnp.where(odd, two, one), jnp.where(odd, one, two)
+        after, before = jnp.where(odd, far1, far2), jnp.where(odd, far2, far1)
+        return jnp.concatenate([first, last, after, before], axis=0)
 
     def store(tracer, value):
         out[tracer, 0] = value
@@ -344,20 +352,22 @@
     )(field, before, after, velocity)
 
 
-def surface_level(velocity, before_v, after_v, first, last, before, after, whole):
+def surface_level(start, velocity, before_v, after_v, own1, own2, got1, got2, whole):
     tracers, _, rows, width = whole.shape
-    values = (velocity, before_v, after_v, first, last, before, after)
+    values = (velocity, before_v, after_v, own1, own2, got1, got2)
     return pl.pallas_call(
         surface_kernel,
         grid=(1,),
         out_shape=jax.ShapeDtypeStruct(whole.shape, jnp.float32),
-        in_specs=[whole_spec(v.shape) for v in values] + [pl.BlockSpec(memory_space=pl.ANY)],
+        in_specs=[pl.BlockSpec(memory_space=pltpu.SMEM)]
+        + [whole_spec(v.shape) for v in values]
+        + [pl.BlockSpec(memory_space=pl.ANY)],
         out_specs=pl.BlockSpec((tracers, 1, rows, width), lambda _: (0, 0, 0, 0)),
-        input_output_aliases={len(values): 0},
+        input_output_aliases={len(values) + 1: 0},
         scratch_shapes=[pltpu.VMEM((4, 8, width), jnp.float32)],
         compiler_params=pltpu.CompilerParams(vmem_limit_bytes=VMEM_LIMIT),
         name="surface_level",
-    )(*values, whole)
+    )(start, *values, whole)
 
 
 def per_device(
@@ -385,14 +395,16 @@
     partial = remap_near(1, near, slot, weight, pieces[1])
     pieces, before_v = lax.optimization_barrier(([pieces[j] for j in others], before_v))
     shared = (near, slot, weight, field, coupling[0], sea_mask[0], partial)
-    last = remap(others, (2, 3), pieces, *shared)
-    before = moved(last, 1, False)
-    pieces, last = lax.optimization_barrier((pieces, last))
-    first = remap(others, (0, 1), pieces, *shared)
-    after = moved(first, -1, False)
-    before_v, before = lax.optimization_barrier((before_v, before))
+    odd = lax.axis_index("tile") & 1
+    start1, start2 = (2 * odd).reshape(1), (2 - 2 * odd).reshape(1)
+    own1 = remap(others, start1, pieces, *shared)
+    got1 = swapped(own1, 1)
+    pieces, own1 = lax.optimization_barrier((pieces, own1))
+    own2 = remap(others, start2, pieces, *shared)
+    got2 = swapped(own2, -1)
+    before_v, got1 = lax.optimization_barrier((before_v, got1))
     whole = upper_levels(field, before_v, after_v, speed)
-    return surface_level(speed, before_v, after_v, first, last, before, after, whole)[None]
+    return surface_level(start1, speed, before_v, after_v, own1, own2, got1, got2, whole)[None]
 
 
 def solution(mesh):

time: 57.1 us -> 52.3 us (0.916)
  starting transfers between devices: 21.2 us -> 15.6 us
  waiting for transfers between devices: 1.35 us -> 6.34 us
  Pallas kernels: 34.4 us -> 30.1 us
    ppermute x8 -> x6, starting transfers between devices: 21.2 us -> 14 us  [moved(): return lax.ppermute(value, ('comp', 'tile'), pairs)]
    pallas_call x3, Pallas kernels: 19.6 us -> 16.6 us  [the longest x2 13.7 us: remap(): pl.pallas_call(functools.partial(remap_kernel, sources), grid=(1,), in_sp...]
    ppermute x8 -> x6, waiting for transfers between devices: 1.35 us -> 4.32 us  [moved(): return lax.ppermute(value, ('comp', 'tile'), pairs)]
    ppermute x0 -> x2, waiting for transfers between devices: none -> 2.02 us  [swapped(): return lax.ppermute(value, 'tile', pairs)]
    ppermute x0 -> x2, starting transfers between devices: none -> 1.63 us  [swapped(): return lax.ppermute(value, 'tile', pairs)]
    pallas_call x1, Pallas kernels: 6.03 us -> 4.67 us  [remap_near(): pl.pallas_call(functools.partial(near_kernel, (source,)), out_shape=jax.S...]
  transfers between devices with their start and end apart: 8 -> 8, of which waited for: 2 -> 3; matrix products, arithmetic and copies ran while one was open for 0% -> 0% of each run, Pallas kernels for 53% -> 49%
where the time goes in v5:
time: 52.3 us; the launch traced here: 52.2 us
  Pallas kernels  30.1 us (58%)
  starting transfers between devices  15.6 us (30%)
  waiting for transfers between devices  6.34 us (12%)
    ppermute x6, starting transfers between devices, moved(): return lax.ppermute(value, ('comp', 'tile'), pairs)  14 us
    pallas_call x2, Pallas kernels, remap(): pl.pallas_call(functools.partial(remap_kernel, sources), grid=(1,), in_sp...  13.7 us
    pallas_call x1, Pallas kernels, remap_near(): pl.pallas_call(functools.partial(near_kernel, (source,)), out_shape=jax.S...  4.67 us
    pallas_call x1, Pallas kernels, upper_levels(): pl.pallas_call(upper_kernel, grid=(levels - 1,), out_shape=jax.ShapeDtype...  4.42 us
    ppermute x6, waiting for transfers between devices, moved(): return lax.ppermute(value, ('comp', 'tile'), pairs)  4.32 us
    pallas_call x1, Pallas kernels, pack(): pl.pallas_call(pack_kernel, grid=(1,), in_specs=[level_spec(field), whole...  2.91 us
    pallas_call x1, Pallas kernels, edges(): pl.pallas_call(edges_kernel, in_specs=[pl.BlockSpec(memory_space=pltpu.HB...  2.47 us
    ppermute x2, waiting for transfers between devices, swapped(): return lax.ppermute(value, 'tile', pairs)  2.02 us
  transfers between devices with their start and end apart: 8, of which 3 were waited for; matrix products, arithmetic and copies ran while one was open for 0% of the time, Pallas kernels for 49%

profile of v5, /device:TPU:1, one launch (start us, length us, event | category | flops | bytes accessed | tf_op | source)
XLA Modules:
  0.0 52.2 jit_solution(15482272795666949211)
XLA Ops:
  0.0 0.0 copy-start
  0.0 0.0 copy-start.5
  0.0 0.0 copy-start.6
  0.0 2.5 %edges.1 = (f32[56,2,1024]{2,1,0:T(2,128)}, f32[56,2,1024]{2,1,0:T(2,128)}) custom-call(f32[16,4,4,1024]{3,2,1,0:T(4,128)} %bitcast.12, f32[2,4,4,1024]{3,2,1,0:T(4,128)} %bitcast.17), custom_call_target="tpu_custom_call" | custom-call | flops 1000000 | bytes 100000 | tf_op jit(solution)/shard_map/edges/pallas_call | solution.py:103
  2.5 0.0 copy-start.9
  2.5 0.0 copy-start.2
  2.5 0.0 copy-start.3
  2.5 0.0 copy-start.4
  2.5 2.5 %collective-permute-start.3 = (f32[56,2,1024]{2,1,0:T(2,128)}, f32[56,2,1024]{2,1,0:T(2,128)S(1)}, u32[]{:S(2)}, u32[]{:S(2)}) collective-permute-start(f32[56,2,1024]{2,1,0:T(2,128)} %get-tuple-element.30), channel_id=1, source_target_pairs={{0,1},{1,2},{2,3},{3,4},{4,5},{5,6},{6,7},{7,8},{8,9},{9,10},{10,1... | collective-permute-start | bytes 1376264 | tf_op jit(solution)/shard_map/ppermute | solution.py:27
  5.1 0.0 copy-done
  5.1 0.0 copy-done.5
  5.1 0.0 copy-done.6
  5.1 2.9 %pack.1 = (f32[16,2048]{1,0:T(8,128)S(1)}, f32[16,2048]{1,0:T(8,128)S(1)}, f32[16,2048]{1,0:T(8,128)S(1)}, f32[16,2048]{1,0:T(8,128)S(1)}) custom-call(f32[16,4,4,1024]{3,2,1,0:T(4,128)S(1)} %bitcast.13, s32[4,2048]{1,0:T(4,128)S(1)} %bitcast.29, s32[4,2048]{1,0:T(4,128)S(1)} %bitcast.30), custom_call_target="tpu_custom_call" | custom-call | flops 1000000 | bytes 100000 | tf_op jit(solution)/shard_map/pack/pallas_call | solution.py:145
  8.0 1.0 %collective-permute-start.4 = (f32[16,2048]{1,0:T(8,128)S(1)}, f32[16,2048]{1,0:T(8,128)S(1)}, u32[]{:S(2)}, u32[]{:S(2)}) collective-permute-start(f32[16,2048]{1,0:T(8,128)S(1)} %get-tuple-element.32), channel_id=1, source_target_pairs={{0,64},{1,65},{2,66},{3,67},{4,68},{5,69},{6,70},{7,71},{8,72},{9,... | collective-permute-start | bytes 393224 | tf_op jit(solution)/shard_map/ppermute | solution.py:27
  9.0 1.6 %collective-permute-start = (f32[16,2048]{1,0:T(8,128)S(1)}, f32[16,2048]{1,0:T(8,128)S(1)}, u32[]{:S(2)}, u32[]{:S(2)}) collective-permute-start(f32[16,2048]{1,0:T(8,128)S(1)} %get-tuple-element.27), channel_id=1, source_target_pairs={{0,65},{1,66},{2,67},{3,68},{4,69},{5,70},{6,71},{7,72},{8,73},{9,... | collective-permute-start | bytes 393224 | tf_op jit(solution)/shard_map/ppermute | solution.py:27
  10.6 5.6 %collective-permute-start.1 = (f32[16,2048]{1,0:T(8,128)S(1)}, f32[16,2048]{1,0:T(8,128)S(1)}, u32[]{:S(2)}, u32[]{:S(2)}) collective-permute-start(f32[16,2048]{1,0:T(8,128)S(1)} %get-tuple-element.28), channel_id=1, source_target_pairs={{0,127},{1,64},{2,65},{3,66},{4,67},{5,68},{6,69},{7,70},{8,71},{9... | collective-permute-start | bytes 393224 | tf_op jit(solution)/shard_map/ppermute | solution.py:27
  16.2 2.5 %collective-permute-start.2 = (f32[16,2048]{1,0:T(8,128)S(1)}, f32[16,2048]{1,0:T(8,128)S(1)}, u32[]{:S(2)}, u32[]{:S(2)}) collective-permute-start(f32[16,2048]{1,0:T(8,128)S(1)} %get-tuple-element.29), channel_id=1, source_target_pairs={{0,126},{1,127},{2,64},{3,65},{4,66},{5,67},{6,68},{7,69},{8,70},{... | collective-permute-start | bytes 393224 | tf_op jit(solution)/shard_map/ppermute | solution.py:27
  18.7 0.0 collective-permute-done.4.piece
  18.7 0.0 copy-done.9
  18.7 0.7 %collective-permute-start.6 = (f32[56,2,1024]{2,1,0:T(2,128)S(1)}, f32[56,2,1024]{2,1,0:T(2,128)S(1)}, u32[]{:S(2)}, u32[]{:S(2)}) collective-permute-start(f32[56,2,1024]{2,1,0:T(2,128)S(1)} %copy-done.9), channel_id=1, source_target_pairs={{0,63},{1,0},{2,1},{3,2},{4,3},{5,4},{6,5},{7,6},{8,7},{9,8},{10,9... | collective-permute-start | bytes 1376264 | tf_op jit(solution)/shard_map/ppermute | solution.py:27
  19.4 0.0 copy-done.2
  19.4 0.0 copy-done.3
  19.4 0.0 copy-done.4
  19.4 0.0 copy-start.7
  19.4 0.0 copy-start.8
  19.5 4.7 %remap_near.1.partial = f32[16,4,1024]{2,1,0:T(4,128)S(1)} custom-call(s32[8,4,1024]{2,1,0:T(4,128)S(1)} %bitcast.20, s32[8,4,1024]{2,1,0:T(4,128)S(1)} %bitcast.23, f32[8,4,1024]{2,1,0:T(4,128)S(1)} %bitcast.26, f32[16,2048]{1,0:T(8,128)S(1)} %collective-permute-done.4.piece), custom_call_target="tpu_custom_call" | custom-call | flops 1000000 | bytes 100000 | tf_op jit(solution)/shard_map/remap_near/pallas_call | solution.py:204
  24.1 4.1 %collective-permute-done.rest_0_ = f32[16,2048]{1,0:T(8,128)S(1)} collective-permute-done((f32[16,2048]{1,0:T(8,128)S(1)}, f32[16,2048]{1,0:T(8,128)S(1)}, u32[]{:S(2)}, u32[]{:S(2)}) %collective-permute-start) | collective-permute-done | bytes 131104 | tf_op jit(solution)/shard_map/ppermute | solution.py:27
  28.2 0.0 collective-permute-done.1.rest_1_
  28.2 0.2 collective-permute-done.2.rest_2_
  28.4 0.0 collective-permute-done.3.before_v
  28.4 0.0 copy-done.7
  28.4 0.0 copy-done.8
  28.5 6.9 %remap.2.own1 = f32[16,2,1024]{2,1,0:T(2,128)S(1)} custom-call(s32[1]{0:T(128)} %bitcast.start, s32[8,4,1024]{2,1,0:T(4,128)S(1)} %bitcast.21, s32[8,4,1024]{2,1,0:T(4,128)S(1)} %bitcast.24, f32[8,4,1024]{2,1,0:T(4,128)S(1)} %bitcast.27, f32[16,4,4,1024]{3,2,1,0:T(4,128)S(1)} %bitcast.14, f32[16,4,1024]{2,1,0:T(4,128)S(1)} %bitcast.31, ...), custom_call_target="tpu_custom_call" | custom-call | flops 15000000512 | bytes 1000000 | tf_op jit(solution)/shard_map/remap/pallas_call | solution.py:239
  35.3 1.5 %collective-permute-start.5 = (f32[16,2,1024]{2,1,0:T(2,128)S(1)}, f32[16,2,1024]{2,1,0:T(2,128)S(1)}, u32[]{:S(2)}, u32[]{:S(2)}) collective-permute-start(f32[16,2,1024]{2,1,0:T(2,128)S(1)} %remap.2.own1), channel_id=1, source_target_pairs={{0,63},{1,2},{2,1},{3,4},{4,3},{5,6},{6,5},{7,8},{8,7},{9,10},{10,... | collective-permute-start | bytes 393224 | tf_op jit(solution)/shard_map/ppermute | solution.py:33
  36.9 0.0 copy-start.1
  36.9 6.9 %remap.3.own2 = f32[16,2,1024]{2,1,0:T(2,128)S(1)} custom-call(s32[1]{0:T(128)} %bitcast.10.start, s32[8,4,1024]{2,1,0:T(4,128)S(1)} %bitcast.22, s32[8,4,1024]{2,1,0:T(4,128)S(1)} %bitcast.25, f32[8,4,1024]{2,1,0:T(4,128)S(1)} %bitcast.28, f32[16,4,4,1024]{3,2,1,0:T(4,128)S(1)} %bitcast.15, f32[16,4,1024]{2,1,0:T(4,128)S(1)} %bitcast.32, ...), custom_call_target="tpu_custom_call" | custom-call | flops 15000000512 | bytes 1000000 | tf_op jit(solution)/shard_map/remap/pallas_call | solution.py:239
  43.7 0.1 collective-permute-start.7
  43.8 2.0 %collective-permute-done.5.got1 = f32[16,2,1024]{2,1,0:T(2,128)S(1)} collective-permute-done((f32[16,2,1024]{2,1,0:T(2,128)S(1)}, f32[16,2,1024]{2,1,0:T(2,128)S(1)}, u32[]{:S(2)}, u32[]{:S(2)}) %collective-permute-start.5) | collective-permute-done | bytes 131104 | tf_op jit(solution)/shard_map/ppermute | solution.py:33
  45.8 0.0 collective-permute-done.6.after_v
  45.8 0.0 copy-done.1
  45.9 4.4 %upper_levels.1.whole = f32[16,4,4,1024]{3,2,1,0:T(4,128)} custom-call(f32[16,4,4,1024]{3,2,1,0:T(4,128)S(1)} %bitcast.16, f32[56,2,1024]{2,1,0:T(2,128)S(1)} %collective-permute-done.3.before_v, f32[56,2,1024]{2,1,0:T(2,128)S(1)} %collective-permute-done.6.after_v, f32[2,4,4,1024]{3,2,1,0:T(4,128)S(1)} %bitcast.18), custom_call_target="tpu_custom_call" | custom-call | flops 1000000 | bytes 100000 | tf_op jit(solution)/shard_map/upper_levels/pallas_call | solution.py:337
  50.3 0.0 collective-permute-done.7.got2
  50.3 1.9 %surface_level.1 = f32[16,4,4,1024]{3,2,1,0:T(4,128)} custom-call(s32[1]{0:T(128)} %bitcast.start, f32[2,4,4,1024]{3,2,1,0:T(4,128)S(1)} %bitcast.19, f32[56,2,1024]{2,1,0:T(2,128)S(1)} %collective-permute-done.3.before_v, f32[56,2,1024]{2,1,0:T(2,128)S(1)} %collective-permute-done.6.after_v, ...), custom_call_target="tpu_custom_call", output_to_operand_aliasing={{}: (8, {})} | custom-call | tf_op jit(solution)/shard_map/surface_level/pallas_call | solution.py:358
Async XLA Ops:
  0.0 5.1 %copy-start = (f32[1,16,4,4,1024]{4,3,2,1,0:T(4,128)S(1)}, f32[1,16,4,4,1024]{4,3,2,1,0:T(4,128)}, u32[]{:S(2)}) copy-start(f32[1,16,4,4,1024]{4,3,2,1,0:T(4,128)} %param.9) | copy-start | bytes 3145732
  0.0 5.1 %copy-start.5 = (s32[1,1,4,2048]{3,2,1,0:T(4,128)S(1)}, s32[1,1,4,2048]{3,2,1,0:T(4,128)}, u32[]{:S(2)}) copy-start(s32[1,1,4,2048]{3,2,1,0:T(4,128)} %param.13) | copy-start | bytes 98308
  0.0 5.1 %copy-start.6 = (s32[1,1,4,2048]{3,2,1,0:T(4,128)S(1)}, s32[1,1,4,2048]{3,2,1,0:T(4,128)}, u32[]{:S(2)}) copy-start(s32[1,1,4,2048]{3,2,1,0:T(4,128)} %param.14) | copy-start | bytes 98308
  2.5 16.2 %copy-start.9 = (f32[56,2,1024]{2,1,0:T(2,128)S(1)}, f32[56,2,1024]{2,1,0:T(2,128)}, u32[]{:S(2)}) copy-start(f32[56,2,1024]{2,1,0:T(2,128)} %get-tuple-element.37) | copy-start | bytes 1376260
  2.5 16.9 %copy-start.2 = (s32[1,8,4,1024]{3,2,1,0:T(4,128)S(1)}, s32[1,8,4,1024]{3,2,1,0:T(4,128)}, u32[]{:S(2)}) copy-start(s32[1,8,4,1024]{3,2,1,0:T(4,128)} %param.15) | copy-start | bytes 393220
  2.5 16.9 %copy-start.3 = (s32[1,8,4,1024]{3,2,1,0:T(4,128)S(1)}, s32[1,8,4,1024]{3,2,1,0:T(4,128)}, u32[]{:S(2)}) copy-start(s32[1,8,4,1024]{3,2,1,0:T(4,128)} %param.16) | copy-start | bytes 393220
  2.5 16.9 %copy-start.4 = (f32[1,8,4,1024]{3,2,1,0:T(4,128)S(1)}, f32[1,8,4,1024]{3,2,1,0:T(4,128)}, u32[]{:S(2)}) copy-start(f32[1,8,4,1024]{3,2,1,0:T(4,128)} %param.17) | copy-start | bytes 393220
  2.5 25.9 %collective-permute-start.3 = (f32[56,2,1024]{2,1,0:T(2,128)}, f32[56,2,1024]{2,1,0:T(2,128)S(1)}, u32[]{:S(2)}, u32[]{:S(2)}) collective-permute-start(f32[56,2,1024]{2,1,0:T(2,128)} %get-tuple-element.30), channel_id=1, source_target_pairs={{0,1},{1,2},{2,3},{3,4},{4,5},{5,6},{6,7},{7,8},{8,9},{9,10},{10,1... | collective-permute-start | bytes 1376264 | tf_op jit(solution)/shard_map/ppermute | solution.py:27
  8.0 10.7 %collective-permute-start.4 = (f32[16,2048]{1,0:T(8,128)S(1)}, f32[16,2048]{1,0:T(8,128)S(1)}, u32[]{:S(2)}, u32[]{:S(2)}) collective-permute-start(f32[16,2048]{1,0:T(8,128)S(1)} %get-tuple-element.32), channel_id=1, source_target_pairs={{0,64},{1,65},{2,66},{3,67},{4,68},{5,69},{6,70},{7,71},{8,72},{9,... | collective-permute-start | bytes 393224 | tf_op jit(solution)/shard_map/ppermute | solution.py:27
  9.0 19.2 %collective-permute-start = (f32[16,2048]{1,0:T(8,128)S(1)}, f32[16,2048]{1,0:T(8,128)S(1)}, u32[]{:S(2)}, u32[]{:S(2)}) collective-permute-start(f32[16,2048]{1,0:T(8,128)S(1)} %get-tuple-element.27), channel_id=1, source_target_pairs={{0,65},{1,66},{2,67},{3,68},{4,69},{5,70},{6,71},{7,72},{8,73},{9,... | collective-permute-start | bytes 393224 | tf_op jit(solution)/shard_map/ppermute | solution.py:27
  10.6 17.6 %collective-permute-start.1 = (f32[16,2048]{1,0:T(8,128)S(1)}, f32[16,2048]{1,0:T(8,128)S(1)}, u32[]{:S(2)}, u32[]{:S(2)}) collective-permute-start(f32[16,2048]{1,0:T(8,128)S(1)} %get-tuple-element.28), channel_id=1, source_target_pairs={{0,127},{1,64},{2,65},{3,66},{4,67},{5,68},{6,69},{7,70},{8,71},{9... | collective-permute-start | bytes 393224 | tf_op jit(solution)/shard_map/ppermute | solution.py:27
  16.2 12.2 %collective-permute-start.2 = (f32[16,2048]{1,0:T(8,128)S(1)}, f32[16,2048]{1,0:T(8,128)S(1)}, u32[]{:S(2)}, u32[]{:S(2)}) collective-permute-start(f32[16,2048]{1,0:T(8,128)S(1)} %get-tuple-element.29), channel_id=1, source_target_pairs={{0,126},{1,127},{2,64},{3,65},{4,66},{5,67},{6,68},{7,69},{8,70},{... | collective-permute-start | bytes 393224 | tf_op jit(solution)/shard_map/ppermute | solution.py:27
  18.7 27.1 %collective-permute-start.6 = (f32[56,2,1024]{2,1,0:T(2,128)S(1)}, f32[56,2,1024]{2,1,0:T(2,128)S(1)}, u32[]{:S(2)}, u32[]{:S(2)}) collective-permute-start(f32[56,2,1024]{2,1,0:T(2,128)S(1)} %copy-done.9), channel_id=1, source_target_pairs={{0,63},{1,0},{2,1},{3,2},{4,3},{5,4},{6,5},{7,6},{8,7},{9,8},{10,9... | collective-permute-start | bytes 1376264 | tf_op jit(solution)/shard_map/ppermute | solution.py:27
  19.4 9.0 %copy-start.7 = (f32[1,16,4,1024]{3,2,1,0:T(4,128)S(1)}, f32[1,16,4,1024]{3,2,1,0:T(4,128)}, u32[]{:S(2)}) copy-start(f32[1,16,4,1024]{3,2,1,0:T(4,128)} %param.11) | copy-start | bytes 786436
  19.4 9.0 %copy-start.8 = (s32[1,4,1024]{2,1,0:T(4,128)S(1)}, s32[1,4,1024]{2,1,0:T(4,128)}, u32[]{:S(2)}) copy-start(s32[1,4,1024]{2,1,0:T(4,128)} %param.12) | copy-start | bytes 49156
  35.3 10.5 %collective-permute-start.5 = (f32[16,2,1024]{2,1,0:T(2,128)S(1)}, f32[16,2,1024]{2,1,0:T(2,128)S(1)}, u32[]{:S(2)}, u32[]{:S(2)}) collective-permute-start(f32[16,2,1024]{2,1,0:T(2,128)S(1)} %remap.2.own1), channel_id=1, source_target_pairs={{0,63},{1,2},{2,1},{3,4},{4,3},{5,6},{6,5},{7,8},{8,7},{9,10},{10,... | collective-permute-start | bytes 393224 | tf_op jit(solution)/shard_map/ppermute | solution.py:33
  36.9 9.0 %copy-start.1 = (f32[1,2,4,4,1024]{4,3,2,1,0:T(4,128)S(1)}, f32[1,2,4,4,1024]{4,3,2,1,0:T(4,128)}, u32[]{:S(2)}) copy-start(f32[1,2,4,4,1024]{4,3,2,1,0:T(4,128)} %param.10) | copy-start | bytes 393220
  43.7 6.5 %collective-permute-start.7 = (f32[16,2,1024]{2,1,0:T(2,128)S(1)}, f32[16,2,1024]{2,1,0:T(2,128)S(1)}, u32[]{:S(2)}, u32[]{:S(2)}) collective-permute-start(f32[16,2,1024]{2,1,0:T(2,128)S(1)} %remap.3.own2), channel_id=1, source_target_pairs={{0,1},{1,0},{2,3},{3,2},{4,5},{5,4},{6,7},{7,6},{8,9},{9,8},{10,11... | collective-permute-start | bytes 393224 | tf_op jit(solution)/shard_map/ppermute | solution.py:33

commit v6 on v5

--- a/solution.py
+++ b/solution.py
@@ -11,7 +11,6 @@
 LOW = 128
 BLOCK = 1024
 PACK_BLOCK = 512
-UNROLL = 4
 VMEM_LIMIT = 48 * 2**20
 FULL_VMEM = 60 * 2**20
 SMALL_COST = pl.CostEstimate(flops=10**6, bytes_accessed=10**5, transcendentals=0)
@@ -87,14 +86,10 @@
             after_v[at] = moving[which, level, :2]
             before_v[at] = moving[which, level, grid_rows - 2 :]
 
-    def body(tracer, carry):
-        for level in range(levels - 1):
-            at = (levels - 1) * tracer + level
-            after_v[at] = upper[tracer, level, :2]
-            before_v[at] = upper[tracer, level, grid_rows - 2 :]
-        return carry
-
-    lax.fori_loop(0, tracers, body, 0, unroll=4)
+    for level in range(levels - 1):
+        at = slice(level * tracers, (level + 1) * tracers)
+        after_v[at] = upper[:, level, :2]
+        before_v[at] = upper[:, level, grid_rows - 2 :]
 
 
 def edges(field, speed):
@@ -249,82 +244,68 @@
     )(start, near, slot, weight, field, coupling, mask, partial, *pieces)
 
 
-def set_factors(factors, speed_x, speed_y):
-    factors[0] = diffusion - 0.5 * speed_x
-    factors[1] = diffusion + 0.5 * speed_x
-    factors[2] = diffusion - 0.5 * speed_y
-    factors[3] = diffusion + 0.5 * speed_y
-
-
-def substep(field, factors):
-    rows, width = field.shape
-    east = pltpu.roll(field, rows - 1, axis=0)
-    west = pltpu.roll(field, 1, axis=0)
+def substep(west, field, east, speed_x, speed_y):
+    width = field.shape[1]
     north = pltpu.roll(field, width - 1, axis=1)
     south = pltpu.roll(field, 1, axis=1)
     return (
         (1 - 4 * diffusion) * field
-        + (factors[0] * east + factors[1] * west)
-        + (factors[2] * north + factors[3] * south)
+        + ((diffusion - 0.5 * speed_x) * east + (diffusion + 0.5 * speed_x) * west)
+        + ((diffusion - 0.5 * speed_y) * north + (diffusion + 0.5 * speed_y) * south)
     )
 
 
-def transported(tracers, factors, padded, store):
-    def body(step, carry):
-        for offset in range(UNROLL):
-            tracer = step * UNROLL + offset
-            store(tracer, substep(substep(padded(tracer), factors), factors)[:4])
-        return carry
-
-    lax.fori_loop(0, tracers // UNROLL, body, 0)
-
-
-def upper_kernel(field, before_v, after_v, velocity, out, factors):
+def transported(rows, speeds):
+    for _ in range(2):
+        rows = [substep(*rows[i - 1 : i + 2], *speeds[i - 1]) for i in range(1, len(rows) - 1)]
+        speeds = speeds[1:-1]
+    return rows
+
+
+def speed_rows(velocity, before_v, after_v, level, tracers):
+    levels, grid_rows = velocity.shape[1:3]
+    pairs = []
+    for row in range(-1, grid_rows + 1):
+        pair = []
+        for which in range(2):
+            at = (levels - 1) * tracers + which * levels + level
+            if row < 0:
+                pair.append(before_v[at, 1:])
+            elif row < grid_rows:
+                pair.append(velocity[which, level, row : row + 1])
+            else:
+                pair.append(after_v[at, :1])
+        pairs.append(pair)
+    return pairs
+
+
+def upper_kernel(field, before_v, after_v, velocity, out):
     level = pl.program_id(0)
-    tracers = field.shape[0]
-    levels = velocity.shape[1]
-    speeds = []
-    for which in range(2):
-        at = 3 * tracers + which * levels + 1 + level
-        speeds.append(
-            jnp.concatenate([velocity[which, 1 + level], after_v[at], before_v[at]], axis=0)
-        )
-    set_factors(factors, *speeds)
-
-    def padded(tracer):
-        at = 3 * tracer + level
-        return jnp.concatenate([field[tracer, 0], after_v[at], before_v[at]], axis=0)
-
-    def store(tracer, value):
-        out[tracer, 0] = value
-
-    transported(tracers, factors, padded, store)
-
-
-def surface_kernel(start, velocity, before_v, after_v, own1, own2, got1, got2, whole, out, factors):
+    tracers, _, grid_rows, _ = field.shape
+    at = pl.ds(level * tracers, tracers)
+    rows = [before_v[at, row] for row in range(2)]
+    rows += [field[:, 0, row] for row in range(grid_rows)]
+    rows += [after_v[at, row] for row in range(2)]
+    speeds = speed_rows(velocity, before_v, after_v, level + 1, tracers)
+    for row, value in enumerate(transported(rows, speeds)):
+        out[:, 0, row] = value
+
+
+def surface_kernel(start, velocity, before_v, after_v, own1, own2, got1, got2, whole, out):
     del whole
-    tracers = own1.shape[0]
     odd = start[0] > 0
-    levels = velocity.shape[1]
-    speeds = []
-    for which in range(2):
-        at = 3 * tracers + which * levels
-        speeds.append(
-            jnp.concatenate([velocity[which, 0], after_v[at], before_v[at]], axis=0)
-        )
-    set_factors(factors, *speeds)
-
-    def padded(tracer):
-        one, two = own1[tracer], own2[tracer]
-        far1, far2 = got1[tracer], got2[tracer]
-        first, last = jnp.where(odd, two, one), jnp.where(odd, one, two)
-        after, before = jnp.where(odd, far1, far2), jnp.where(odd, far2, far1)
-        return jnp.concatenate([first, last, after, before], axis=0)
-
-    def store(tracer, value):
-        out[tracer, 0] = value
-
-    transported(tracers, factors, padded, store)
+    first, last = [], []
+    before, after = [], []
+    for row in range(2):
+        one, two = own1[:, row], own2[:, row]
+        far1, far2 = got1[:, row], got2[:, row]
+        first.append(jnp.where(odd, two, one))
+        last.append(jnp.where(odd, one, two))
+        before.append(jnp.where(odd, far2, far1))
+        after.append(jnp.where(odd, far1, far2))
+    speeds = speed_rows(velocity, before_v, after_v, 0, own1.shape[0])
+    for row, value in enumerate(transported(before + first + last + after, speeds)):
+        out[:, 0, row] = value
 
 
 def whole_spec(shape):
@@ -345,7 +326,6 @@
             whole_spec(velocity.shape),
         ],
         out_specs=pl.BlockSpec(block, lambda level: (0, level + 1, 0, 0)),
-        scratch_shapes=[pltpu.VMEM((4, 8, width), jnp.float32)],
         compiler_params=pltpu.CompilerParams(vmem_limit_bytes=VMEM_LIMIT),
         cost_estimate=SMALL_COST,
         name="upper_levels",
@@ -364,7 +344,6 @@
         + [pl.BlockSpec(memory_space=pl.ANY)],
         out_specs=pl.BlockSpec((tracers, 1, rows, width), lambda _: (0, 0, 0, 0)),
         input_output_aliases={len(values) + 1: 0},
-        scratch_shapes=[pltpu.VMEM((4, 8, width), jnp.float32)],
         compiler_params=pltpu.CompilerParams(vmem_limit_bytes=VMEM_LIMIT),
         name="surface_level",
     )(start, *values, whole)

time: 52.3 us -> 49.7 us (0.950)
  Pallas kernels: 30.1 us -> 27.5 us
    pallas_call x1, Pallas kernels: 4.42 us -> 2.49 us  [upper_levels(): pl.pallas_call(upper_kernel, grid=(levels - 1,), out_shape=jax.ShapeDtype...]
    pallas_call x1, Pallas kernels: 1.88 us -> 1.25 us  [surface_level(): pl.pallas_call(surface_kernel, grid=(1,), out_shape=jax.ShapeDtypeStruct(...]
  transfers between devices with their start and end apart: 8 -> 8, of which waited for: 3 -> 3; matrix products, arithmetic and copies ran while one was open for 0% -> 0% of each run, Pallas kernels for 49% -> 48%
where the time goes in v6:
time: 49.7 us; the launch traced here: 49.5 us
  Pallas kernels  27.5 us (55%)
  starting transfers between devices  15.6 us (31%)
  waiting for transfers between devices  6.34 us (13%)
    ppermute x6, starting transfers between devices, moved(): return lax.ppermute(value, ('comp', 'tile'), pairs)  14 us
    pallas_call x2, Pallas kernels, remap(): pl.pallas_call(functools.partial(remap_kernel, sources), grid=(1,), in_sp...  13.7 us
    pallas_call x1, Pallas kernels, remap_near(): pl.pallas_call(functools.partial(near_kernel, (source,)), out_shape=jax.S...  4.67 us
    ppermute x6, waiting for transfers between devices, moved(): return lax.ppermute(value, ('comp', 'tile'), pairs)  4.32 us
    pallas_call x1, Pallas kernels, pack(): pl.pallas_call(pack_kernel, grid=(1,), in_specs=[level_spec(field), whole...  2.92 us
    pallas_call x1, Pallas kernels, upper_levels(): pl.pallas_call(upper_kernel, grid=(levels - 1,), out_shape=jax.ShapeDtype...  2.49 us
    pallas_call x1, Pallas kernels, edges(): pl.pallas_call(edges_kernel, in_specs=[pl.BlockSpec(memory_space=pltpu.HB...  2.42 us
    ppermute x2, waiting for transfers between devices, swapped(): return lax.ppermute(value, 'tile', pairs)  2.02 us
  transfers between devices with their start and end apart: 8, of which 3 were waited for; matrix products, arithmetic and copies ran while one was open for 0% of the time, Pallas kernels for 48%

profile of v6, /device:TPU:1, one launch (start us, length us, event | category | flops | bytes accessed | tf_op | source)
XLA Modules:
  0.0 49.5 jit_solution(15758993178712716917)
XLA Ops:
  0.0 0.0 copy-start
  0.0 0.0 copy-start.5
  0.0 0.0 copy-start.6
  0.0 2.4 %edges.1 = (f32[56,2,1024]{2,1,0:T(2,128)}, f32[56,2,1024]{2,1,0:T(2,128)}) custom-call(f32[16,4,4,1024]{3,2,1,0:T(4,128)} %bitcast.12, f32[2,4,4,1024]{3,2,1,0:T(4,128)} %bitcast.17), custom_call_target="tpu_custom_call" | custom-call | flops 1000000 | bytes 100000 | tf_op jit(solution)/shard_map/edges/pallas_call | solution.py:98
  2.4 0.0 copy-start.9
  2.5 0.0 copy-start.2
  2.5 0.0 copy-start.3
  2.5 0.0 copy-start.4
  2.5 2.5 %collective-permute-start.3 = (f32[56,2,1024]{2,1,0:T(2,128)}, f32[56,2,1024]{2,1,0:T(2,128)S(1)}, u32[]{:S(2)}, u32[]{:S(2)}) collective-permute-start(f32[56,2,1024]{2,1,0:T(2,128)} %get-tuple-element.30), channel_id=1, source_target_pairs={{0,1},{1,2},{2,3},{3,4},{4,5},{5,6},{6,7},{7,8},{8,9},{9,10},{10,1... | collective-permute-start | bytes 1376264 | tf_op jit(solution)/shard_map/ppermute | solution.py:26
  5.0 0.0 copy-done
  5.0 0.0 copy-done.5
  5.0 0.0 copy-done.6
  5.0 2.9 %pack.1 = (f32[16,2048]{1,0:T(8,128)S(1)}, f32[16,2048]{1,0:T(8,128)S(1)}, f32[16,2048]{1,0:T(8,128)S(1)}, f32[16,2048]{1,0:T(8,128)S(1)}) custom-call(f32[16,4,4,1024]{3,2,1,0:T(4,128)S(1)} %bitcast.13, s32[4,2048]{1,0:T(4,128)S(1)} %bitcast.29, s32[4,2048]{1,0:T(4,128)S(1)} %bitcast.30), custom_call_target="tpu_custom_call" | custom-call | flops 1000000 | bytes 100000 | tf_op jit(solution)/shard_map/pack/pallas_call | solution.py:140
  8.0 1.0 %collective-permute-start.4 = (f32[16,2048]{1,0:T(8,128)S(1)}, f32[16,2048]{1,0:T(8,128)S(1)}, u32[]{:S(2)}, u32[]{:S(2)}) collective-permute-start(f32[16,2048]{1,0:T(8,128)S(1)} %get-tuple-element.32), channel_id=1, source_target_pairs={{0,64},{1,65},{2,66},{3,67},{4,68},{5,69},{6,70},{7,71},{8,72},{9,... | collective-permute-start | bytes 393224 | tf_op jit(solution)/shard_map/ppermute | solution.py:26
  9.0 1.6 %collective-permute-start = (f32[16,2048]{1,0:T(8,128)S(1)}, f32[16,2048]{1,0:T(8,128)S(1)}, u32[]{:S(2)}, u32[]{:S(2)}) collective-permute-start(f32[16,2048]{1,0:T(8,128)S(1)} %get-tuple-element.27), channel_id=1, source_target_pairs={{0,65},{1,66},{2,67},{3,68},{4,69},{5,70},{6,71},{7,72},{8,73},{9,... | collective-permute-start | bytes 393224 | tf_op jit(solution)/shard_map/ppermute | solution.py:26
  10.6 5.6 %collective-permute-start.1 = (f32[16,2048]{1,0:T(8,128)S(1)}, f32[16,2048]{1,0:T(8,128)S(1)}, u32[]{:S(2)}, u32[]{:S(2)}) collective-permute-start(f32[16,2048]{1,0:T(8,128)S(1)} %get-tuple-element.28), channel_id=1, source_target_pairs={{0,127},{1,64},{2,65},{3,66},{4,67},{5,68},{6,69},{7,70},{8,71},{9... | collective-permute-start | bytes 393224 | tf_op jit(solution)/shard_map/ppermute | solution.py:26
  16.2 2.5 %collective-permute-start.2 = (f32[16,2048]{1,0:T(8,128)S(1)}, f32[16,2048]{1,0:T(8,128)S(1)}, u32[]{:S(2)}, u32[]{:S(2)}) collective-permute-start(f32[16,2048]{1,0:T(8,128)S(1)} %get-tuple-element.29), channel_id=1, source_target_pairs={{0,126},{1,127},{2,64},{3,65},{4,66},{5,67},{6,68},{7,69},{8,70},{... | collective-permute-start | bytes 393224 | tf_op jit(solution)/shard_map/ppermute | solution.py:26
  18.7 0.0 collective-permute-done.4.piece
  18.7 0.0 copy-done.9
  18.7 0.7 %collective-permute-start.6 = (f32[56,2,1024]{2,1,0:T(2,128)S(1)}, f32[56,2,1024]{2,1,0:T(2,128)S(1)}, u32[]{:S(2)}, u32[]{:S(2)}) collective-permute-start(f32[56,2,1024]{2,1,0:T(2,128)S(1)} %copy-done.9), channel_id=1, source_target_pairs={{0,63},{1,0},{2,1},{3,2},{4,3},{5,4},{6,5},{7,6},{8,7},{9,8},{10,9... | collective-permute-start | bytes 1376264 | tf_op jit(solution)/shard_map/ppermute | solution.py:26
  19.4 0.0 copy-done.2
  19.4 0.0 copy-done.3
  19.4 0.0 copy-done.4
  19.4 0.0 copy-start.7
  19.4 0.0 copy-start.8
  19.4 4.7 %remap_near.1.partial = f32[16,4,1024]{2,1,0:T(4,128)S(1)} custom-call(s32[8,4,1024]{2,1,0:T(4,128)S(1)} %bitcast.20, s32[8,4,1024]{2,1,0:T(4,128)S(1)} %bitcast.23, f32[8,4,1024]{2,1,0:T(4,128)S(1)} %bitcast.26, f32[16,2048]{1,0:T(8,128)S(1)} %collective-permute-done.4.piece), custom_call_target="tpu_custom_call" | custom-call | flops 1000000 | bytes 100000 | tf_op jit(solution)/shard_map/remap_near/pallas_call | solution.py:199
  24.1 4.1 %collective-permute-done.rest_0_ = f32[16,2048]{1,0:T(8,128)S(1)} collective-permute-done((f32[16,2048]{1,0:T(8,128)S(1)}, f32[16,2048]{1,0:T(8,128)S(1)}, u32[]{:S(2)}, u32[]{:S(2)}) %collective-permute-start) | collective-permute-done | bytes 131104 | tf_op jit(solution)/shard_map/ppermute | solution.py:26
  28.2 0.0 collective-permute-done.1.rest_1_
  28.2 0.2 collective-permute-done.2.rest_2_
  28.4 0.0 collective-permute-done.3.before_v
  28.4 0.0 copy-done.7
  28.4 0.0 copy-done.8
  28.4 6.9 %remap.2.own1 = f32[16,2,1024]{2,1,0:T(2,128)S(1)} custom-call(s32[1]{0:T(128)} %bitcast.start, s32[8,4,1024]{2,1,0:T(4,128)S(1)} %bitcast.21, s32[8,4,1024]{2,1,0:T(4,128)S(1)} %bitcast.24, f32[8,4,1024]{2,1,0:T(4,128)S(1)} %bitcast.27, f32[16,4,4,1024]{3,2,1,0:T(4,128)S(1)} %bitcast.14, f32[16,4,1024]{2,1,0:T(4,128)S(1)} %bitcast.31, ...), custom_call_target="tpu_custom_call" | custom-call | flops 15000000512 | bytes 1000000 | tf_op jit(solution)/shard_map/remap/pallas_call | solution.py:234
  35.3 1.5 %collective-permute-start.5 = (f32[16,2,1024]{2,1,0:T(2,128)S(1)}, f32[16,2,1024]{2,1,0:T(2,128)S(1)}, u32[]{:S(2)}, u32[]{:S(2)}) collective-permute-start(f32[16,2,1024]{2,1,0:T(2,128)S(1)} %remap.2.own1), channel_id=1, source_target_pairs={{0,63},{1,2},{2,1},{3,4},{4,3},{5,6},{6,5},{7,8},{8,7},{9,10},{10,... | collective-permute-start | bytes 393224 | tf_op jit(solution)/shard_map/ppermute | solution.py:32
  36.8 0.0 copy-start.1
  36.8 6.9 %remap.3.own2 = f32[16,2,1024]{2,1,0:T(2,128)S(1)} custom-call(s32[1]{0:T(128)} %bitcast.10.start, s32[8,4,1024]{2,1,0:T(4,128)S(1)} %bitcast.22, s32[8,4,1024]{2,1,0:T(4,128)S(1)} %bitcast.25, f32[8,4,1024]{2,1,0:T(4,128)S(1)} %bitcast.28, f32[16,4,4,1024]{3,2,1,0:T(4,128)S(1)} %bitcast.15, f32[16,4,1024]{2,1,0:T(4,128)S(1)} %bitcast.32, ...), custom_call_target="tpu_custom_call" | custom-call | flops 15000000512 | bytes 1000000 | tf_op jit(solution)/shard_map/remap/pallas_call | solution.py:234
  43.7 0.1 collective-permute-start.7
  43.8 2.0 %collective-permute-done.5.got1 = f32[16,2,1024]{2,1,0:T(2,128)S(1)} collective-permute-done((f32[16,2,1024]{2,1,0:T(2,128)S(1)}, f32[16,2,1024]{2,1,0:T(2,128)S(1)}, u32[]{:S(2)}, u32[]{:S(2)}) %collective-permute-start.5) | collective-permute-done | bytes 131104 | tf_op jit(solution)/shard_map/ppermute | solution.py:32
  45.8 0.0 collective-permute-done.6.after_v
  45.8 0.0 copy-done.1
  45.8 2.5 %upper_levels.1.whole = f32[16,4,4,1024]{3,2,1,0:T(4,128)} custom-call(f32[16,4,4,1024]{3,2,1,0:T(4,128)S(1)} %bitcast.16, f32[56,2,1024]{2,1,0:T(2,128)S(1)} %collective-permute-done.3.before_v, f32[56,2,1024]{2,1,0:T(2,128)S(1)} %collective-permute-done.6.after_v, f32[2,4,4,1024]{3,2,1,0:T(4,128)S(1)} %bitcast.18), custom_call_target="tpu_custom_call" | custom-call | flops 1000000 | bytes 100000 | tf_op jit(solution)/shard_map/upper_levels/pallas_call | solution.py:318
  48.3 0.0 collective-permute-done.7.got2
  48.3 1.2 %surface_level.1 = f32[16,4,4,1024]{3,2,1,0:T(4,128)} custom-call(s32[1]{0:T(128)} %bitcast.start, f32[2,4,4,1024]{3,2,1,0:T(4,128)S(1)} %bitcast.19, f32[56,2,1024]{2,1,0:T(2,128)S(1)} %collective-permute-done.3.before_v, f32[56,2,1024]{2,1,0:T(2,128)S(1)} %collective-permute-done.6.after_v, ...), custom_call_target="tpu_custom_call", output_to_operand_aliasing={{}: (8, {})} | custom-call | tf_op jit(solution)/shard_map/surface_level/pallas_call | solution.py:338
Async XLA Ops:
  0.0 5.0 %copy-start = (f32[1,16,4,4,1024]{4,3,2,1,0:T(4,128)S(1)}, f32[1,16,4,4,1024]{4,3,2,1,0:T(4,128)}, u32[]{:S(2)}) copy-start(f32[1,16,4,4,1024]{4,3,2,1,0:T(4,128)} %param.9) | copy-start | bytes 3145732
  0.0 5.0 %copy-start.5 = (s32[1,1,4,2048]{3,2,1,0:T(4,128)S(1)}, s32[1,1,4,2048]{3,2,1,0:T(4,128)}, u32[]{:S(2)}) copy-start(s32[1,1,4,2048]{3,2,1,0:T(4,128)} %param.13) | copy-start | bytes 98308
  0.0 5.0 %copy-start.6 = (s32[1,1,4,2048]{3,2,1,0:T(4,128)S(1)}, s32[1,1,4,2048]{3,2,1,0:T(4,128)}, u32[]{:S(2)}) copy-start(s32[1,1,4,2048]{3,2,1,0:T(4,128)} %param.14) | copy-start | bytes 98308
  2.4 16.2 %copy-start.9 = (f32[56,2,1024]{2,1,0:T(2,128)S(1)}, f32[56,2,1024]{2,1,0:T(2,128)}, u32[]{:S(2)}) copy-start(f32[56,2,1024]{2,1,0:T(2,128)} %get-tuple-element.37) | copy-start | bytes 1376260
  2.5 16.9 %copy-start.2 = (s32[1,8,4,1024]{3,2,1,0:T(4,128)S(1)}, s32[1,8,4,1024]{3,2,1,0:T(4,128)}, u32[]{:S(2)}) copy-start(s32[1,8,4,1024]{3,2,1,0:T(4,128)} %param.15) | copy-start | bytes 393220
  2.5 16.9 %copy-start.3 = (s32[1,8,4,1024]{3,2,1,0:T(4,128)S(1)}, s32[1,8,4,1024]{3,2,1,0:T(4,128)}, u32[]{:S(2)}) copy-start(s32[1,8,4,1024]{3,2,1,0:T(4,128)} %param.16) | copy-start | bytes 393220
  2.5 16.9 %copy-start.4 = (f32[1,8,4,1024]{3,2,1,0:T(4,128)S(1)}, f32[1,8,4,1024]{3,2,1,0:T(4,128)}, u32[]{:S(2)}) copy-start(f32[1,8,4,1024]{3,2,1,0:T(4,128)} %param.17) | copy-start | bytes 393220
  2.5 25.9 %collective-permute-start.3 = (f32[56,2,1024]{2,1,0:T(2,128)}, f32[56,2,1024]{2,1,0:T(2,128)S(1)}, u32[]{:S(2)}, u32[]{:S(2)}) collective-permute-start(f32[56,2,1024]{2,1,0:T(2,128)} %get-tuple-element.30), channel_id=1, source_target_pairs={{0,1},{1,2},{2,3},{3,4},{4,5},{5,6},{6,7},{7,8},{8,9},{9,10},{10,1... | collective-permute-start | bytes 1376264 | tf_op jit(solution)/shard_map/ppermute | solution.py:26
  8.0 10.7 %collective-permute-start.4 = (f32[16,2048]{1,0:T(8,128)S(1)}, f32[16,2048]{1,0:T(8,128)S(1)}, u32[]{:S(2)}, u32[]{:S(2)}) collective-permute-start(f32[16,2048]{1,0:T(8,128)S(1)} %get-tuple-element.32), channel_id=1, source_target_pairs={{0,64},{1,65},{2,66},{3,67},{4,68},{5,69},{6,70},{7,71},{8,72},{9,... | collective-permute-start | bytes 393224 | tf_op jit(solution)/shard_map/ppermute | solution.py:26
  9.0 19.2 %collective-permute-start = (f32[16,2048]{1,0:T(8,128)S(1)}, f32[16,2048]{1,0:T(8,128)S(1)}, u32[]{:S(2)}, u32[]{:S(2)}) collective-permute-start(f32[16,2048]{1,0:T(8,128)S(1)} %get-tuple-element.27), channel_id=1, source_target_pairs={{0,65},{1,66},{2,67},{3,68},{4,69},{5,70},{6,71},{7,72},{8,73},{9,... | collective-permute-start | bytes 393224 | tf_op jit(solution)/shard_map/ppermute | solution.py:26
  10.6 17.6 %collective-permute-start.1 = (f32[16,2048]{1,0:T(8,128)S(1)}, f32[16,2048]{1,0:T(8,128)S(1)}, u32[]{:S(2)}, u32[]{:S(2)}) collective-permute-start(f32[16,2048]{1,0:T(8,128)S(1)} %get-tuple-element.28), channel_id=1, source_target_pairs={{0,127},{1,64},{2,65},{3,66},{4,67},{5,68},{6,69},{7,70},{8,71},{9... | collective-permute-start | bytes 393224 | tf_op jit(solution)/shard_map/ppermute | solution.py:26
  16.2 12.2 %collective-permute-start.2 = (f32[16,2048]{1,0:T(8,128)S(1)}, f32[16,2048]{1,0:T(8,128)S(1)}, u32[]{:S(2)}, u32[]{:S(2)}) collective-permute-start(f32[16,2048]{1,0:T(8,128)S(1)} %get-tuple-element.29), channel_id=1, source_target_pairs={{0,126},{1,127},{2,64},{3,65},{4,66},{5,67},{6,68},{7,69},{8,70},{... | collective-permute-start | bytes 393224 | tf_op jit(solution)/shard_map/ppermute | solution.py:26
  18.7 27.1 %collective-permute-start.6 = (f32[56,2,1024]{2,1,0:T(2,128)S(1)}, f32[56,2,1024]{2,1,0:T(2,128)S(1)}, u32[]{:S(2)}, u32[]{:S(2)}) collective-permute-start(f32[56,2,1024]{2,1,0:T(2,128)S(1)} %copy-done.9), channel_id=1, source_target_pairs={{0,63},{1,0},{2,1},{3,2},{4,3},{5,4},{6,5},{7,6},{8,7},{9,8},{10,9... | collective-permute-start | bytes 1376264 | tf_op jit(solution)/shard_map/ppermute | solution.py:26
  19.4 9.0 %copy-start.7 = (f32[1,16,4,1024]{3,2,1,0:T(4,128)S(1)}, f32[1,16,4,1024]{3,2,1,0:T(4,128)}, u32[]{:S(2)}) copy-start(f32[1,16,4,1024]{3,2,1,0:T(4,128)} %param.11) | copy-start | bytes 786436
  19.4 9.0 %copy-start.8 = (s32[1,4,1024]{2,1,0:T(4,128)S(1)}, s32[1,4,1024]{2,1,0:T(4,128)}, u32[]{:S(2)}) copy-start(s32[1,4,1024]{2,1,0:T(4,128)} %param.12) | copy-start | bytes 49156
  35.3 10.5 %collective-permute-start.5 = (f32[16,2,1024]{2,1,0:T(2,128)S(1)}, f32[16,2,1024]{2,1,0:T(2,128)S(1)}, u32[]{:S(2)}, u32[]{:S(2)}) collective-permute-start(f32[16,2,1024]{2,1,0:T(2,128)S(1)} %remap.2.own1), channel_id=1, source_target_pairs={{0,63},{1,2},{2,1},{3,4},{4,3},{5,6},{6,5},{7,8},{8,7},{9,10},{10,... | collective-permute-start | bytes 393224 | tf_op jit(solution)/shard_map/ppermute | solution.py:32
  36.8 9.0 %copy-start.1 = (f32[1,2,4,4,1024]{4,3,2,1,0:T(4,128)S(1)}, f32[1,2,4,4,1024]{4,3,2,1,0:T(4,128)}, u32[]{:S(2)}) copy-start(f32[1,2,4,4,1024]{4,3,2,1,0:T(4,128)} %param.10) | copy-start | bytes 393220
  43.7 4.6 %collective-permute-start.7 = (f32[16,2,1024]{2,1,0:T(2,128)S(1)}, f32[16,2,1024]{2,1,0:T(2,128)S(1)}, u32[]{:S(2)}, u32[]{:S(2)}) collective-permute-start(f32[16,2,1024]{2,1,0:T(2,128)S(1)} %remap.3.own2), channel_id=1, source_target_pairs={{0,1},{1,0},{2,3},{3,2},{4,5},{5,4},{6,7},{7,6},{8,9},{9,8},{10,11... | collective-permute-start | bytes 393224 | tf_op jit(solution)/shard_map/ppermute | solution.py:32

commit v7 on v6

--- a/solution.py
+++ b/solution.py
@@ -10,6 +10,7 @@
 diffusion = 0.12
 LOW = 128
 BLOCK = 1024
+LANE_TERMS = (0, 1)
 PACK_BLOCK = 512
 VMEM_LIMIT = 48 * 2**20
 FULL_VMEM = 60 * 2**20
@@ -150,23 +151,68 @@
     )(field, rows, cols)
 
 
-def added_reads(sources, near, slot, weight, table, tracers, row, at):
+def lane_chosen(piece, low, bits, rows, first, level):
+    if level == 0:
+        part = piece[rows, first * LOW : (first + 1) * LOW]
+        return jnp.take_along_axis(part, low, axis=1, mode="promise_in_bounds")
+    half = 1 << (level - 1)
+    even = lane_chosen(piece, low, bits, rows, first, level - 1)
+    odd = lane_chosen(piece, low, bits, rows, first + half, level - 1)
+    return jnp.where(bits[level - 1], odd, even)
+
+
+def lane_reads(sources, pieces, which, entry):
+    tracers, capacity = pieces[0].shape
+    low = jnp.broadcast_to(entry & (LOW - 1), (8, LOW))
+    high = jnp.broadcast_to(entry // LOW, (8, LOW))
+    wide = jnp.broadcast_to(which, (8, LOW))
+    depth = (capacity // LOW).bit_length() - 1
+    bits = [((high >> bit) & 1) == 1 for bit in range(depth)]
+    halves = []
+    for at in range(0, tracers, 8):
+        read = None
+        for source, piece in zip(sources, pieces):
+            part = lane_chosen(piece, low, bits, slice(at, at + 8), 0, depth)
+            read = part if read is None else jnp.where(wide == source, part, read)
+        halves.append(read)
+    return jnp.concatenate(halves, axis=0)
+
+
+def product_reads(sources, table, which, entry, tracers):
+    product = low_product(table, entry, tracers)
+    high = high_part(entry, tracers)
+    count = len(product) // len(sources)
+    wide = jnp.broadcast_to(which, high.shape)
+    read = None
+    for rank, source in enumerate(sources):
+        part = chosen(product[rank * count : (rank + 1) * count], high)
+        read = part if read is None else jnp.where(wide == source, part, read)
+    return read
+
+
+def added_reads(sources, pieces, near, slot, weight, table, tracers, row, col):
+    lane_terms = {k: [] for k in LANE_TERMS}
+    lane_work = [(k, at) for k in LANE_TERMS for at in range(0, BLOCK, LOW)]
+    products = [k for k in range(near.shape[0]) if k not in LANE_TERMS]
     total = None
-    for k in range(near.shape[0]):
-        which = near[k, pl.ds(row, 1), at]
-        entry = slot[k, pl.ds(row, 1), at]
-        product = low_product(table, entry, tracers)
-        high = high_part(entry, tracers)
-        count = len(product) // len(sources)
-        wide = jnp.broadcast_to(which, high.shape)
-        read = chosen(product[:count], high)
-        inside = which == sources[0]
-        for rank in range(1, len(sources)):
-            part = chosen(product[rank * count : (rank + 1) * count], high)
-            read = jnp.where(wide == sources[rank], part, read)
-            inside = inside | (which == sources[rank])
-        term = jnp.where(inside, weight[k, pl.ds(row, 1), at], 0.0) * read
+
+    lists = [[v[k, pl.ds(row, 1), pl.ds(col, BLOCK)] for v in (near, slot, weight)] for k in range(near.shape[0])]
+    for item in lists:
+        inside = item[0] == sources[0]
+        for source in sources[1:]:
+            inside = inside | (item[0] == source)
+        item[2] = jnp.where(inside, item[2], 0.0)
+
+    for place, k in enumerate(products):
+        which, entry, share = lists[k]
+        term = share * product_reads(sources, table, which, entry, tracers)
         total = term if total is None else total + term
+        begin, end = (len(lane_work) * p // len(products) for p in (place, place + 1))
+        for lane_k, start in lane_work[begin:end]:
+            which, entry, share = (v[:, start : start + LOW] for v in lists[lane_k])
+            lane_terms[lane_k].append(share * lane_reads(sources, pieces, which, entry))
+    for parts in lane_terms.values():
+        total = total + jnp.concatenate(parts, axis=1)
     return total
 
 
@@ -186,8 +232,10 @@
     for row in range(near.shape[1]):
 
         def body(step, carry, row=row):
-            at = pl.ds(pl.multiple_of(step * BLOCK, BLOCK), BLOCK)
-            out[:, row, at] = added_reads(sources, near, slot, weight, table, tracers, row, at)
+            col = pl.multiple_of(step * BLOCK, BLOCK)
+            out[:, row, pl.ds(col, BLOCK)] = added_reads(
+                sources, [piece], near, slot, weight, table, tracers, row, col
+            )
             return carry
 
         lax.fori_loop(0, width // BLOCK, body, 0)
@@ -214,8 +262,9 @@
         row = start[0] + place
 
         def body(step, carry, place=place, row=row):
-            at = pl.ds(pl.multiple_of(step * BLOCK, BLOCK), BLOCK)
-            total = added_reads(sources, near, slot, weight, table, tracers, row, at)
+            col = pl.multiple_of(step * BLOCK, BLOCK)
+            at = pl.ds(col, BLOCK)
+            total = added_reads(sources, pieces, near, slot, weight, table, tracers, row, col)
             total = total + partial[:, row, at]
             own = field[:, 0, row, at]
             wet = mask[pl.ds(row, 1), at].astype(jnp.float32)

time: 49.7 us -> 48.2 us (0.970)
  Pallas kernels: 27.5 us -> 23.7 us
  waiting for transfers between devices: 6.34 us -> 8.67 us
    pallas_call x2, Pallas kernels: 13.7 us -> 10.8 us  [remap(): pl.pallas_call(functools.partial(remap_kernel, sources), grid=(1,), in_sp...]
    ppermute x2, waiting for transfers between devices: 2.02 us -> 3.48 us  [swapped(): return lax.ppermute(value, 'tile', pairs)]
    ppermute x6, waiting for transfers between devices: 4.32 us -> 5.19 us  [moved(): return lax.ppermute(value, ('comp', 'tile'), pairs)]
    pallas_call x1, Pallas kernels: 4.67 us -> 3.79 us  [remap_near(): pl.pallas_call(functools.partial(near_kernel, (source,)), out_shape=jax.S...]
  transfers between devices with their start and end apart: 8 -> 8, of which waited for: 3 -> 3; matrix products, arithmetic and copies ran while one was open for 0% -> 0% of each run, Pallas kernels for 48% -> 42%
where the time goes in v7:
time: 48.2 us; the launch traced here: 48.1 us
  Pallas kernels  23.7 us (49%)
  starting transfers between devices  15.6 us (32%)
  waiting for transfers between devices  8.67 us (18%)
    ppermute x6, starting transfers between devices, moved(): return lax.ppermute(value, ('comp', 'tile'), pairs)  14 us
    pallas_call x2, Pallas kernels, remap(): pl.pallas_call(functools.partial(remap_kernel, sources), grid=(1,), in_sp...  10.8 us
    ppermute x6, waiting for transfers between devices, moved(): return lax.ppermute(value, ('comp', 'tile'), pairs)  5.19 us
    pallas_call x1, Pallas kernels, remap_near(): pl.pallas_call(functools.partial(near_kernel, (source,)), out_shape=jax.S...  3.79 us
    ppermute x2, waiting for transfers between devices, swapped(): return lax.ppermute(value, 'tile', pairs)  3.48 us
    pallas_call x1, Pallas kernels, pack(): pl.pallas_call(pack_kernel, grid=(1,), in_specs=[level_spec(field), whole...  2.92 us
    pallas_call x1, Pallas kernels, upper_levels(): pl.pallas_call(upper_kernel, grid=(levels - 1,), out_shape=jax.ShapeDtype...  2.49 us
    pallas_call x1, Pallas kernels, edges(): pl.pallas_call(edges_kernel, in_specs=[pl.BlockSpec(memory_space=pltpu.HB...  2.42 us
  transfers between devices with their start and end apart: 8, of which 3 were waited for; matrix products, arithmetic and copies ran while one was open for 0% of the time, Pallas kernels for 42%

profile of v7, /device:TPU:1, one launch (start us, length us, event | category | flops | bytes accessed | tf_op | source)
XLA Modules:
  0.0 48.1 jit_solution(5841731532588468100)
XLA Ops:
  0.0 0.0 copy-start
  0.0 0.0 copy-start.5
  0.0 0.0 copy-start.6
  0.0 2.4 %edges.1 = (f32[56,2,1024]{2,1,0:T(2,128)}, f32[56,2,1024]{2,1,0:T(2,128)}) custom-call(f32[16,4,4,1024]{3,2,1,0:T(4,128)} %bitcast.12, f32[2,4,4,1024]{3,2,1,0:T(4,128)} %bitcast.17), custom_call_target="tpu_custom_call" | custom-call | flops 1000000 | bytes 100000 | tf_op jit(solution)/shard_map/edges/pallas_call | solution.py:99
  2.4 0.0 copy-start.9
  2.5 0.0 copy-start.2
  2.5 0.0 copy-start.3
  2.5 0.0 copy-start.4
  2.5 2.5 %collective-permute-start.3 = (f32[56,2,1024]{2,1,0:T(2,128)}, f32[56,2,1024]{2,1,0:T(2,128)S(1)}, u32[]{:S(2)}, u32[]{:S(2)}) collective-permute-start(f32[56,2,1024]{2,1,0:T(2,128)} %get-tuple-element.30), channel_id=1, source_target_pairs={{0,1},{1,2},{2,3},{3,4},{4,5},{5,6},{6,7},{7,8},{8,9},{9,10},{10,1... | collective-permute-start | bytes 1376264 | tf_op jit(solution)/shard_map/ppermute | solution.py:27
  5.0 0.0 copy-done
  5.0 0.0 copy-done.5
  5.0 0.0 copy-done.6
  5.0 2.9 %pack.1 = (f32[16,2048]{1,0:T(8,128)S(1)}, f32[16,2048]{1,0:T(8,128)S(1)}, f32[16,2048]{1,0:T(8,128)S(1)}, f32[16,2048]{1,0:T(8,128)S(1)}) custom-call(f32[16,4,4,1024]{3,2,1,0:T(4,128)S(1)} %bitcast.13, s32[4,2048]{1,0:T(4,128)S(1)} %bitcast.29, s32[4,2048]{1,0:T(4,128)S(1)} %bitcast.30), custom_call_target="tpu_custom_call" | custom-call | flops 1000000 | bytes 100000 | tf_op jit(solution)/shard_map/pack/pallas_call | solution.py:141
  8.0 1.0 %collective-permute-start.4 = (f32[16,2048]{1,0:T(8,128)S(1)}, f32[16,2048]{1,0:T(8,128)S(1)}, u32[]{:S(2)}, u32[]{:S(2)}) collective-permute-start(f32[16,2048]{1,0:T(8,128)S(1)} %get-tuple-element.32), channel_id=1, source_target_pairs={{0,64},{1,65},{2,66},{3,67},{4,68},{5,69},{6,70},{7,71},{8,72},{9,... | collective-permute-start | bytes 393224 | tf_op jit(solution)/shard_map/ppermute | solution.py:27
  9.0 1.6 %collective-permute-start = (f32[16,2048]{1,0:T(8,128)S(1)}, f32[16,2048]{1,0:T(8,128)S(1)}, u32[]{:S(2)}, u32[]{:S(2)}) collective-permute-start(f32[16,2048]{1,0:T(8,128)S(1)} %get-tuple-element.27), channel_id=1, source_target_pairs={{0,65},{1,66},{2,67},{3,68},{4,69},{5,70},{6,71},{7,72},{8,73},{9,... | collective-permute-start | bytes 393224 | tf_op jit(solution)/shard_map/ppermute | solution.py:27
  10.6 5.6 %collective-permute-start.1 = (f32[16,2048]{1,0:T(8,128)S(1)}, f32[16,2048]{1,0:T(8,128)S(1)}, u32[]{:S(2)}, u32[]{:S(2)}) collective-permute-start(f32[16,2048]{1,0:T(8,128)S(1)} %get-tuple-element.28), channel_id=1, source_target_pairs={{0,127},{1,64},{2,65},{3,66},{4,67},{5,68},{6,69},{7,70},{8,71},{9... | collective-permute-start | bytes 393224 | tf_op jit(solution)/shard_map/ppermute | solution.py:27
  16.2 2.5 %collective-permute-start.2 = (f32[16,2048]{1,0:T(8,128)S(1)}, f32[16,2048]{1,0:T(8,128)S(1)}, u32[]{:S(2)}, u32[]{:S(2)}) collective-permute-start(f32[16,2048]{1,0:T(8,128)S(1)} %get-tuple-element.29), channel_id=1, source_target_pairs={{0,126},{1,127},{2,64},{3,65},{4,66},{5,67},{6,68},{7,69},{8,70},{... | collective-permute-start | bytes 393224 | tf_op jit(solution)/shard_map/ppermute | solution.py:27
  18.7 0.0 collective-permute-done.4.piece
  18.7 0.0 copy-done.9
  18.7 0.7 %collective-permute-start.6 = (f32[56,2,1024]{2,1,0:T(2,128)S(1)}, f32[56,2,1024]{2,1,0:T(2,128)S(1)}, u32[]{:S(2)}, u32[]{:S(2)}) collective-permute-start(f32[56,2,1024]{2,1,0:T(2,128)S(1)} %copy-done.9), channel_id=1, source_target_pairs={{0,63},{1,0},{2,1},{3,2},{4,3},{5,4},{6,5},{7,6},{8,7},{9,8},{10,9... | collective-permute-start | bytes 1376264 | tf_op jit(solution)/shard_map/ppermute | solution.py:27
  19.4 0.0 copy-done.2
  19.4 0.0 copy-done.3
  19.4 0.0 copy-done.4
  19.4 0.0 copy-start.7
  19.4 0.0 copy-start.8
  19.4 3.8 %remap_near.1.partial = f32[16,4,1024]{2,1,0:T(4,128)S(1)} custom-call(s32[8,4,1024]{2,1,0:T(4,128)S(1)} %bitcast.20, s32[8,4,1024]{2,1,0:T(4,128)S(1)} %bitcast.23, f32[8,4,1024]{2,1,0:T(4,128)S(1)} %bitcast.26, f32[16,2048]{1,0:T(8,128)S(1)} %collective-permute-done.4.piece), custom_call_target="tpu_custom_call" | custom-call | flops 1000000 | bytes 100000 | tf_op jit(solution)/shard_map/remap_near/pallas_call | solution.py:247
  23.2 4.9 %collective-permute-done.rest_0_ = f32[16,2048]{1,0:T(8,128)S(1)} collective-permute-done((f32[16,2048]{1,0:T(8,128)S(1)}, f32[16,2048]{1,0:T(8,128)S(1)}, u32[]{:S(2)}, u32[]{:S(2)}) %collective-permute-start) | collective-permute-done | bytes 131104 | tf_op jit(solution)/shard_map/ppermute | solution.py:27
  28.2 0.0 collective-permute-done.1.rest_1_
  28.2 0.2 collective-permute-done.2.rest_2_
  28.4 0.0 collective-permute-done.3.before_v
  28.4 0.0 copy-done.7
  28.4 0.0 copy-done.8
  28.4 5.4 %remap.2.own1 = f32[16,2,1024]{2,1,0:T(2,128)S(1)} custom-call(s32[1]{0:T(128)} %bitcast.start, s32[8,4,1024]{2,1,0:T(4,128)S(1)} %bitcast.21, s32[8,4,1024]{2,1,0:T(4,128)S(1)} %bitcast.24, f32[8,4,1024]{2,1,0:T(4,128)S(1)} %bitcast.27, f32[16,4,4,1024]{3,2,1,0:T(4,128)S(1)} %bitcast.14, f32[16,4,1024]{2,1,0:T(4,128)S(1)} %bitcast.31, ...), custom_call_target="tpu_custom_call" | custom-call | flops 15000000512 | bytes 1000000 | tf_op jit(solution)/shard_map/remap/pallas_call | solution.py:283
  33.8 1.5 %collective-permute-start.5 = (f32[16,2,1024]{2,1,0:T(2,128)S(1)}, f32[16,2,1024]{2,1,0:T(2,128)S(1)}, u32[]{:S(2)}, u32[]{:S(2)}) collective-permute-start(f32[16,2,1024]{2,1,0:T(2,128)S(1)} %remap.2.own1), channel_id=1, source_target_pairs={{0,63},{1,2},{2,1},{3,4},{4,3},{5,6},{6,5},{7,8},{8,7},{9,10},{10,... | collective-permute-start | bytes 393224 | tf_op jit(solution)/shard_map/ppermute | solution.py:33
  35.4 0.0 copy-start.1
  35.4 5.4 %remap.3.own2 = f32[16,2,1024]{2,1,0:T(2,128)S(1)} custom-call(s32[1]{0:T(128)} %bitcast.10.start, s32[8,4,1024]{2,1,0:T(4,128)S(1)} %bitcast.22, s32[8,4,1024]{2,1,0:T(4,128)S(1)} %bitcast.25, f32[8,4,1024]{2,1,0:T(4,128)S(1)} %bitcast.28, f32[16,4,4,1024]{3,2,1,0:T(4,128)S(1)} %bitcast.15, f32[16,4,1024]{2,1,0:T(4,128)S(1)} %bitcast.32, ...), custom_call_target="tpu_custom_call" | custom-call | flops 15000000512 | bytes 1000000 | tf_op jit(solution)/shard_map/remap/pallas_call | solution.py:283
  40.8 0.1 collective-permute-start.7
  40.9 3.5 %collective-permute-done.5.got1 = f32[16,2,1024]{2,1,0:T(2,128)S(1)} collective-permute-done((f32[16,2,1024]{2,1,0:T(2,128)S(1)}, f32[16,2,1024]{2,1,0:T(2,128)S(1)}, u32[]{:S(2)}, u32[]{:S(2)}) %collective-permute-start.5) | collective-permute-done | bytes 131104 | tf_op jit(solution)/shard_map/ppermute | solution.py:33
  44.3 0.0 collective-permute-done.6.after_v
  44.3 0.0 copy-done.1
  44.3 2.5 %upper_levels.1.whole = f32[16,4,4,1024]{3,2,1,0:T(4,128)} custom-call(f32[16,4,4,1024]{3,2,1,0:T(4,128)S(1)} %bitcast.16, f32[56,2,1024]{2,1,0:T(2,128)S(1)} %collective-permute-done.3.before_v, f32[56,2,1024]{2,1,0:T(2,128)S(1)} %collective-permute-done.6.after_v, f32[2,4,4,1024]{3,2,1,0:T(4,128)S(1)} %bitcast.18), custom_call_target="tpu_custom_call" | custom-call | flops 1000000 | bytes 100000 | tf_op jit(solution)/shard_map/upper_levels/pallas_call | solution.py:367
  46.8 0.0 collective-permute-done.7.got2
  46.8 1.2 %surface_level.1 = f32[16,4,4,1024]{3,2,1,0:T(4,128)} custom-call(s32[1]{0:T(128)} %bitcast.start, f32[2,4,4,1024]{3,2,1,0:T(4,128)S(1)} %bitcast.19, f32[56,2,1024]{2,1,0:T(2,128)S(1)} %collective-permute-done.3.before_v, f32[56,2,1024]{2,1,0:T(2,128)S(1)} %collective-permute-done.6.after_v, ...), custom_call_target="tpu_custom_call", output_to_operand_aliasing={{}: (8, {})} | custom-call | tf_op jit(solution)/shard_map/surface_level/pallas_call | solution.py:387
Async XLA Ops:
  0.0 5.0 %copy-start = (f32[1,16,4,4,1024]{4,3,2,1,0:T(4,128)S(1)}, f32[1,16,4,4,1024]{4,3,2,1,0:T(4,128)}, u32[]{:S(2)}) copy-start(f32[1,16,4,4,1024]{4,3,2,1,0:T(4,128)} %param.9) | copy-start | bytes 3145732
  0.0 5.0 %copy-start.5 = (s32[1,1,4,2048]{3,2,1,0:T(4,128)S(1)}, s32[1,1,4,2048]{3,2,1,0:T(4,128)}, u32[]{:S(2)}) copy-start(s32[1,1,4,2048]{3,2,1,0:T(4,128)} %param.13) | copy-start | bytes 98308
  0.0 5.0 %copy-start.6 = (s32[1,1,4,2048]{3,2,1,0:T(4,128)S(1)}, s32[1,1,4,2048]{3,2,1,0:T(4,128)}, u32[]{:S(2)}) copy-start(s32[1,1,4,2048]{3,2,1,0:T(4,128)} %param.14) | copy-start | bytes 98308
  2.4 16.2 %copy-start.9 = (f32[56,2,1024]{2,1,0:T(2,128)S(1)}, f32[56,2,1024]{2,1,0:T(2,128)}, u32[]{:S(2)}) copy-start(f32[56,2,1024]{2,1,0:T(2,128)} %get-tuple-element.37) | copy-start | bytes 1376260
  2.5 16.9 %copy-start.2 = (s32[1,8,4,1024]{3,2,1,0:T(4,128)S(1)}, s32[1,8,4,1024]{3,2,1,0:T(4,128)}, u32[]{:S(2)}) copy-start(s32[1,8,4,1024]{3,2,1,0:T(4,128)} %param.15) | copy-start | bytes 393220
  2.5 16.9 %copy-start.3 = (s32[1,8,4,1024]{3,2,1,0:T(4,128)S(1)}, s32[1,8,4,1024]{3,2,1,0:T(4,128)}, u32[]{:S(2)}) copy-start(s32[1,8,4,1024]{3,2,1,0:T(4,128)} %param.16) | copy-start | bytes 393220
  2.5 16.9 %copy-start.4 = (f32[1,8,4,1024]{3,2,1,0:T(4,128)S(1)}, f32[1,8,4,1024]{3,2,1,0:T(4,128)}, u32[]{:S(2)}) copy-start(f32[1,8,4,1024]{3,2,1,0:T(4,128)} %param.17) | copy-start | bytes 393220
  2.5 25.9 %collective-permute-start.3 = (f32[56,2,1024]{2,1,0:T(2,128)}, f32[56,2,1024]{2,1,0:T(2,128)S(1)}, u32[]{:S(2)}, u32[]{:S(2)}) collective-permute-start(f32[56,2,1024]{2,1,0:T(2,128)} %get-tuple-element.30), channel_id=1, source_target_pairs={{0,1},{1,2},{2,3},{3,4},{4,5},{5,6},{6,7},{7,8},{8,9},{9,10},{10,1... | collective-permute-start | bytes 1376264 | tf_op jit(solution)/shard_map/ppermute | solution.py:27
  8.0 10.7 %collective-permute-start.4 = (f32[16,2048]{1,0:T(8,128)S(1)}, f32[16,2048]{1,0:T(8,128)S(1)}, u32[]{:S(2)}, u32[]{:S(2)}) collective-permute-start(f32[16,2048]{1,0:T(8,128)S(1)} %get-tuple-element.32), channel_id=1, source_target_pairs={{0,64},{1,65},{2,66},{3,67},{4,68},{5,69},{6,70},{7,71},{8,72},{9,... | collective-permute-start | bytes 393224 | tf_op jit(solution)/shard_map/ppermute | solution.py:27
  9.0 19.2 %collective-permute-start = (f32[16,2048]{1,0:T(8,128)S(1)}, f32[16,2048]{1,0:T(8,128)S(1)}, u32[]{:S(2)}, u32[]{:S(2)}) collective-permute-start(f32[16,2048]{1,0:T(8,128)S(1)} %get-tuple-element.27), channel_id=1, source_target_pairs={{0,65},{1,66},{2,67},{3,68},{4,69},{5,70},{6,71},{7,72},{8,73},{9,... | collective-permute-start | bytes 393224 | tf_op jit(solution)/shard_map/ppermute | solution.py:27
  10.6 17.6 %collective-permute-start.1 = (f32[16,2048]{1,0:T(8,128)S(1)}, f32[16,2048]{1,0:T(8,128)S(1)}, u32[]{:S(2)}, u32[]{:S(2)}) collective-permute-start(f32[16,2048]{1,0:T(8,128)S(1)} %get-tuple-element.28), channel_id=1, source_target_pairs={{0,127},{1,64},{2,65},{3,66},{4,67},{5,68},{6,69},{7,70},{8,71},{9... | collective-permute-start | bytes 393224 | tf_op jit(solution)/shard_map/ppermute | solution.py:27
  16.2 12.2 %collective-permute-start.2 = (f32[16,2048]{1,0:T(8,128)S(1)}, f32[16,2048]{1,0:T(8,128)S(1)}, u32[]{:S(2)}, u32[]{:S(2)}) collective-permute-start(f32[16,2048]{1,0:T(8,128)S(1)} %get-tuple-element.29), channel_id=1, source_target_pairs={{0,126},{1,127},{2,64},{3,65},{4,66},{5,67},{6,68},{7,69},{8,70},{... | collective-permute-start | bytes 393224 | tf_op jit(solution)/shard_map/ppermute | solution.py:27
  18.7 25.7 %collective-permute-start.6 = (f32[56,2,1024]{2,1,0:T(2,128)S(1)}, f32[56,2,1024]{2,1,0:T(2,128)S(1)}, u32[]{:S(2)}, u32[]{:S(2)}) collective-permute-start(f32[56,2,1024]{2,1,0:T(2,128)S(1)} %copy-done.9), channel_id=1, source_target_pairs={{0,63},{1,0},{2,1},{3,2},{4,3},{5,4},{6,5},{7,6},{8,7},{9,8},{10,9... | collective-permute-start | bytes 1376264 | tf_op jit(solution)/shard_map/ppermute | solution.py:27
  19.4 9.0 %copy-start.7 = (f32[1,16,4,1024]{3,2,1,0:T(4,128)S(1)}, f32[1,16,4,1024]{3,2,1,0:T(4,128)}, u32[]{:S(2)}) copy-start(f32[1,16,4,1024]{3,2,1,0:T(4,128)} %param.11) | copy-start | bytes 786436
  19.4 9.0 %copy-start.8 = (s32[1,4,1024]{2,1,0:T(4,128)S(1)}, s32[1,4,1024]{2,1,0:T(4,128)}, u32[]{:S(2)}) copy-start(s32[1,4,1024]{2,1,0:T(4,128)} %param.12) | copy-start | bytes 49156
  33.8 10.5 %collective-permute-start.5 = (f32[16,2,1024]{2,1,0:T(2,128)S(1)}, f32[16,2,1024]{2,1,0:T(2,128)S(1)}, u32[]{:S(2)}, u32[]{:S(2)}) collective-permute-start(f32[16,2,1024]{2,1,0:T(2,128)S(1)} %remap.2.own1), channel_id=1, source_target_pairs={{0,63},{1,2},{2,1},{3,4},{4,3},{5,6},{6,5},{7,8},{8,7},{9,10},{10,... | collective-permute-start | bytes 393224 | tf_op jit(solution)/shard_map/ppermute | solution.py:33
  35.4 9.0 %copy-start.1 = (f32[1,2,4,4,1024]{4,3,2,1,0:T(4,128)S(1)}, f32[1,2,4,4,1024]{4,3,2,1,0:T(4,128)}, u32[]{:S(2)}) copy-start(f32[1,2,4,4,1024]{4,3,2,1,0:T(4,128)} %param.10) | copy-start | bytes 393220
  40.8 6.1 %collective-permute-start.7 = (f32[16,2,1024]{2,1,0:T(2,128)S(1)}, f32[16,2,1024]{2,1,0:T(2,128)S(1)}, u32[]{:S(2)}, u32[]{:S(2)}) collective-permute-start(f32[16,2,1024]{2,1,0:T(2,128)S(1)} %remap.3.own2), channel_id=1, source_target_pairs={{0,1},{1,0},{2,3},{3,2},{4,5},{5,4},{6,7},{7,6},{8,9},{9,8},{10,11... | collective-permute-start | bytes 393224 | tf_op jit(solution)/shard_map/ppermute | solution.py:33

commit v8 on v7

--- a/solution.py
+++ b/solution.py
@@ -328,8 +328,9 @@
     return pairs
 
 
-def upper_kernel(field, before_v, after_v, velocity, out):
-    level = pl.program_id(0)
+def upper_kernel(first, field, before_v, after_v, velocity, *rest):
+    out = rest[-1]
+    level = pl.program_id(0) + (first - 1)
     tracers, _, grid_rows, _ = field.shape
     at = pl.ds(level * tracers, tracers)
     rows = [before_v[at, row] for row in range(2)]
@@ -340,7 +341,7 @@
         out[:, 0, row] = value
 
 
-def surface_kernel(start, velocity, before_v, after_v, own1, own2, got1, got2, whole, out):
+def surface_kernel(start, got2, got1, velocity, before_v, after_v, own1, own2, whole, out):
     del whole
     odd = start[0] > 0
     first, last = [], []
@@ -361,29 +362,31 @@
     return pl.BlockSpec(shape, lambda *_: (0,) * len(shape))
 
 
-def upper_levels(field, before, after, velocity):
-    tracers, levels, rows, width = field.shape
+def upper_levels(first, count, field, before_v, after_v, velocity, *whole):
+    tracers, _, rows, width = field.shape
     block = (tracers, 1, rows, width)
     return pl.pallas_call(
-        upper_kernel,
-        grid=(levels - 1,),
+        functools.partial(upper_kernel, first),
+        grid=(count,),
         out_shape=jax.ShapeDtypeStruct(field.shape, jnp.float32),
         in_specs=[
-            pl.BlockSpec(block, lambda level: (0, level + 1, 0, 0)),
-            whole_spec(before.shape),
-            whole_spec(after.shape),
+            pl.BlockSpec(block, lambda step: (0, step + first, 0, 0)),
+            whole_spec(before_v.shape),
+            whole_spec(after_v.shape),
             whole_spec(velocity.shape),
-        ],
-        out_specs=pl.BlockSpec(block, lambda level: (0, level + 1, 0, 0)),
+        ]
+        + [pl.BlockSpec(memory_space=pl.ANY)] * len(whole),
+        out_specs=pl.BlockSpec(block, lambda step: (0, step + first, 0, 0)),
+        input_output_aliases={4: 0} if whole else {},
         compiler_params=pltpu.CompilerParams(vmem_limit_bytes=VMEM_LIMIT),
         cost_estimate=SMALL_COST,
         name="upper_levels",
-    )(field, before, after, velocity)
+    )(field, before_v, after_v, velocity, *whole)
 
 
 def surface_level(start, velocity, before_v, after_v, own1, own2, got1, got2, whole):
     tracers, _, rows, width = whole.shape
-    values = (velocity, before_v, after_v, own1, own2, got1, got2)
+    values = (got2, got1, velocity, before_v, after_v, own1, own2)
     return pl.pallas_call(
         surface_kernel,
         grid=(1,),
@@ -430,8 +433,9 @@
     pieces, own1 = lax.optimization_barrier((pieces, own1))
     own2 = remap(others, start2, pieces, *shared)
     got2 = swapped(own2, -1)
-    before_v, got1 = lax.optimization_barrier((before_v, got1))
-    whole = upper_levels(field, before_v, after_v, speed)
+    whole = upper_levels(1, levels - 2, field, before_v, after_v, speed)
+    whole, got1 = lax.optimization_barrier((whole, got1))
+    whole = upper_levels(levels - 1, 1, field, before_v, after_v, speed, whole)
     return surface_level(start1, speed, before_v, after_v, own1, own2, got1, got2, whole)[None]
 
 

time: 48.2 us -> 46.9 us (0.973)
  waiting for transfers between devices: 8.67 us -> 6.84 us
  Pallas kernels: 23.7 us -> 24.2 us
    ppermute x2, waiting for transfers between devices: 3.48 us -> 1.65 us  [swapped(): return lax.ppermute(value, 'tile', pairs)]
    pallas_call x1 -> x2, Pallas kernels: 2.49 us -> 3.04 us  [upper_levels(): pl.pallas_call(functools.partial(upper_kernel, first), grid=(count,), out...]
  transfers between devices with their start and end apart: 8 -> 8, of which waited for: 3 -> 3; matrix products, arithmetic and copies ran while one was open for 0% -> 0% of each run, Pallas kernels for 42% -> 44%
where the time goes in v8:
time: 46.9 us; the launch traced here: 46.8 us
  Pallas kernels  24.2 us (52%)
  starting transfers between devices  15.6 us (33%)
  waiting for transfers between devices  6.84 us (15%)
    ppermute x6, starting transfers between devices, moved(): return lax.ppermute(value, ('comp', 'tile'), pairs)  14 us
    pallas_call x2, Pallas kernels, remap(): pl.pallas_call(functools.partial(remap_kernel, sources), grid=(1,), in_sp...  10.8 us
    ppermute x6, waiting for transfers between devices, moved(): return lax.ppermute(value, ('comp', 'tile'), pairs)  5.19 us
    pallas_call x1, Pallas kernels, remap_near(): pl.pallas_call(functools.partial(near_kernel, (source,)), out_shape=jax.S...  3.79 us
    pallas_call x2, Pallas kernels, upper_levels(): pl.pallas_call(functools.partial(upper_kernel, first), grid=(count,), out...  3.04 us
    pallas_call x1, Pallas kernels, pack(): pl.pallas_call(pack_kernel, grid=(1,), in_specs=[level_spec(field), whole...  2.92 us
    pallas_call x1, Pallas kernels, edges(): pl.pallas_call(edges_kernel, in_specs=[pl.BlockSpec(memory_space=pltpu.HB...  2.42 us
    ppermute x2, waiting for transfers between devices, swapped(): return lax.ppermute(value, 'tile', pairs)  1.65 us
  transfers between devices with their start and end apart: 8, of which 3 were waited for; matrix products, arithmetic and copies ran while one was open for 0% of the time, Pallas kernels for 44%

profile of v8, /device:TPU:1, one launch (start us, length us, event | category | flops | bytes accessed | tf_op | source)
XLA Modules:
  0.0 46.8 jit_solution(3940488378388884092)
XLA Ops:
  0.0 0.0 copy-start
  0.0 0.0 copy-start.5
  0.0 0.0 copy-start.6
  0.0 2.4 %edges.1 = (f32[56,2,1024]{2,1,0:T(2,128)}, f32[56,2,1024]{2,1,0:T(2,128)}) custom-call(f32[16,4,4,1024]{3,2,1,0:T(4,128)} %bitcast.12, f32[2,4,4,1024]{3,2,1,0:T(4,128)} %bitcast.18), custom_call_target="tpu_custom_call" | custom-call | flops 1000000 | bytes 100000 | tf_op jit(solution)/shard_map/edges/pallas_call | solution.py:99
  2.4 0.0 copy-start.9
  2.5 0.0 copy-start.2
  2.5 0.0 copy-start.3
  2.5 0.0 copy-start.4
  2.5 2.5 %collective-permute-start.4 = (f32[56,2,1024]{2,1,0:T(2,128)}, f32[56,2,1024]{2,1,0:T(2,128)S(1)}, u32[]{:S(2)}, u32[]{:S(2)}) collective-permute-start(f32[56,2,1024]{2,1,0:T(2,128)} %get-tuple-element.31), channel_id=1, source_target_pairs={{0,1},{1,2},{2,3},{3,4},{4,5},{5,6},{6,7},{7,8},{8,9},{9,10},{10,1... | collective-permute-start | bytes 1376264 | tf_op jit(solution)/shard_map/ppermute | solution.py:27
  5.0 0.0 copy-done
  5.0 0.0 copy-done.5
  5.0 0.0 copy-done.6
  5.0 2.9 %pack.1 = (f32[16,2048]{1,0:T(8,128)S(1)}, f32[16,2048]{1,0:T(8,128)S(1)}, f32[16,2048]{1,0:T(8,128)S(1)}, f32[16,2048]{1,0:T(8,128)S(1)}) custom-call(f32[16,4,4,1024]{3,2,1,0:T(4,128)S(1)} %bitcast.13, s32[4,2048]{1,0:T(4,128)S(1)} %bitcast.31, s32[4,2048]{1,0:T(4,128)S(1)} %bitcast.32), custom_call_target="tpu_custom_call" | custom-call | flops 1000000 | bytes 100000 | tf_op jit(solution)/shard_map/pack/pallas_call | solution.py:141
  8.0 1.0 %collective-permute-start = (f32[16,2048]{1,0:T(8,128)S(1)}, f32[16,2048]{1,0:T(8,128)S(1)}, u32[]{:S(2)}, u32[]{:S(2)}) collective-permute-start(f32[16,2048]{1,0:T(8,128)S(1)} %get-tuple-element.27), channel_id=1, source_target_pairs={{0,64},{1,65},{2,66},{3,67},{4,68},{5,69},{6,70},{7,71},{8,72},{9,... | collective-permute-start | bytes 393224 | tf_op jit(solution)/shard_map/ppermute | solution.py:27
  9.0 1.6 %collective-permute-start.1 = (f32[16,2048]{1,0:T(8,128)S(1)}, f32[16,2048]{1,0:T(8,128)S(1)}, u32[]{:S(2)}, u32[]{:S(2)}) collective-permute-start(f32[16,2048]{1,0:T(8,128)S(1)} %get-tuple-element.28), channel_id=1, source_target_pairs={{0,65},{1,66},{2,67},{3,68},{4,69},{5,70},{6,71},{7,72},{8,73},{9,... | collective-permute-start | bytes 393224 | tf_op jit(solution)/shard_map/ppermute | solution.py:27
  10.6 5.6 %collective-permute-start.2 = (f32[16,2048]{1,0:T(8,128)S(1)}, f32[16,2048]{1,0:T(8,128)S(1)}, u32[]{:S(2)}, u32[]{:S(2)}) collective-permute-start(f32[16,2048]{1,0:T(8,128)S(1)} %get-tuple-element.29), channel_id=1, source_target_pairs={{0,127},{1,64},{2,65},{3,66},{4,67},{5,68},{6,69},{7,70},{8,71},{9... | collective-permute-start | bytes 393224 | tf_op jit(solution)/shard_map/ppermute | solution.py:27
  16.2 2.5 %collective-permute-start.3 = (f32[16,2048]{1,0:T(8,128)S(1)}, f32[16,2048]{1,0:T(8,128)S(1)}, u32[]{:S(2)}, u32[]{:S(2)}) collective-permute-start(f32[16,2048]{1,0:T(8,128)S(1)} %get-tuple-element.30), channel_id=1, source_target_pairs={{0,126},{1,127},{2,64},{3,65},{4,66},{5,67},{6,68},{7,69},{8,70},{... | collective-permute-start | bytes 393224 | tf_op jit(solution)/shard_map/ppermute | solution.py:27
  18.7 0.0 collective-permute-done.piece
  18.7 0.0 copy-done.9
  18.7 0.7 %collective-permute-start.6 = (f32[56,2,1024]{2,1,0:T(2,128)S(1)}, f32[56,2,1024]{2,1,0:T(2,128)S(1)}, u32[]{:S(2)}, u32[]{:S(2)}) collective-permute-start(f32[56,2,1024]{2,1,0:T(2,128)S(1)} %copy-done.9), channel_id=1, source_target_pairs={{0,63},{1,0},{2,1},{3,2},{4,3},{5,4},{6,5},{7,6},{8,7},{9,8},{10,9... | collective-permute-start | bytes 1376264 | tf_op jit(solution)/shard_map/ppermute | solution.py:27
  19.4 0.0 copy-done.2
  19.4 0.0 copy-done.3
  19.4 0.0 copy-done.4
  19.4 0.0 copy-start.7
  19.4 0.0 copy-start.8
  19.4 3.8 %remap_near.1.partial = f32[16,4,1024]{2,1,0:T(4,128)S(1)} custom-call(s32[8,4,1024]{2,1,0:T(4,128)S(1)} %bitcast.22, s32[8,4,1024]{2,1,0:T(4,128)S(1)} %bitcast.25, f32[8,4,1024]{2,1,0:T(4,128)S(1)} %bitcast.28, f32[16,2048]{1,0:T(8,128)S(1)} %collective-permute-done.piece), custom_call_target="tpu_custom_call" | custom-call | flops 1000000 | bytes 100000 | tf_op jit(solution)/shard_map/remap_near/pallas_call | solution.py:247
  23.2 4.9 %collective-permute-done.1.rest_0_ = f32[16,2048]{1,0:T(8,128)S(1)} collective-permute-done((f32[16,2048]{1,0:T(8,128)S(1)}, f32[16,2048]{1,0:T(8,128)S(1)}, u32[]{:S(2)}, u32[]{:S(2)}) %collective-permute-start.1) | collective-permute-done | bytes 131104 | tf_op jit(solution)/shard_map/ppermute | solution.py:27
  28.2 0.0 collective-permute-done.2.rest_1_
  28.2 0.2 collective-permute-done.3.rest_2_
  28.4 0.0 collective-permute-done.4.before_v
  28.4 0.0 copy-done.7
  28.4 0.0 copy-done.8
  28.4 5.4 %remap.2.own1 = f32[16,2,1024]{2,1,0:T(2,128)S(1)} custom-call(s32[1]{0:T(128)} %bitcast.start, s32[8,4,1024]{2,1,0:T(4,128)S(1)} %bitcast.23, s32[8,4,1024]{2,1,0:T(4,128)S(1)} %bitcast.26, f32[8,4,1024]{2,1,0:T(4,128)S(1)} %bitcast.29, f32[16,4,4,1024]{3,2,1,0:T(4,128)S(1)} %bitcast.14, f32[16,4,1024]{2,1,0:T(4,128)S(1)} %bitcast.33, ...), custom_call_target="tpu_custom_call" | custom-call | flops 15000000512 | bytes 1000000 | tf_op jit(solution)/shard_map/remap/pallas_call | solution.py:283
  33.8 1.5 %collective-permute-start.7 = (f32[16,2,1024]{2,1,0:T(2,128)S(1)}, f32[16,2,1024]{2,1,0:T(2,128)S(1)}, u32[]{:S(2)}, u32[]{:S(2)}) collective-permute-start(f32[16,2,1024]{2,1,0:T(2,128)S(1)} %remap.2.own1), channel_id=1, source_target_pairs={{0,63},{1,2},{2,1},{3,4},{4,3},{5,6},{6,5},{7,8},{8,7},{9,10},{10,... | collective-permute-start | bytes 393224 | tf_op jit(solution)/shard_map/ppermute | solution.py:33
  35.4 0.0 copy-start.1
  35.4 5.4 %remap.3.own2 = f32[16,2,1024]{2,1,0:T(2,128)S(1)} custom-call(s32[1]{0:T(128)} %bitcast.1.start, s32[8,4,1024]{2,1,0:T(4,128)S(1)} %bitcast.24, s32[8,4,1024]{2,1,0:T(4,128)S(1)} %bitcast.27, f32[8,4,1024]{2,1,0:T(4,128)S(1)} %bitcast.30, f32[16,4,4,1024]{3,2,1,0:T(4,128)S(1)} %bitcast.15, f32[16,4,1024]{2,1,0:T(4,128)S(1)} %bitcast.34, ...), custom_call_target="tpu_custom_call" | custom-call | flops 15000000512 | bytes 1000000 | tf_op jit(solution)/shard_map/remap/pallas_call | solution.py:283
  40.8 0.1 collective-permute-start.5
  40.9 0.0 collective-permute-done.6.after_v
  40.9 0.0 copy-done.1
  40.9 1.8 %upper_levels.2.rest_0_ = f32[16,4,4,1024]{3,2,1,0:T(4,128)} custom-call(f32[16,4,4,1024]{3,2,1,0:T(4,128)S(1)} %bitcast.16, f32[56,2,1024]{2,1,0:T(2,128)S(1)} %collective-permute-done.4.before_v, f32[56,2,1024]{2,1,0:T(2,128)S(1)} %collective-permute-done.6.after_v, f32[2,4,4,1024]{3,2,1,0:T(4,128)S(1)} %bitcast.19), custom_call_target="tpu_custom_call" | custom-call | flops 1000000 | bytes 100000 | tf_op jit(solution)/shard_map/upper_levels/pallas_call | solution.py:368
  42.7 1.6 %collective-permute-done.7.got1 = f32[16,2,1024]{2,1,0:T(2,128)S(1)} collective-permute-done((f32[16,2,1024]{2,1,0:T(2,128)S(1)}, f32[16,2,1024]{2,1,0:T(2,128)S(1)}, u32[]{:S(2)}, u32[]{:S(2)}) %collective-permute-start.7) | collective-permute-done | bytes 131104 | tf_op jit(solution)/shard_map/ppermute | solution.py:33
  44.3 1.2 %upper_levels.3.whole = f32[16,4,4,1024]{3,2,1,0:T(4,128)} custom-call(f32[16,4,4,1024]{3,2,1,0:T(4,128)S(1)} %bitcast.17, f32[56,2,1024]{2,1,0:T(2,128)S(1)} %collective-permute-done.4.before_v, f32[56,2,1024]{2,1,0:T(2,128)S(1)} %collective-permute-done.6.after_v, f32[2,4,4,1024]{3,2,1,0:T(4,128)S(1)} %bitcast.20, ...), custom_call_target="tpu_custom_call", output_to_operand_aliasing={{}: (4, {})} | custom-call | flops 1000000 | bytes 100000 | tf_op jit(solution)/shard_map/upper_levels/pallas_call | solution.py:368
  45.6 0.0 collective-permute-done.5.got2
  45.6 1.2 %surface_level.1 = f32[16,4,4,1024]{3,2,1,0:T(4,128)} custom-call(s32[1]{0:T(128)} %bitcast.start, f32[16,2,1024]{2,1,0:T(2,128)S(1)} %collective-permute-done.5.got2, f32[16,2,1024]{2,1,0:T(2,128)S(1)} %collective-permute-done.7.got1, f32[2,4,4,1024]{3,2,1,0:T(4,128)S(1)} %bitcast.21, ...), custom_call_target="tpu_custom_call", output_to_operand_aliasing={{}: (8, {})} | custom-call | tf_op jit(solution)/shard_map/surface_level/pallas_call | solution.py:390
Async XLA Ops:
  0.0 5.0 %copy-start = (f32[1,16,4,4,1024]{4,3,2,1,0:T(4,128)S(1)}, f32[1,16,4,4,1024]{4,3,2,1,0:T(4,128)}, u32[]{:S(2)}) copy-start(f32[1,16,4,4,1024]{4,3,2,1,0:T(4,128)} %param.9) | copy-start | bytes 3145732
  0.0 5.0 %copy-start.5 = (s32[1,1,4,2048]{3,2,1,0:T(4,128)S(1)}, s32[1,1,4,2048]{3,2,1,0:T(4,128)}, u32[]{:S(2)}) copy-start(s32[1,1,4,2048]{3,2,1,0:T(4,128)} %param.13) | copy-start | bytes 98308
  0.0 5.0 %copy-start.6 = (s32[1,1,4,2048]{3,2,1,0:T(4,128)S(1)}, s32[1,1,4,2048]{3,2,1,0:T(4,128)}, u32[]{:S(2)}) copy-start(s32[1,1,4,2048]{3,2,1,0:T(4,128)} %param.14) | copy-start | bytes 98308
  2.4 16.2 %copy-start.9 = (f32[56,2,1024]{2,1,0:T(2,128)S(1)}, f32[56,2,1024]{2,1,0:T(2,128)}, u32[]{:S(2)}) copy-start(f32[56,2,1024]{2,1,0:T(2,128)} %get-tuple-element.39) | copy-start | bytes 1376260
  2.5 16.9 %copy-start.2 = (s32[1,8,4,1024]{3,2,1,0:T(4,128)S(1)}, s32[1,8,4,1024]{3,2,1,0:T(4,128)}, u32[]{:S(2)}) copy-start(s32[1,8,4,1024]{3,2,1,0:T(4,128)} %param.15) | copy-start | bytes 393220
  2.5 16.9 %copy-start.3 = (s32[1,8,4,1024]{3,2,1,0:T(4,128)S(1)}, s32[1,8,4,1024]{3,2,1,0:T(4,128)}, u32[]{:S(2)}) copy-start(s32[1,8,4,1024]{3,2,1,0:T(4,128)} %param.16) | copy-start | bytes 393220
  2.5 16.9 %copy-start.4 = (f32[1,8,4,1024]{3,2,1,0:T(4,128)S(1)}, f32[1,8,4,1024]{3,2,1,0:T(4,128)}, u32[]{:S(2)}) copy-start(f32[1,8,4,1024]{3,2,1,0:T(4,128)} %param.17) | copy-start | bytes 393220
  2.5 25.9 %collective-permute-start.4 = (f32[56,2,1024]{2,1,0:T(2,128)}, f32[56,2,1024]{2,1,0:T(2,128)S(1)}, u32[]{:S(2)}, u32[]{:S(2)}) collective-permute-start(f32[56,2,1024]{2,1,0:T(2,128)} %get-tuple-element.31), channel_id=1, source_target_pairs={{0,1},{1,2},{2,3},{3,4},{4,5},{5,6},{6,7},{7,8},{8,9},{9,10},{10,1... | collective-permute-start | bytes 1376264 | tf_op jit(solution)/shard_map/ppermute | solution.py:27
  8.0 10.7 %collective-permute-start = (f32[16,2048]{1,0:T(8,128)S(1)}, f32[16,2048]{1,0:T(8,128)S(1)}, u32[]{:S(2)}, u32[]{:S(2)}) collective-permute-start(f32[16,2048]{1,0:T(8,128)S(1)} %get-tuple-element.27), channel_id=1, source_target_pairs={{0,64},{1,65},{2,66},{3,67},{4,68},{5,69},{6,70},{7,71},{8,72},{9,... | collective-permute-start | bytes 393224 | tf_op jit(solution)/shard_map/ppermute | solution.py:27
  9.0 19.2 %collective-permute-start.1 = (f32[16,2048]{1,0:T(8,128)S(1)}, f32[16,2048]{1,0:T(8,128)S(1)}, u32[]{:S(2)}, u32[]{:S(2)}) collective-permute-start(f32[16,2048]{1,0:T(8,128)S(1)} %get-tuple-element.28), channel_id=1, source_target_pairs={{0,65},{1,66},{2,67},{3,68},{4,69},{5,70},{6,71},{7,72},{8,73},{9,... | collective-permute-start | bytes 393224 | tf_op jit(solution)/shard_map/ppermute | solution.py:27
  10.6 17.6 %collective-permute-start.2 = (f32[16,2048]{1,0:T(8,128)S(1)}, f32[16,2048]{1,0:T(8,128)S(1)}, u32[]{:S(2)}, u32[]{:S(2)}) collective-permute-start(f32[16,2048]{1,0:T(8,128)S(1)} %get-tuple-element.29), channel_id=1, source_target_pairs={{0,127},{1,64},{2,65},{3,66},{4,67},{5,68},{6,69},{7,70},{8,71},{9... | collective-permute-start | bytes 393224 | tf_op jit(solution)/shard_map/ppermute | solution.py:27
  16.2 12.2 %collective-permute-start.3 = (f32[16,2048]{1,0:T(8,128)S(1)}, f32[16,2048]{1,0:T(8,128)S(1)}, u32[]{:S(2)}, u32[]{:S(2)}) collective-permute-start(f32[16,2048]{1,0:T(8,128)S(1)} %get-tuple-element.30), channel_id=1, source_target_pairs={{0,126},{1,127},{2,64},{3,65},{4,66},{5,67},{6,68},{7,69},{8,70},{... | collective-permute-start | bytes 393224 | tf_op jit(solution)/shard_map/ppermute | solution.py:27
  18.7 22.2 %collective-permute-start.6 = (f32[56,2,1024]{2,1,0:T(2,128)S(1)}, f32[56,2,1024]{2,1,0:T(2,128)S(1)}, u32[]{:S(2)}, u32[]{:S(2)}) collective-permute-start(f32[56,2,1024]{2,1,0:T(2,128)S(1)} %copy-done.9), channel_id=1, source_target_pairs={{0,63},{1,0},{2,1},{3,2},{4,3},{5,4},{6,5},{7,6},{8,7},{9,8},{10,9... | collective-permute-start | bytes 1376264 | tf_op jit(solution)/shard_map/ppermute | solution.py:27
  19.4 9.0 %copy-start.7 = (f32[1,16,4,1024]{3,2,1,0:T(4,128)S(1)}, f32[1,16,4,1024]{3,2,1,0:T(4,128)}, u32[]{:S(2)}) copy-start(f32[1,16,4,1024]{3,2,1,0:T(4,128)} %param.11) | copy-start | bytes 786436
  19.4 9.0 %copy-start.8 = (s32[1,4,1024]{2,1,0:T(4,128)S(1)}, s32[1,4,1024]{2,1,0:T(4,128)}, u32[]{:S(2)}) copy-start(s32[1,4,1024]{2,1,0:T(4,128)} %param.12) | copy-start | bytes 49156
  33.8 10.5 %collective-permute-start.7 = (f32[16,2,1024]{2,1,0:T(2,128)S(1)}, f32[16,2,1024]{2,1,0:T(2,128)S(1)}, u32[]{:S(2)}, u32[]{:S(2)}) collective-permute-start(f32[16,2,1024]{2,1,0:T(2,128)S(1)} %remap.2.own1), channel_id=1, source_target_pairs={{0,63},{1,2},{2,1},{3,4},{4,3},{5,6},{6,5},{7,8},{8,7},{9,10},{10,... | collective-permute-start | bytes 393224 | tf_op jit(solution)/shard_map/ppermute | solution.py:33
  35.4 5.5 %copy-start.1 = (f32[1,2,4,4,1024]{4,3,2,1,0:T(4,128)S(1)}, f32[1,2,4,4,1024]{4,3,2,1,0:T(4,128)}, u32[]{:S(2)}) copy-start(f32[1,2,4,4,1024]{4,3,2,1,0:T(4,128)} %param.10) | copy-start | bytes 393220
  40.8 4.8 %collective-permute-start.5 = (f32[16,2,1024]{2,1,0:T(2,128)S(1)}, f32[16,2,1024]{2,1,0:T(2,128)S(1)}, u32[]{:S(2)}, u32[]{:S(2)}) collective-permute-start(f32[16,2,1024]{2,1,0:T(2,128)S(1)} %remap.3.own2), channel_id=1, source_target_pairs={{0,1},{1,0},{2,3},{3,2},{4,5},{5,4},{6,7},{7,6},{8,9},{9,8},{10,11... | collective-permute-start | bytes 393224 | tf_op jit(solution)/shard_map/ppermute | solution.py:33

commit v9 on v8

--- a/solution.py
+++ b/solution.py
@@ -83,10 +83,9 @@
         copy.wait()
     for which in range(2):
         for level in range(levels):
-            at = (levels - 1) * tracers + which * levels + level
-            after_v[at] = moving[which, level, :2]
-            before_v[at] = moving[which, level, grid_rows - 2 :]
-
+            at = (levels - 1) * tracers + level
+            after_v[at, which : which + 1] = moving[which, level, :1]
+            before_v[at, which : which + 1] = moving[which, level, grid_rows - 1 :]
     for level in range(levels - 1):
         at = slice(level * tracers, (level + 1) * tracers)
         after_v[at] = upper[:, level, :2]
@@ -95,7 +94,7 @@
 
 def edges(field, speed):
     tracers, levels, grid_rows, width = field.shape
-    edge = jax.ShapeDtypeStruct(((levels - 1) * tracers + 2 * levels, 2, width), jnp.float32)
+    edge = jax.ShapeDtypeStruct(((levels - 1) * tracers + levels, 2, width), jnp.float32)
     return pl.pallas_call(
         edges_kernel,
         in_specs=[pl.BlockSpec(memory_space=pltpu.HBM)] * 2,
@@ -317,13 +316,13 @@
     for row in range(-1, grid_rows + 1):
         pair = []
         for which in range(2):
-            at = (levels - 1) * tracers + which * levels + level
+            at = (levels - 1) * tracers + level
             if row < 0:
-                pair.append(before_v[at, 1:])
+                pair.append(before_v[at, which : which + 1])
             elif row < grid_rows:
                 pair.append(velocity[which, level, row : row + 1])
             else:
-                pair.append(after_v[at, :1])
+                pair.append(after_v[at, which : which + 1])
         pairs.append(pair)
     return pairs
 

time: 46.9 us -> 46.7 us (level)
  waiting for transfers between devices: 6.84 us -> 5.83 us
  starting transfers between devices: 15.6 us -> 16.3 us
    ppermute x2, starting transfers between devices: 1.62 us -> 2.34 us  [swapped(): return lax.ppermute(value, 'tile', pairs)]
    ppermute x6, waiting for transfers between devices: 5.19 us -> 4.49 us  [moved(): return lax.ppermute(value, ('comp', 'tile'), pairs)]
  transfers between devices with their start and end apart: 8 -> 8, of which waited for: 3 -> 4; matrix products, arithmetic and copies ran while one was open for 0% -> 0% of each run, Pallas kernels for 44% -> 44%
where the time goes in v9:
time: 46.7 us; the launch traced here: 46.5 us
  Pallas kernels  24.2 us (52%)
  starting transfers between devices  16.3 us (35%)
  waiting for transfers between devices  5.83 us (12%)
    ppermute x6, starting transfers between devices, moved(): return lax.ppermute(value, ('comp', 'tile'), pairs)  14 us
    pallas_call x2, Pallas kernels, remap(): pl.pallas_call(functools.partial(remap_kernel, sources), grid=(1,), in_sp...  10.8 us
    ppermute x6, waiting for transfers between devices, moved(): return lax.ppermute(value, ('comp', 'tile'), pairs)  4.49 us
    pallas_call x1, Pallas kernels, remap_near(): pl.pallas_call(functools.partial(near_kernel, (source,)), out_shape=jax.S...  3.8 us
    pallas_call x2, Pallas kernels, upper_levels(): pl.pallas_call(functools.partial(upper_kernel, first), grid=(count,), out...  3.04 us
    pallas_call x1, Pallas kernels, pack(): pl.pallas_call(pack_kernel, grid=(1,), in_specs=[level_spec(field), whole...  2.92 us
    pallas_call x1, Pallas kernels, edges(): pl.pallas_call(edges_kernel, in_specs=[pl.BlockSpec(memory_space=pltpu.HB...  2.38 us
    ppermute x2, starting transfers between devices, swapped(): return lax.ppermute(value, 'tile', pairs)  2.34 us
  transfers between devices with their start and end apart: 8, of which 4 were waited for; matrix products, arithmetic and copies ran while one was open for 0% of the time, Pallas kernels for 44%

profile of v9, /device:TPU:1, one launch (start us, length us, event | category | flops | bytes accessed | tf_op | source)
XLA Modules:
  0.0 46.5 jit_solution(6237869926766822039)
XLA Ops:
  0.0 0.0 copy-start
  0.0 0.0 copy-start.5
  0.0 0.0 copy-start.6
  0.0 2.4 %edges.1 = (f32[52,2,1024]{2,1,0:T(2,128)}, f32[52,2,1024]{2,1,0:T(2,128)}) custom-call(f32[16,4,4,1024]{3,2,1,0:T(4,128)} %bitcast.12, f32[2,4,4,1024]{3,2,1,0:T(4,128)} %bitcast.18), custom_call_target="tpu_custom_call" | custom-call | flops 1000000 | bytes 100000 | tf_op jit(solution)/shard_map/edges/pallas_call | solution.py:98
  2.4 0.0 copy-start.9
  2.4 0.0 copy-start.2
  2.4 0.0 copy-start.3
  2.4 0.0 copy-start.4
  2.4 2.5 %collective-permute-start.4 = (f32[52,2,1024]{2,1,0:T(2,128)}, f32[52,2,1024]{2,1,0:T(2,128)S(1)}, u32[]{:S(2)}, u32[]{:S(2)}) collective-permute-start(f32[52,2,1024]{2,1,0:T(2,128)} %get-tuple-element.31), channel_id=1, source_target_pairs={{0,1},{1,2},{2,3},{3,4},{4,5},{5,6},{6,7},{7,8},{8,9},{9,10},{10,1... | collective-permute-start | bytes 1277960 | tf_op jit(solution)/shard_map/ppermute | solution.py:27
  5.0 0.0 copy-done
  5.0 0.0 copy-done.5
  5.0 0.0 copy-done.6
  5.0 2.9 %pack.1 = (f32[16,2048]{1,0:T(8,128)S(1)}, f32[16,2048]{1,0:T(8,128)S(1)}, f32[16,2048]{1,0:T(8,128)S(1)}, f32[16,2048]{1,0:T(8,128)S(1)}) custom-call(f32[16,4,4,1024]{3,2,1,0:T(4,128)S(1)} %bitcast.13, s32[4,2048]{1,0:T(4,128)S(1)} %bitcast.31, s32[4,2048]{1,0:T(4,128)S(1)} %bitcast.32), custom_call_target="tpu_custom_call" | custom-call | flops 1000000 | bytes 100000 | tf_op jit(solution)/shard_map/pack/pallas_call | solution.py:140
  7.9 1.0 %collective-permute-start = (f32[16,2048]{1,0:T(8,128)S(1)}, f32[16,2048]{1,0:T(8,128)S(1)}, u32[]{:S(2)}, u32[]{:S(2)}) collective-permute-start(f32[16,2048]{1,0:T(8,128)S(1)} %get-tuple-element.27), channel_id=1, source_target_pairs={{0,64},{1,65},{2,66},{3,67},{4,68},{5,69},{6,70},{7,71},{8,72},{9,... | collective-permute-start | bytes 393224 | tf_op jit(solution)/shard_map/ppermute | solution.py:27
  8.9 1.6 %collective-permute-start.1 = (f32[16,2048]{1,0:T(8,128)S(1)}, f32[16,2048]{1,0:T(8,128)S(1)}, u32[]{:S(2)}, u32[]{:S(2)}) collective-permute-start(f32[16,2048]{1,0:T(8,128)S(1)} %get-tuple-element.28), channel_id=1, source_target_pairs={{0,65},{1,66},{2,67},{3,68},{4,69},{5,70},{6,71},{7,72},{8,73},{9,... | collective-permute-start | bytes 393224 | tf_op jit(solution)/shard_map/ppermute | solution.py:27
  10.5 5.6 %collective-permute-start.2 = (f32[16,2048]{1,0:T(8,128)S(1)}, f32[16,2048]{1,0:T(8,128)S(1)}, u32[]{:S(2)}, u32[]{:S(2)}) collective-permute-start(f32[16,2048]{1,0:T(8,128)S(1)} %get-tuple-element.29), channel_id=1, source_target_pairs={{0,127},{1,64},{2,65},{3,66},{4,67},{5,68},{6,69},{7,70},{8,71},{9... | collective-permute-start | bytes 393224 | tf_op jit(solution)/shard_map/ppermute | solution.py:27
  16.1 2.5 %collective-permute-start.3 = (f32[16,2048]{1,0:T(8,128)S(1)}, f32[16,2048]{1,0:T(8,128)S(1)}, u32[]{:S(2)}, u32[]{:S(2)}) collective-permute-start(f32[16,2048]{1,0:T(8,128)S(1)} %get-tuple-element.30), channel_id=1, source_target_pairs={{0,126},{1,127},{2,64},{3,65},{4,66},{5,67},{6,68},{7,69},{8,70},{... | collective-permute-start | bytes 393224 | tf_op jit(solution)/shard_map/ppermute | solution.py:27
  18.6 0.0 collective-permute-done.piece
  18.6 0.0 copy-done.9
  18.6 0.7 %collective-permute-start.6 = (f32[52,2,1024]{2,1,0:T(2,128)S(1)}, f32[52,2,1024]{2,1,0:T(2,128)S(1)}, u32[]{:S(2)}, u32[]{:S(2)}) collective-permute-start(f32[52,2,1024]{2,1,0:T(2,128)S(1)} %copy-done.9), channel_id=1, source_target_pairs={{0,63},{1,0},{2,1},{3,2},{4,3},{5,4},{6,5},{7,6},{8,7},{9,8},{10,9... | collective-permute-start | bytes 1277960 | tf_op jit(solution)/shard_map/ppermute | solution.py:27
  19.3 0.0 copy-done.2
  19.3 0.0 copy-done.3
  19.3 0.0 copy-done.4
  19.3 0.0 copy-start.7
  19.4 0.0 copy-start.8
  19.4 3.8 %remap_near.1.partial = f32[16,4,1024]{2,1,0:T(4,128)S(1)} custom-call(s32[8,4,1024]{2,1,0:T(4,128)S(1)} %bitcast.22, s32[8,4,1024]{2,1,0:T(4,128)S(1)} %bitcast.25, f32[8,4,1024]{2,1,0:T(4,128)S(1)} %bitcast.28, f32[16,2048]{1,0:T(8,128)S(1)} %collective-permute-done.piece), custom_call_target="tpu_custom_call" | custom-call | flops 1000000 | bytes 100000 | tf_op jit(solution)/shard_map/remap_near/pallas_call | solution.py:246
  23.2 4.2 %collective-permute-done.1.rest_0_ = f32[16,2048]{1,0:T(8,128)S(1)} collective-permute-done((f32[16,2048]{1,0:T(8,128)S(1)}, f32[16,2048]{1,0:T(8,128)S(1)}, u32[]{:S(2)}, u32[]{:S(2)}) %collective-permute-start.1) | collective-permute-done | bytes 131104 | tf_op jit(solution)/shard_map/ppermute | solution.py:27
  27.4 0.0 collective-permute-done.2.rest_1_
  27.4 0.2 collective-permute-done.3.rest_2_
  27.7 0.0 collective-permute-done.4.before_v
  27.7 0.0 copy-done.7
  27.7 0.0 copy-done.8
  27.7 5.4 %remap.2.own1 = f32[16,2,1024]{2,1,0:T(2,128)S(1)} custom-call(s32[1]{0:T(128)} %bitcast.start, s32[8,4,1024]{2,1,0:T(4,128)S(1)} %bitcast.23, s32[8,4,1024]{2,1,0:T(4,128)S(1)} %bitcast.26, f32[8,4,1024]{2,1,0:T(4,128)S(1)} %bitcast.29, f32[16,4,4,1024]{3,2,1,0:T(4,128)S(1)} %bitcast.14, f32[16,4,1024]{2,1,0:T(4,128)S(1)} %bitcast.33, ...), custom_call_target="tpu_custom_call" | custom-call | flops 15000000512 | bytes 1000000 | tf_op jit(solution)/shard_map/remap/pallas_call | solution.py:282
  33.1 2.3 %collective-permute-start.7 = (f32[16,2,1024]{2,1,0:T(2,128)S(1)}, f32[16,2,1024]{2,1,0:T(2,128)S(1)}, u32[]{:S(2)}, u32[]{:S(2)}) collective-permute-start(f32[16,2,1024]{2,1,0:T(2,128)S(1)} %remap.2.own1), channel_id=1, source_target_pairs={{0,63},{1,2},{2,1},{3,4},{4,3},{5,6},{6,5},{7,8},{8,7},{9,10},{10,... | collective-permute-start | bytes 393224 | tf_op jit(solution)/shard_map/ppermute | solution.py:33
  35.3 0.0 copy-start.1
  35.3 5.4 %remap.3.own2 = f32[16,2,1024]{2,1,0:T(2,128)S(1)} custom-call(s32[1]{0:T(128)} %bitcast.1.start, s32[8,4,1024]{2,1,0:T(4,128)S(1)} %bitcast.24, s32[8,4,1024]{2,1,0:T(4,128)S(1)} %bitcast.27, f32[8,4,1024]{2,1,0:T(4,128)S(1)} %bitcast.30, f32[16,4,4,1024]{3,2,1,0:T(4,128)S(1)} %bitcast.15, f32[16,4,1024]{2,1,0:T(4,128)S(1)} %bitcast.34, ...), custom_call_target="tpu_custom_call" | custom-call | flops 15000000512 | bytes 1000000 | tf_op jit(solution)/shard_map/remap/pallas_call | solution.py:282
  40.7 0.1 collective-permute-start.5
  40.8 0.0 collective-permute-done.6.after_v
  40.8 0.0 copy-done.1
  40.8 1.8 %upper_levels.2.rest_0_ = f32[16,4,4,1024]{3,2,1,0:T(4,128)} custom-call(f32[16,4,4,1024]{3,2,1,0:T(4,128)S(1)} %bitcast.16, f32[52,2,1024]{2,1,0:T(2,128)S(1)} %collective-permute-done.4.before_v, f32[52,2,1024]{2,1,0:T(2,128)S(1)} %collective-permute-done.6.after_v, f32[2,4,4,1024]{3,2,1,0:T(4,128)S(1)} %bitcast.19), custom_call_target="tpu_custom_call" | custom-call | flops 1000000 | bytes 100000 | tf_op jit(solution)/shard_map/upper_levels/pallas_call | solution.py:367
  42.6 1.0 %collective-permute-done.7.got1 = f32[16,2,1024]{2,1,0:T(2,128)S(1)} collective-permute-done((f32[16,2,1024]{2,1,0:T(2,128)S(1)}, f32[16,2,1024]{2,1,0:T(2,128)S(1)}, u32[]{:S(2)}, u32[]{:S(2)}) %collective-permute-start.7) | collective-permute-done | bytes 131104 | tf_op jit(solution)/shard_map/ppermute | solution.py:33
  43.6 1.2 %upper_levels.3.whole = f32[16,4,4,1024]{3,2,1,0:T(4,128)} custom-call(f32[16,4,4,1024]{3,2,1,0:T(4,128)S(1)} %bitcast.17, f32[52,2,1024]{2,1,0:T(2,128)S(1)} %collective-permute-done.4.before_v, f32[52,2,1024]{2,1,0:T(2,128)S(1)} %collective-permute-done.6.after_v, f32[2,4,4,1024]{3,2,1,0:T(4,128)S(1)} %bitcast.20, ...), custom_call_target="tpu_custom_call", output_to_operand_aliasing={{}: (4, {})} | custom-call | flops 1000000 | bytes 100000 | tf_op jit(solution)/shard_map/upper_levels/pallas_call | solution.py:367
  44.8 0.4 collective-permute-done.5.got2
  45.2 1.2 %surface_level.1 = f32[16,4,4,1024]{3,2,1,0:T(4,128)} custom-call(s32[1]{0:T(128)} %bitcast.start, f32[16,2,1024]{2,1,0:T(2,128)S(1)} %collective-permute-done.5.got2, f32[16,2,1024]{2,1,0:T(2,128)S(1)} %collective-permute-done.7.got1, f32[2,4,4,1024]{3,2,1,0:T(4,128)S(1)} %bitcast.21, ...), custom_call_target="tpu_custom_call", output_to_operand_aliasing={{}: (8, {})} | custom-call | tf_op jit(solution)/shard_map/surface_level/pallas_call | solution.py:389
Async XLA Ops:
  0.0 5.0 %copy-start = (f32[1,16,4,4,1024]{4,3,2,1,0:T(4,128)S(1)}, f32[1,16,4,4,1024]{4,3,2,1,0:T(4,128)}, u32[]{:S(2)}) copy-start(f32[1,16,4,4,1024]{4,3,2,1,0:T(4,128)} %param.9) | copy-start | bytes 3145732
  0.0 5.0 %copy-start.5 = (s32[1,1,4,2048]{3,2,1,0:T(4,128)S(1)}, s32[1,1,4,2048]{3,2,1,0:T(4,128)}, u32[]{:S(2)}) copy-start(s32[1,1,4,2048]{3,2,1,0:T(4,128)} %param.13) | copy-start | bytes 98308
  0.0 5.0 %copy-start.6 = (s32[1,1,4,2048]{3,2,1,0:T(4,128)S(1)}, s32[1,1,4,2048]{3,2,1,0:T(4,128)}, u32[]{:S(2)}) copy-start(s32[1,1,4,2048]{3,2,1,0:T(4,128)} %param.14) | copy-start | bytes 98308
  2.4 16.2 %copy-start.9 = (f32[52,2,1024]{2,1,0:T(2,128)S(1)}, f32[52,2,1024]{2,1,0:T(2,128)}, u32[]{:S(2)}) copy-start(f32[52,2,1024]{2,1,0:T(2,128)} %get-tuple-element.39) | copy-start | bytes 1277956
  2.4 16.9 %copy-start.2 = (s32[1,8,4,1024]{3,2,1,0:T(4,128)S(1)}, s32[1,8,4,1024]{3,2,1,0:T(4,128)}, u32[]{:S(2)}) copy-start(s32[1,8,4,1024]{3,2,1,0:T(4,128)} %param.15) | copy-start | bytes 393220
  2.4 16.9 %copy-start.3 = (s32[1,8,4,1024]{3,2,1,0:T(4,128)S(1)}, s32[1,8,4,1024]{3,2,1,0:T(4,128)}, u32[]{:S(2)}) copy-start(s32[1,8,4,1024]{3,2,1,0:T(4,128)} %param.16) | copy-start | bytes 393220
  2.4 16.9 %copy-start.4 = (f32[1,8,4,1024]{3,2,1,0:T(4,128)S(1)}, f32[1,8,4,1024]{3,2,1,0:T(4,128)}, u32[]{:S(2)}) copy-start(f32[1,8,4,1024]{3,2,1,0:T(4,128)} %param.17) | copy-start | bytes 393220
  2.4 25.2 %collective-permute-start.4 = (f32[52,2,1024]{2,1,0:T(2,128)}, f32[52,2,1024]{2,1,0:T(2,128)S(1)}, u32[]{:S(2)}, u32[]{:S(2)}) collective-permute-start(f32[52,2,1024]{2,1,0:T(2,128)} %get-tuple-element.31), channel_id=1, source_target_pairs={{0,1},{1,2},{2,3},{3,4},{4,5},{5,6},{6,7},{7,8},{8,9},{9,10},{10,1... | collective-permute-start | bytes 1277960 | tf_op jit(solution)/shard_map/ppermute | solution.py:27
  7.9 10.7 %collective-permute-start = (f32[16,2048]{1,0:T(8,128)S(1)}, f32[16,2048]{1,0:T(8,128)S(1)}, u32[]{:S(2)}, u32[]{:S(2)}) collective-permute-start(f32[16,2048]{1,0:T(8,128)S(1)} %get-tuple-element.27), channel_id=1, source_target_pairs={{0,64},{1,65},{2,66},{3,67},{4,68},{5,69},{6,70},{7,71},{8,72},{9,... | collective-permute-start | bytes 393224 | tf_op jit(solution)/shard_map/ppermute | solution.py:27
  8.9 18.5 %collective-permute-start.1 = (f32[16,2048]{1,0:T(8,128)S(1)}, f32[16,2048]{1,0:T(8,128)S(1)}, u32[]{:S(2)}, u32[]{:S(2)}) collective-permute-start(f32[16,2048]{1,0:T(8,128)S(1)} %get-tuple-element.28), channel_id=1, source_target_pairs={{0,65},{1,66},{2,67},{3,68},{4,69},{5,70},{6,71},{7,72},{8,73},{9,... | collective-permute-start | bytes 393224 | tf_op jit(solution)/shard_map/ppermute | solution.py:27
  10.5 16.9 %collective-permute-start.2 = (f32[16,2048]{1,0:T(8,128)S(1)}, f32[16,2048]{1,0:T(8,128)S(1)}, u32[]{:S(2)}, u32[]{:S(2)}) collective-permute-start(f32[16,2048]{1,0:T(8,128)S(1)} %get-tuple-element.29), channel_id=1, source_target_pairs={{0,127},{1,64},{2,65},{3,66},{4,67},{5,68},{6,69},{7,70},{8,71},{9... | collective-permute-start | bytes 393224 | tf_op jit(solution)/shard_map/ppermute | solution.py:27
  16.1 11.5 %collective-permute-start.3 = (f32[16,2048]{1,0:T(8,128)S(1)}, f32[16,2048]{1,0:T(8,128)S(1)}, u32[]{:S(2)}, u32[]{:S(2)}) collective-permute-start(f32[16,2048]{1,0:T(8,128)S(1)} %get-tuple-element.30), channel_id=1, source_target_pairs={{0,126},{1,127},{2,64},{3,65},{4,66},{5,67},{6,68},{7,69},{8,70},{... | collective-permute-start | bytes 393224 | tf_op jit(solution)/shard_map/ppermute | solution.py:27
  18.6 22.2 %collective-permute-start.6 = (f32[52,2,1024]{2,1,0:T(2,128)S(1)}, f32[52,2,1024]{2,1,0:T(2,128)S(1)}, u32[]{:S(2)}, u32[]{:S(2)}) collective-permute-start(f32[52,2,1024]{2,1,0:T(2,128)S(1)} %copy-done.9), channel_id=1, source_target_pairs={{0,63},{1,0},{2,1},{3,2},{4,3},{5,4},{6,5},{7,6},{8,7},{9,8},{10,9... | collective-permute-start | bytes 1277960 | tf_op jit(solution)/shard_map/ppermute | solution.py:27
  19.3 8.3 %copy-start.7 = (f32[1,16,4,1024]{3,2,1,0:T(4,128)S(1)}, f32[1,16,4,1024]{3,2,1,0:T(4,128)}, u32[]{:S(2)}) copy-start(f32[1,16,4,1024]{3,2,1,0:T(4,128)} %param.11) | copy-start | bytes 786436
  19.4 8.3 %copy-start.8 = (s32[1,4,1024]{2,1,0:T(4,128)S(1)}, s32[1,4,1024]{2,1,0:T(4,128)}, u32[]{:S(2)}) copy-start(s32[1,4,1024]{2,1,0:T(4,128)} %param.12) | copy-start | bytes 49156
  33.1 10.5 %collective-permute-start.7 = (f32[16,2,1024]{2,1,0:T(2,128)S(1)}, f32[16,2,1024]{2,1,0:T(2,128)S(1)}, u32[]{:S(2)}, u32[]{:S(2)}) collective-permute-start(f32[16,2,1024]{2,1,0:T(2,128)S(1)} %remap.2.own1), channel_id=1, source_target_pairs={{0,63},{1,2},{2,1},{3,4},{4,3},{5,6},{6,5},{7,8},{8,7},{9,10},{10,... | collective-permute-start | bytes 393224 | tf_op jit(solution)/shard_map/ppermute | solution.py:33
  35.3 5.5 %copy-start.1 = (f32[1,2,4,4,1024]{4,3,2,1,0:T(4,128)S(1)}, f32[1,2,4,4,1024]{4,3,2,1,0:T(4,128)}, u32[]{:S(2)}) copy-start(f32[1,2,4,4,1024]{4,3,2,1,0:T(4,128)} %param.10) | copy-start | bytes 393220
  40.7 4.5 %collective-permute-start.5 = (f32[16,2,1024]{2,1,0:T(2,128)S(1)}, f32[16,2,1024]{2,1,0:T(2,128)S(1)}, u32[]{:S(2)}, u32[]{:S(2)}) collective-permute-start(f32[16,2,1024]{2,1,0:T(2,128)S(1)} %remap.3.own2), channel_id=1, source_target_pairs={{0,1},{1,0},{2,3},{3,2},{4,5},{5,4},{6,7},{7,6},{8,9},{9,8},{10,11... | collective-permute-start | bytes 393224 | tf_op jit(solution)/shard_map/ppermute | solution.py:33
